TPU v7x, 256 devices: a whole 4x4x8 slice. The times are simulated.
256 devices in a mesh: dp: 8 (over z), group: 4 (over x), tensor: 8 (over y, core).
Axes of the slice: x: 4, y: 4, z: 8, core: 2. Of those that a mesh axis runs over, the one named last changes fastest.
Arguments:
- learn_x: bfloat16 [32768, 8192], P(('dp', 'group'), 'tensor'), may hold values from -6.5 to 6.5
- learn_dy: bfloat16 [32768, 1024], P(('dp', 'group'), 'tensor'), may hold values from -0.59765625 to 0.59765625
- block_tenant: int32 [256], P(('dp', 'group')), may hold values from 0 to 63, as said below
- block_count: int32 [256], P(('dp', 'group')), may hold values from 32 to 128
- adapter_a: float32 [64, 32, 8192], P(('dp', 'group'), None, 'tensor'), may hold values from -0.0625 to 0.0625
- adapter_b: float32 [64, 32, 1024], P(('dp', 'group'), None, 'tensor'), may hold values from -0.1875 to 0.1875
- moment_a: float32 [64, 32, 8192], P(('dp', 'group'), None, 'tensor'), may hold values from -12 to 12
- moment_b: float32 [64, 32, 1024], P(('dp', 'group'), None, 'tensor'), may hold values from -12 to 12
- second_a: float32 [64, 32, 8192], P(('dp', 'group'), None, 'tensor'), may hold values from 0.01 to 0.5
- second_b: float32 [64, 32, 1024], P(('dp', 'group'), None, 'tensor'), may hold values from 0.01 to 0.5
- tenant_group: int32 [64], replicated, may hold values from 0 to 3, as said below
- decode_inputs: bfloat16 [4, 1024, 2, 8192], P('group', 'dp'), may hold values from -6.5 to 6.5
- dec_weight: bfloat16 [8192, 1024], P(None, 'tensor'), may hold values from -0.0625 to 0.0625
- request_adapter: int32 [4, 1024], P('group', 'dp'), may hold values from 0 to 63, as said below
Outputs:
- updated_a: float32 [64, 32, 8192], P(('dp', 'group'), None, 'tensor')
- updated_b: float32 [64, 32, 1024], P(('dp', 'group'), None, 'tensor')
- moment_a_new: float32 [64, 32, 8192], P(('dp', 'group'), None, 'tensor')
- moment_b_new: float32 [64, 32, 1024], P(('dp', 'group'), None, 'tensor')
- second_a_new: float32 [64, 32, 8192], P(('dp', 'group'), None, 'tensor')
- second_b_new: float32 [64, 32, 1024], P(('dp', 'group'), None, 'tensor')
- decode_output: bfloat16 [4, 1024, 2, 1024], P('group', 'dp', None, 'tensor')
Inputs may be any that keep to these rules, and one draw needn't show every extreme that they name: `block_tenant`: the state of tenant t lies on index t // 2 of dp+group, whose group index is (t // 2) % 4. The 8 blocks of one device (one index of dp+group) name tenants of each group index exactly 8 / 4 times, in any order. `tenant_group`: for each index i of dp, the tenants i * 8 to (i + 1) * 8 - 1 include exactly 2 tenants of each group; so each group serves exactly 16 tenants. Each request's tenant is served by the request's group: tenant_group[request_adapter[g, q]] == g; every tenant that a group serves is named by some request of that group.
All inputs are finite; a program needn't handle non-finite values.
Results may differ from a plain program's by a relative error of at most 0.012.
Values may be sent and summed in bfloat16 or wider, within the bound.
No kernel may reach another device: no remote copies, remote signals or barrier semaphores. Data moves between devices by JAX's collectives and lax.ppermute only.
A program may use at most 64 MiB of HBM per device.

v0:
```python
import functools

import jax
import jax.numpy as jnp
from jax import lax
from jax.experimental import pallas as pl
from jax.experimental.pallas import tpu as pltpu
from jax.sharding import PartitionSpec as P

STEP_NUM = 10

adapter_scale = 2.0
beta_one = 0.9
beta_two = 0.999
step_rate = 0.001
adam_eps = 1e-08

BF = jnp.bfloat16
F32 = jnp.float32
MIB = 1024 * 1024


def dot(a, b, dims):
    return lax.dot_general(a, b, (dims, ((), ())), preferred_element_type=F32)


def shift(x, axis, distance):
    size = lax.axis_size(axis)
    return lax.ppermute(x, axis, [(i, (i + distance) % size) for i in range(size)])


def spread(x, axis):
    return [x] + [shift(x, axis, d) for d in range(1, lax.axis_size(axis))]


def ring(x, size, owned):
    ahead = behind = x
    arrays, firsts = [x], [0]
    for hop in range(1, size // 2 + 1):
        ahead = shift(ahead, "dp", 1)
        arrays.append(ahead)
        firsts.append(hop * owned)
        if hop < size // 2:
            behind = shift(behind, "dp", -1)
            arrays.append(behind)
            firsts.append((size - hop) * owned)
    return arrays, firsts


def two_stage(x, size, owned):
    near = [shift(x, "dp", d) for d in (1, -1, 2, -2)]
    far = [shift(near[2], "dp", 1), shift(near[3], "dp", -1), shift(near[2], "dp", 2)]
    firsts = [d % size * owned for d in (0, 1, -1, 2, -2, 3, -3, 4)]
    return [x, *near, *far], firsts


def two_stage_reduce(x, size):
    upper, lower = x[size // 2], x[-1]
    half = upper.shape[0]
    after = [shift(x[3], "dp", 1), shift(upper, "dp", 2)]
    before = [shift(x[5], "dp", -1), shift(lower, "dp", -2)]
    ahead = jnp.concatenate(
        [add(x[2][:half], after[0][:half], after[1]), add(x[2][half:], after[0][half:])]
    )
    behind = jnp.concatenate(
        [add(x[6][:half], before[0][:half]), add(x[6][half:], before[0][half:], before[1])]
    )
    near = [shift(x[1], "dp", 1), shift(x[7], "dp", -1)]
    return [*near, shift(ahead, "dp", 2), shift(behind, "dp", -2)]


def spot(memory, n=1):
    return [pl.BlockSpec(memory_space=memory)] * n


vmem = functools.partial(spot, pltpu.VMEM)
smem = functools.partial(spot, pltpu.SMEM)
anywhere = functools.partial(spot, pl.ANY)
SMALL = pltpu.CompilerParams(vmem_limit_bytes=14 * MIB)
LARGE = pltpu.CompilerParams(vmem_limit_bytes=61 * MIB)


def shape(dims, dtype=BF):
    return jax.ShapeDtypeStruct(dims, dtype)


def block_of(ref, index, rows):
    return ref.at[pl.ds(pl.multiple_of(index * rows, rows), rows), :]


def fetch(refs, rooms, sems):
    copies = [
        pltpu.make_async_copy(ref, room, sems.at[i]) for i, (ref, room) in enumerate(zip(refs, rooms))
    ]
    for copy in copies:
        copy.start()
    return copies


def begin_kernel(rows, groups, tenant, count, x, dy, *refs):
    packs, refs = refs[:groups], refs[groups:]
    source, ids, dy_here, room, sems, x_sems, out_sems = refs
    blocks = 2 * groups
    width = x.shape[1]
    loads = fetch([dy], [dy_here], sems)
    group = lax.axis_index("group")
    names = [tenant[b] for b in range(blocks)]
    far = [lax.rem(lax.rem(name // 2, groups) - group + groups, groups) for name in names]
    for b in range(blocks):
        place = 2 * far[b]
        for e in range(b):
            place += (far[e] == far[b]).astype(jnp.int32)
        source[place] = b
        ids[place] = names[b]
    moves = []
    for s in range(blocks):
        part = pl.ds((s % 2) * rows, rows)
        moves.append(
            pltpu.make_async_copy(
                block_of(x, source[s], rows), room.at[s // 2, part, :width], x_sems.at[s]
            )
        )
        moves[-1].start()
    loads[0].wait()
    for s in range(blocks):
        block = block_of(dy_here, source[s], rows)[...].astype(F32)
        live = lax.broadcasted_iota(jnp.int32, block.shape, 0) < count[source[s]]
        block = jnp.where(live, block, 0.0).astype(BF)
        room[s // 2, (s % 2) * rows : (s % 2 + 1) * rows, width:] = block
    stores = []
    for d in range(groups):
        lane = lax.broadcasted_iota(jnp.int32, (16, dy.shape[1]), 1)
        both = jnp.where(lane == 0, ids[2 * d], ids[2 * d + 1])
        room[d, 2 * rows :, width:] = both.astype(F32).astype(BF)
        room[d, 2 * rows :, :width] = jnp.zeros((16, width), BF)
        moves[2 * d].wait()
        moves[2 * d + 1].wait()
        stores.append(pltpu.make_async_copy(room.at[d], packs[d], out_sems.at[d]))
        stores[-1].start()
    for store in stores:
        store.wait()


def begin(tenant, count, x, dy, groups):
    rows = x.shape[0] // tenant.shape[0]
    wide = x.shape[1] + dy.shape[1]
    return pl.pallas_call(
        functools.partial(begin_kernel, rows, groups),
        in_specs=smem(2) + anywhere(2),
        out_specs=anywhere(groups),
        out_shape=[shape((2 * rows + 16, wide))] * groups,
        scratch_shapes=[
            pltpu.SMEM((2 * groups,), jnp.int32),
            pltpu.SMEM((2 * groups,), jnp.int32),
            pltpu.VMEM(dy.shape, BF),
            pltpu.VMEM((groups, 2 * rows + 16, wide), BF),
            pltpu.SemaphoreType.DMA((1,)),
            pltpu.SemaphoreType.DMA((2 * groups,)),
            pltpu.SemaphoreType.DMA((groups,)),
        ],
        compiler_params=LARGE,
    )(tenant, count, x, dy)


def frozen_kernel(tensor, x, weight, out, x_out):
    step = pl.program_id(0)
    width = x_out.shape[1]
    pieces = x.shape[2] // width
    block = x[...].reshape(out.shape[0], x.shape[2])

    @pl.when(step == 0)
    def _():
        out[...] = jnp.zeros_like(out)

    out[...] += dot(block, weight[...], ((1,), (0,)))
    for i in range(pieces):

        @pl.when(tensor[0] == step * pieces + i)
        def _():
            x_out[...] = block[:, i * width : (i + 1) * width]


def frozen(tensor, requests, weight, part, parts, width):
    count = requests.shape[0] // parts
    steps = requests.shape[1]
    width_b = weight.shape[1]
    wide = 4 * width
    return pl.pallas_call(
        frozen_kernel,
        grid_spec=pltpu.PrefetchScalarGridSpec(
            num_scalar_prefetch=1,
            grid=(requests.shape[2] // wide,),
            in_specs=[
                pl.BlockSpec((count, steps, wide), lambda k, tensor: (part, 0, k)),
                pl.BlockSpec((wide, width_b), lambda k, tensor: (k, 0)),
            ],
            out_specs=[
                pl.BlockSpec((count * steps, width_b), lambda k, tensor: (0, 0)),
                pl.BlockSpec((count * steps, width), lambda k, tensor: (0, 0)),
            ],
        ),
        out_shape=[shape((count * steps, width_b), F32), shape((count * steps, width))],
        compiler_params=LARGE,
    )(tensor, requests, weight)


def low_kernel(rank, rows, size, owned, firsts, *refs):
    parts = len(firsts)
    tables, refs = refs[:parts], refs[parts:]
    *blocks, out, names, table, here, sems = refs
    wide = table.shape[1]
    width = wide - 128
    row = lax.axis_index("dp")
    span = owned * len(blocks)
    used = 2 * rows
    rooms = [
        table.at[first * rank : first * rank + ref.shape[0], :] for first, ref in zip(firsts, tables)
    ]
    rooms += [here.at[d] for d in range(len(blocks))]
    copies = fetch([*tables, *blocks], rooms, sems)
    for copy in copies[:parts]:
        copy.wait()
    half = used // rows * len(blocks) * rank
    for s in range(2 * len(blocks)):
        if s % 2 == 0:
            copies[parts + s // 2].wait()
            ids = here[s // 2, used : used + 16, width:].astype(F32)
        name = ids[0, s % 2].astype(jnp.int32)
        place = lax.rem(row - name // span + size, size) * owned + lax.rem(name, owned)
        names[s] = name
        block = here[s // 2, (s % 2) * rows : (s % 2 + 1) * rows, :]
        chosen = block_of(table, place, rank)[...]
        low_in = dot(chosen[:, :width], block[:, :width], ((1,), (1,)))
        low_back = dot(chosen[:, width:], block[:, width:], ((1,), (1,)))
        out[s * rank : (s + 1) * rank, :] = low_in.astype(BF)
        out[half + s * rank : half + (s + 1) * rank, :] = low_back.astype(BF)


def low(tables, firsts, blocks, rank, rows, size, owned):
    wide = blocks[0].shape[1]
    total = sum(table.shape[0] for table in tables)
    return pl.pallas_call(
        functools.partial(low_kernel, rank, rows, size, owned, firsts),
        in_specs=anywhere(len(tables) + len(blocks)),
        out_specs=vmem() + smem(),
        out_shape=[
            shape((4 * len(blocks) * rank, rows)),
            shape((2 * len(blocks),), jnp.int32),
        ],
        scratch_shapes=[
            pltpu.VMEM((total, wide), BF),
            pltpu.VMEM((len(blocks),) + blocks[0].shape, BF),
            pltpu.SemaphoreType.DMA((len(tables) + len(blocks),)),
        ],
        compiler_params=LARGE,
    )(*tables, *blocks)


def added(refs):
    total = refs[0][...].astype(F32)
    for ref in refs[1:]:
        total = total + ref[...].astype(F32)
    return total


def grad_kernel(rank, rows, parts, owned, names, *refs):
    lows, refs = refs[:parts], refs[parts:]
    groups = lows[0].shape[0] // (4 * rank)
    blocks, refs = refs[:groups], refs[groups:]
    *outs, sums, lows_here, here, half, sems, out_sems = refs
    width = sums.shape[2] - 128
    row = lax.axis_index("dp")
    span, size = owned * groups, len(outs) - 1
    copies = fetch(
        [*lows, *[ref.at[: 2 * rows, :] for ref in blocks]],
        [*[lows_here.at[d] for d in range(parts)], *[here.at[d] for d in range(groups)]],
        sems,
    )
    sums[...] = jnp.zeros_like(sums)
    for copy in copies[:parts]:
        copy.wait()
    total = added([lows_here.at[d] for d in range(parts)]).astype(BF)
    middle = 2 * groups * rank
    for s in range(2 * groups):
        if s % 2 == 0:
            copies[parts + s // 2].wait()
        block = here[s // 2, (s % 2) * rows : (s % 2 + 1) * rows, :]
        low_in = total[s * rank : (s + 1) * rank]
        low_back = total[middle + s * rank : middle + (s + 1) * rank]
        name = names[s]
        place = lax.rem(name // span - row + size, size) * owned + lax.rem(name, owned)
        sums[place, :, :width] += dot(low_back, block[:, :width], ((1,), (0,)))
        sums[place, :, width:] += dot(low_in, block[:, width:], ((1,), (0,)))
    stores = []
    far = size // 2
    order = [3, 5, far, 2, 6, 1, 7, 0]
    for d in order:
        for j in range(2):
            half[d, j * rank : (j + 1) * rank, :] = (adapter_scale * sums[2 * d + j]).astype(BF)
        if d == far:
            ends = [(half.at[d, :rank], outs[far]), (half.at[d, rank:], outs[-1])]
        else:
            ends = [(half.at[d], outs[d])]
        for source, out in ends:
            stores.append(pltpu.make_async_copy(source, out, out_sems.at[len(stores)]))
            stores[-1].start()
    for store in stores:
        store.wait()


def grad(names, lows, blocks, rank, rows, targets, owned):
    wide = blocks[0].shape[1]
    return pl.pallas_call(
        functools.partial(grad_kernel, rank, rows, len(lows), owned),
        in_specs=smem() + anywhere(len(lows) + len(blocks)),
        out_specs=anywhere(targets + 1),
        out_shape=[
            shape((rank if d in (targets // 2, targets) else 2 * rank, wide))
            for d in range(targets + 1)
        ],
        scratch_shapes=[
            pltpu.VMEM((2 * targets, rank, wide), F32),
            pltpu.VMEM((len(lows),) + lows[0].shape, BF),
            pltpu.VMEM((len(blocks), 2 * rows, wide), BF),
            pltpu.VMEM((targets, 2 * rank, wide), BF),
            pltpu.SemaphoreType.DMA((len(lows) + len(blocks),)),
            pltpu.SemaphoreType.DMA((targets + 1,)),
        ],
        compiler_params=LARGE,
    )(names, *lows, *blocks)


def adam_update(weights, moment, second, gradient):
    moment_new = beta_one * moment + (1.0 - beta_one) * gradient
    second_new = beta_two * second + (1.0 - beta_two) * gradient * gradient
    unbiased_m = moment_new / (1.0 - beta_one**STEP_NUM)
    unbiased_v = second_new / (1.0 - beta_two**STEP_NUM)
    weights_new = weights - step_rate * unbiased_m / (jnp.sqrt(unbiased_v) + adam_eps)
    return (weights_new, moment_new, second_new)


def adam_kernel(parts, *refs):
    grads, refs = refs[:parts], refs[parts:]
    states, outs, refs = refs[:6], refs[6:13], refs[13:]
    here, olds, news, fresh, sems, out_sems = refs[0], refs[1:7], refs[7:13], *refs[13:]
    copies = fetch([*states, *grads], [*olds, *[here.at[d] for d in range(parts)]], sems)
    width = olds[0].shape[1]
    for copy in copies:
        copy.wait()
    total = added([here.at[d] for d in range(parts)])
    for first, cols in ((0, slice(0, width)), (3, slice(width, None))):
        values = adam_update(*[ref[...] for ref in olds[first : first + 3]], total[:, cols])
        for ref, value in zip(news[first : first + 3], values):
            ref[...] = value
        fresh[:, cols] = values[0].astype(BF)
    for store in fetch([*news, fresh], outs, out_sems):
        store.wait()


def adam(grads, state_a, state_b):
    rows, width = state_a[0].shape
    width_b = state_b[0].shape[1]
    wide = width + width_b
    states = [pltpu.VMEM((rows, width), F32)] * 3 + [pltpu.VMEM((rows, width_b), F32)] * 3
    return pl.pallas_call(
        functools.partial(adam_kernel, len(grads)),
        in_specs=anywhere(len(grads) + 6),
        out_specs=anywhere(7),
        out_shape=[shape((rows, width), F32)] * 3
        + [shape((rows, width_b), F32)] * 3
        + [shape((rows, wide))],
        scratch_shapes=[pltpu.VMEM((len(grads), rows, wide), BF)]
        + states
        + states
        + [
            pltpu.VMEM((rows, wide), BF),
            pltpu.SemaphoreType.DMA((len(grads) + 6,)),
            pltpu.SemaphoreType.DMA((7,)),
        ],
        compiler_params=LARGE,
    )(*grads, *state_a, *state_b)


def pick_kernel(rank, index, *refs):
    *refs, out = refs
    for i in range(2):
        device, slot = index[i] // 2, index[i] % 2
        for d, ref in enumerate(refs):

            @pl.when(device == d)
            def _():
                out[i * rank : (i + 1) * rank, :] = block_of(ref, slot, rank)[...]


def pick(index, arrays, rank):
    return pl.pallas_call(
        functools.partial(pick_kernel, rank),
        in_specs=smem(1) + vmem(len(arrays)),
        out_specs=vmem()[0],
        out_shape=shape(arrays[0].shape),
        compiler_params=SMALL,
    )(index, *arrays)


def decode_in_kernel(rank, firsts, parts, slots, *refs):
    xs, refs = refs[:parts], refs[parts:]
    *refs, out = refs
    width = xs[0].shape[1]
    count = xs[0].shape[0]
    for i, x in enumerate(xs):
        here = slots[:, i * count : (i + 1) * count]
        total = jnp.zeros((rank, count), F32)
        for first, ref in zip(firsts, refs):
            both = dot(ref[:, :width], x[...], ((1,), (1,)))
            for j in range(ref.shape[0] // rank):
                total += jnp.where(here == first + j, both[j * rank : (j + 1) * rank], 0.0)
        out[:, i * count : (i + 1) * count] = total


def decode_in(slots, xs, fresh, firsts, rank):
    return pl.pallas_call(
        functools.partial(decode_in_kernel, rank, firsts, len(xs)),
        in_specs=vmem(1 + len(xs) + len(fresh)),
        out_specs=vmem()[0],
        out_shape=shape((rank, slots.shape[1]), F32),
        compiler_params=SMALL,
    )(slots, *xs, *fresh)


def decode_out_kernel(rank, parts, firsts, slots, *refs):
    frozen, refs = refs[:2], refs[2:]
    lows, fresh, out = refs[:parts], refs[parts:-1], refs[-1]
    width_b = out.shape[1]
    total = added(lows).astype(BF).astype(F32)
    result = jnp.concatenate([ref[...] for ref in frozen], axis=0)
    for first, ref in zip(firsts, fresh):
        wide = ref.shape[1]
        both = jnp.concatenate(
            [jnp.where(slots[...] == first + j, total, 0.0) for j in range(ref.shape[0] // rank)],
            axis=0,
        )
        part = dot(both.T.astype(BF), ref[:, wide - width_b :], ((1,), (0,)))
        result += adapter_scale * part
    out[...] = result.astype(BF)


def decode_out(slots, frozen, lows, fresh, firsts, rank):
    return pl.pallas_call(
        functools.partial(decode_out_kernel, rank, len(lows), firsts),
        in_specs=vmem(1 + len(frozen) + len(lows) + len(fresh)),
        out_specs=vmem()[0],
        out_shape=shape((slots.shape[1], frozen[0].shape[1])),
        compiler_params=SMALL,
    )(slots, *frozen, *lows, *fresh)


def add(x, *more):
    total = x.astype(F32)
    for y in more:
        total = total + y.astype(F32)
    return total.astype(x.dtype)


def tensor_parts(x):
    size = lax.axis_size("tensor")
    x = add(x, lax.ppermute(x, "tensor", [(i, i ^ 1) for i in range(size)]))
    return [x] + [
        lax.ppermute(x, "tensor", [(i, (i + 2 * d) % size) for i in range(size)])
        for d in range(1, size // 2)
    ]


def local(
    learn_x,
    learn_dy,
    block_tenant,
    block_count,
    adapter_a,
    adapter_b,
    moment_a,
    moment_b,
    second_a,
    second_b,
    tenant_group,
    decode_inputs,
    dec_weight,
    request_adapter,
):
    groups = lax.axis_size("group")
    rows_dp = lax.axis_size("dp")
    group = lax.axis_index("group")
    row = lax.axis_index("dp")
    owned, rank, width = adapter_a.shape
    width_b = adapter_b.shape[2]
    span = groups * owned
    barrier = lax.optimization_barrier

    def flat(x):
        return x.reshape(owned * rank, x.shape[2])

    blocks = block_tenant.shape[0]
    rows = learn_x.shape[0] // blocks
    packed = begin(block_tenant, block_count, learn_x, learn_dy, groups)
    packed, state = barrier((packed, (adapter_a, adapter_b)))
    arrived = [packed[0]] + [shift(packed[d], "group", d) for d in range(1, groups)]
    own = jnp.concatenate([flat(x).astype(BF) for x in state], axis=1)
    tables, firsts = ring(own, rows_dp, owned)
    requests = decode_inputs[0]
    steps = requests.shape[1]
    tensor = lax.axis_index("tensor").reshape(1)
    tables, requests = barrier((tables, requests))
    early = frozen(tensor, requests, dec_weight, 0, 2, width)
    arrived, tables, early = barrier((arrived, tables, early))

    partial, names = low(tables, firsts, arrived, rank, rows, rows_dp, owned)
    sums = grad(names, tensor_parts(partial), arrived, rank, rows, rows_dp, owned)
    pieces = [sums[0], *two_stage_reduce(sums, rows_dp)]
    *new, fresh = adam(
        pieces,
        [flat(x) for x in (adapter_a, moment_a, second_a)],
        [flat(x) for x in (adapter_b, moment_b, second_b)],
    )

    tenant_ids = jnp.arange(tenant_group.shape[0], dtype=jnp.int32)
    served = (tenant_group == group).astype(jnp.int32)
    by_row = served.reshape(rows_dp, span)
    slot_of = jnp.cumsum(by_row, axis=1) - by_row
    mine = lax.dynamic_slice_in_dim(by_row, row, 1, 0)[0]
    mine_slot = lax.dynamic_slice_in_dim(slot_of, row, 1, 0)[0]
    position = jnp.arange(span, dtype=jnp.int32)
    relative = ((group - position // owned) % groups) * owned + position % owned
    wanted = jnp.sum(
        jnp.where(
            (mine[None, :] == 1)
            & (mine_slot[None, :] == jnp.arange(owned, dtype=jnp.int32)[:, None]),
            relative[None, :],
            0,
        ),
        axis=1,
        dtype=jnp.int32,
    )
    slot_here = ((row - tenant_ids // span) % rows_dp) * owned + slot_of.reshape(-1)
    slot_here = jnp.where(served == 1, slot_here, -1)
    request_slot = jnp.sum(
        jnp.where(request_adapter[0][:, None] == tenant_ids[None, :], slot_here[None, :], 0),
        axis=1,
        dtype=jnp.int32,
    )
    count = requests.shape[0] * steps
    slots = jnp.broadcast_to(request_slot[:, None], (requests.shape[0], steps)).reshape(1, count)
    *new, fresh = adam(
        pieces,
        [flat(x) for x in (adapter_a, moment_a, second_a)],
        [flat(x) for x in (adapter_b, moment_b, second_b)],
    )
    in_row = spread(fresh, "group")
    fresh, wanted, slots, requests = barrier((fresh, wanted, slots, requests))
    late = frozen(tensor, requests, dec_weight, 1, 2, width)
    in_row, wanted, slots, late = barrier((in_row, wanted, slots, late))
    served_fresh, firsts = two_stage(pick(wanted, in_row, rank), rows_dp, owned)

    dec_part = decode_in(slots, [early[1], late[1]], served_fresh, firsts, rank)
    decoded = decode_out(
        slots, [early[0], late[0]], tensor_parts(dec_part), served_fresh, firsts, rank
    )
    new_a = [x.reshape(adapter_a.shape) for x in new[:3]]
    new_b = [x.reshape(adapter_b.shape) for x in new[3:]]
    return (
        new_a[0],
        new_b[0],
        new_a[1],
        new_b[1],
        new_a[2],
        new_b[2],
        decoded.reshape((1,) + requests.shape[:2] + (width_b,)),
    )


def solution(mesh):
    state = P(("dp", "group"), None, "tensor")
    return jax.shard_map(
        local,
        mesh=mesh,
        in_specs=(
            P(("dp", "group"), "tensor"),
            P(("dp", "group"), "tensor"),
            P(("dp", "group")),
            P(("dp", "group")),
            state,
            state,
            state,
            state,
            state,
            state,
            P(),
            P("group", "dp", None, None),
            P(None, "tensor"),
            P("group", "dp"),
        ),
        out_specs=(
            state,
            state,
            state,
            state,
            state,
            state,
            P("group", "dp", None, "tensor"),
        ),
        check_vma=False,
    )
```

profile of v0, /device:TPU:14, one launch (start us, length us, event | category | flops | bytes accessed | tf_op | source)
XLA Modules:
  0.0 136.3 jit_solution(797022400518176303)
XLA Ops:
  0.7 4.0 %shard_map.189 = (bf16[272,1152]{1,0:T(8,128)(2,1)}, bf16[272,1152]{1,0:T(8,128)(2,1)}, bf16[272,1152]{1,0:T(8,128)(2,1)}, bf16[272,1152]{1,0:T(8,128)(2,1)}) custom-call(s32[8]{0:T(128)} %tenant.1, s32[8]{0:T(128)} %count.1, bf16[1024,1024]{1,0:T(8,128)(2,1)} %x.1, bf16[1024,128]{1,0:T(8,128)(2,1)} %dy.1), custom_call_target="tpu_custom_call" | custom-call | tf_op jit(solution)/shard_map/pallas_call | solution.py:147
  5.3 2.4 %collective-permute-start.1 = (bf16[272,1152]{1,0:T(8,128)(2,1)}, bf16[272,1152]{1,0:T(8,128)(2,1)S(1)}, u32[]{:S(2)}, u32[]{:S(2)}) collective-permute-start(bf16[272,1152]{1,0:T(8,128)(2,1)} %get-tuple-element.79), channel_id=1, source_target_pairs={{0,16},{8,24},{16,0},{24,8},{1,17},{9,25},{17,1},{25,9},{2,18},{10... | collective-permute-start | bytes 1880072 | tf_op jit(solution)/shard_map/ppermute | solution.py:29
  7.8 2.0 %collective-permute-start.3 = (bf16[64,1152]{1,0:T(8,128)(2,1)S(1)}, bf16[64,1152]{1,0:T(8,128)(2,1)S(1)}, u32[]{:S(2)}, u32[]{:S(2)}) collective-permute-start(bf16[64,1152]{1,0:T(8,128)(2,1)S(1)} %pad_maximum_fusion.refs_0_), channel_id=1, source_target_pairs={{0,32},{32,64},{64,96},{96,128},{128,160},{160,192},{192,224},{224... | collective-permute-start | bytes 442376 | tf_op jit(solution)/shard_map/ppermute | solution.py:29
  9.8 4.0 %collective-permute-start.4 = (bf16[64,1152]{1,0:T(8,128)(2,1)S(1)}, bf16[64,1152]{1,0:T(8,128)(2,1)S(1)}, u32[]{:S(2)}, u32[]{:S(2)}) collective-permute-start(bf16[64,1152]{1,0:T(8,128)(2,1)S(1)} %pad_maximum_fusion.refs_0_), channel_id=1, source_target_pairs={{0,224},{32,0},{64,32},{96,64},{128,96},{160,128},{192,160},{224,1... | collective-permute-start | bytes 442376 | tf_op jit(solution)/shard_map/ppermute | solution.py:29
  13.8 3.2 %collective-permute-done.3.refs_1_ = bf16[64,1152]{1,0:T(8,128)(2,1)S(1)} collective-permute-done((bf16[64,1152]{1,0:T(8,128)(2,1)S(1)}, bf16[64,1152]{1,0:T(8,128)(2,1)S(1)}, u32[]{:S(2)}, u32[]{:S(2)}) %collective-permute-start.3) | collective-permute-done | bytes 147488 | tf_op jit(solution)/shard_map/ppermute | solution.py:29
  17.0 3.2 %collective-permute-start.6 = (bf16[64,1152]{1,0:T(8,128)(2,1)S(1)}, bf16[64,1152]{1,0:T(8,128)(2,1)S(1)}, u32[]{:S(2)}, u32[]{:S(2)}) collective-permute-start(bf16[64,1152]{1,0:T(8,128)(2,1)S(1)} %collective-permute-done.4.refs_2_), channel_id=1, source_target_pairs={{0,224},{32,0},{64,32},{96,64},{128,96},{160,128},{192,160},{224,1... | collective-permute-start | bytes 442376 | tf_op jit(solution)/shard_map/ppermute | solution.py:29
  20.2 3.1 %collective-permute-done.5.refs_3_ = bf16[64,1152]{1,0:T(8,128)(2,1)S(1)} collective-permute-done((bf16[64,1152]{1,0:T(8,128)(2,1)S(1)}, bf16[64,1152]{1,0:T(8,128)(2,1)S(1)}, u32[]{:S(2)}, u32[]{:S(2)}) %collective-permute-start.5) | collective-permute-done | bytes 147488 | tf_op jit(solution)/shard_map/ppermute | solution.py:29
  23.4 3.2 %collective-permute-start.8 = (bf16[64,1152]{1,0:T(8,128)(2,1)S(1)}, bf16[64,1152]{1,0:T(8,128)(2,1)S(1)}, u32[]{:S(2)}, u32[]{:S(2)}) collective-permute-start(bf16[64,1152]{1,0:T(8,128)(2,1)S(1)} %collective-permute-done.6.refs_4_), channel_id=1, source_target_pairs={{0,224},{32,0},{64,32},{96,64},{128,96},{160,128},{192,160},{224,1... | collective-permute-start | bytes 442376 | tf_op jit(solution)/shard_map/ppermute | solution.py:29
  26.6 3.1 %collective-permute-done.7.refs_5_ = bf16[64,1152]{1,0:T(8,128)(2,1)S(1)} collective-permute-done((bf16[64,1152]{1,0:T(8,128)(2,1)S(1)}, bf16[64,1152]{1,0:T(8,128)(2,1)S(1)}, u32[]{:S(2)}, u32[]{:S(2)}) %collective-permute-start.7) | collective-permute-done | bytes 147488 | tf_op jit(solution)/shard_map/ppermute | solution.py:29
  29.7 6.3 %collective-permute-done.9.refs_7_ = bf16[64,1152]{1,0:T(8,128)(2,1)S(1)} collective-permute-done((bf16[64,1152]{1,0:T(8,128)(2,1)S(1)}, bf16[64,1152]{1,0:T(8,128)(2,1)S(1)}, u32[]{:S(2)}, u32[]{:S(2)}) %collective-permute-start.9) | collective-permute-done | bytes 147488 | tf_op jit(solution)/shard_map/ppermute | solution.py:29
  36.1 3.5 %shard_map.190 = (f32[128,128]{1,0:T(8,128)}, bf16[128,1024]{1,0:T(8,128)(2,1)}) custom-call(s32[1]{0:T(128)} %bitcast.3.tensor, bf16[128,2,8192]{2,1,0:T(2,128)(2,1)} %bitcast.22, bf16[8192,128]{1,0:T(8,128)(2,1)} %weight.3), custom_call_target="tpu_custom_call" | custom-call | tf_op jit(solution)/shard_map/pallas_call | solution.py:188
  40.9 3.8 %shard_map.191 = (bf16[512,128]{1,0:T(8,128)(2,1)}, s32[8]{0:T(128)}) custom-call(bf16[64,1152]{1,0:T(8,128)(2,1)} %copy-done.9, bf16[64,1152]{1,0:T(8,128)(2,1)} %copy-done.13, bf16[64,1152]{1,0:T(8,128)(2,1)} %copy-done.14, bf16[64,1152]{1,0:T(8,128)(2,1)} %copy-done.15, bf16[64,1152]{1,0:T(8,128)(2,1)} %copy-done.17, bf16[64,1152]{1,0:T(8,128)(2,1)} %copy-done.18, ...), custom_call_target="tpu_custom_call" | custom-call | tf_op jit(solution)/shard_map/pallas_call | solution.py:242
  49.9 2.5 %collective-permute-start.13 = (bf16[512,128]{1,0:T(8,128)(2,1)S(1)}, bf16[512,128]{1,0:T(8,128)(2,1)S(1)}, u32[]{:S(2)}, u32[]{:S(2)}) collective-permute-start(bf16[512,128]{1,0:T(8,128)(2,1)S(1)} %add_convert_fusion.refs_0_), channel_id=1, source_target_pairs={{0,6},{1,7},{2,0},{3,1},{4,2},{5,3},{6,4},{7,5},{8,14},{9,15},{10,... | collective-permute-start | bytes 393224 | tf_op jit(solution)/shard_map/ppermute | solution.py:468
  53.0 3.9 %collective-permute-done.12.refs_2_ = bf16[512,128]{1,0:T(8,128)(2,1)S(1)} collective-permute-done((bf16[512,128]{1,0:T(8,128)(2,1)S(1)}, bf16[512,128]{1,0:T(8,128)(2,1)S(1)}, u32[]{:S(2)}, u32[]{:S(2)}) %collective-permute-start.12) | collective-permute-done | bytes 131104 | tf_op jit(solution)/shard_map/ppermute | solution.py:468
  58.5 4.2 %shard_map.192 = (bf16[64,1152]{1,0:T(8,128)(2,1)}, bf16[64,1152]{1,0:T(8,128)(2,1)}, bf16[64,1152]{1,0:T(8,128)(2,1)}, bf16[64,1152]{1,0:T(8,128)(2,1)}, bf16[3...) custom-call(s32[8]{0:T(128)} %get-tuple-element.106.names, ...), custom_call_target="tpu_custom_call" | custom-call | tf_op jit(solution)/shard_map/pallas_call | solution.py:313
  64.8 3.8 %collective-permute-start.14 = (bf16[64,1152]{1,0:T(8,128)(2,1)}, bf16[64,1152]{1,0:T(8,128)(2,1)S(1)}, u32[]{:S(2)}, u32[]{:S(2)}) collective-permute-start(bf16[64,1152]{1,0:T(8,128)(2,1)} %get-tuple-element.109), channel_id=1, source_target_pairs={{0,32},{32,64},{64,96},{96,128},{128,160},{160,192},{192,224},{224... | collective-permute-start | bytes 442376 | tf_op jit(solution)/shard_map/ppermute | solution.py:29
  68.5 5.2 %collective-permute-done.17 = bf16[32,1152]{1,0:T(8,128)(2,1)S(1)} collective-permute-done((bf16[32,1152]{1,0:T(8,128)(2,1)}, bf16[32,1152]{1,0:T(8,128)(2,1)S(1)}, u32[]{:S(2)}, u32[]{:S(2)}) %collective-permute-start.17) | collective-permute-done | bytes 73760 | tf_op jit(solution)/shard_map/ppermute | solution.py:29
  75.8 2.0 %collective-permute-start.18 = (bf16[64,1152]{1,0:T(8,128)(2,1)S(1)}, bf16[64,1152]{1,0:T(8,128)(2,1)S(1)}, u32[]{:S(2)}, u32[]{:S(2)}) collective-permute-start(bf16[64,1152]{1,0:T(8,128)(2,1)S(1)} %pad_maximum_fusion.1), channel_id=1, source_target_pairs={{0,64},{32,96},{64,128},{96,160},{128,192},{160,224},{192,0},{224,... | collective-permute-start | bytes 442376 | tf_op jit(solution)/shard_map/ppermute | solution.py:29
  80.3 2.2 %collective-permute-start.21 = (bf16[64,1152]{1,0:T(8,128)(2,1)S(1)}, bf16[64,1152]{1,0:T(8,128)(2,1)S(1)}, u32[]{:S(2)}, u32[]{:S(2)}) collective-permute-start(bf16[64,1152]{1,0:T(8,128)(2,1)S(1)} %pad_maximum_fusion.2), channel_id=1, source_target_pairs={{0,192},{32,224},{64,0},{96,32},{128,64},{160,96},{192,128},{224,1... | collective-permute-start | bytes 442376 | tf_op jit(solution)/shard_map/ppermute | solution.py:29
  83.2 3.2 %collective-permute-done.21.refs_4_ = bf16[64,1152]{1,0:T(8,128)(2,1)S(1)} collective-permute-done((bf16[64,1152]{1,0:T(8,128)(2,1)S(1)}, bf16[64,1152]{1,0:T(8,128)(2,1)S(1)}, u32[]{:S(2)}, u32[]{:S(2)}) %collective-permute-start.21) | collective-permute-done | bytes 147488 | tf_op jit(solution)/shard_map/ppermute | solution.py:29
  87.1 2.8 %shard_map.193 = (f32[64,1024]{1,0:T(8,128)}, f32[64,1024]{1,0:T(8,128)}, f32[64,1024]{1,0:T(8,128)}, f32[64,128]{1,0:T(8,128)}, f32[64,128]{1,0:T(8,128)}, /*index=5*/f32[64,128]{1,0:T(8,128)}, bf16[64,1152]{1,0:T(8,128)(2,1)}) custom-call(bf16[64,1152]{1,0:T(8,128)(2,1)} %get-tuple-element.108.refs_0_, bf16[64,1152]{1,0:T(8,128)(2,1)} %copy-done.11, ...), custom_call_target="tpu_custom_call" | custom-call | tf_op jit(solution)/shard_map/pallas_call | solution.py:365
  89.9 3.6 %collective-permute-start.22 = (bf16[64,1152]{1,0:T(8,128)(2,1)}, bf16[64,1152]{1,0:T(8,128)(2,1)S(1)}, u32[]{:S(2)}, u32[]{:S(2)}) collective-permute-start(bf16[64,1152]{1,0:T(8,128)(2,1)} %get-tuple-element.135.refs_0_), channel_id=1, source_target_pairs={{0,8},{8,16},{16,24},{24,0},{1,9},{9,17},{17,25},{25,1},{2,10},{10... | collective-permute-start | bytes 442376 | tf_op jit(solution)/shard_map/ppermute | solution.py:29
  95.2 3.5 %shard_map.194 = (f32[128,128]{1,0:T(8,128)}, bf16[128,1024]{1,0:T(8,128)(2,1)}) custom-call(s32[1]{0:T(128)} %bitcast.3.tensor, bf16[128,2,8192]{2,1,0:T(2,128)(2,1)} %bitcast.23, bf16[8192,128]{1,0:T(8,128)(2,1)} %weight.3), custom_call_target="tpu_custom_call" | custom-call | tf_op jit(solution)/shard_map/pallas_call | solution.py:188
  104.1 2.7 %collective-permute-start.28 = (bf16[64,1152]{1,0:T(8,128)(2,1)S(1)}, bf16[64,1152]{1,0:T(8,128)(2,1)S(1)}, u32[]{:S(2)}, u32[]{:S(2)}) collective-permute-start(bf16[64,1152]{1,0:T(8,128)(2,1)S(1)} %shard_map.195.refs_2_.refs_6_), channel_id=1, source_target_pairs={{0,192},{32,224},{64,0},{96,32},{128,64},{160,96},{192,128},{224,1... | collective-permute-start | bytes 442376 | tf_op jit(solution)/shard_map/ppermute | solution.py:29
  106.8 2.9 %collective-permute-start.25 = (bf16[64,1152]{1,0:T(8,128)(2,1)S(1)}, bf16[64,1152]{1,0:T(8,128)(2,1)S(1)}, u32[]{:S(2)}, u32[]{:S(2)}) collective-permute-start(bf16[64,1152]{1,0:T(8,128)(2,1)S(1)} %shard_map.195.refs_2_.refs_6_), channel_id=1, source_target_pairs={{0,32},{32,64},{64,96},{96,128},{128,160},{160,192},{192,224},{224... | collective-permute-start | bytes 442376 | tf_op jit(solution)/shard_map/ppermute | solution.py:29
  110.0 2.2 %collective-permute-done.27.refs_5_.refs_9_ = bf16[64,1152]{1,0:T(8,128)(2,1)S(1)} collective-permute-done((bf16[64,1152]{1,0:T(8,128)(2,1)S(1)}, bf16[64,1152]{1,0:T(8,128)(2,1)S(1)}, u32[]{:S(2)}, u32[]{:S(2)}) %collective-permute-start.27) | collective-permute-done | bytes 147488 | tf_op jit(solution)/shard_map/ppermute | solution.py:29
  112.2 2.6 %collective-permute-start.29 = (bf16[64,1152]{1,0:T(8,128)(2,1)S(1)}, bf16[64,1152]{1,0:T(8,128)(2,1)S(1)}, u32[]{:S(2)}, u32[]{:S(2)}) collective-permute-start(bf16[64,1152]{1,0:T(8,128)(2,1)S(1)} %collective-permute-done.27.refs_5_.refs_9_), channel_id=1, source_target_pairs={{0,32},{32,64},{64,96},{96,128},{128,160},{160,192},{192,224},{224... | collective-permute-start | bytes 442376 | tf_op jit(solution)/shard_map/ppermute | solution.py:29
  117.3 2.1 %collective-permute-done.29.refs_7_.refs_11_ = bf16[64,1152]{1,0:T(8,128)(2,1)S(1)} collective-permute-done((bf16[64,1152]{1,0:T(8,128)(2,1)S(1)}, bf16[64,1152]{1,0:T(8,128)(2,1)S(1)}, u32[]{:S(2)}, u32[]{:S(2)}) %collective-permute-start.29) | collective-permute-done | bytes 147488 | tf_op jit(solution)/shard_map/ppermute | solution.py:29
  119.9 3.6 %collective-permute-done.31.refs_9_.refs_13_ = bf16[64,1152]{1,0:T(8,128)(2,1)S(1)} collective-permute-done((bf16[64,1152]{1,0:T(8,128)(2,1)S(1)}, bf16[64,1152]{1,0:T(8,128)(2,1)S(1)}, u32[]{:S(2)}, u32[]{:S(2)}) %collective-permute-start.31) | collective-permute-done | bytes 147488 | tf_op jit(solution)/shard_map/ppermute | solution.py:29
  127.4 2.5 %collective-permute-start.33 = (f32[32,256]{1,0:T(8,128)S(1)}, f32[32,256]{1,0:T(8,128)S(1)}, u32[]{:S(2)}, u32[]{:S(2)}) collective-permute-start(f32[32,256]{1,0:T(8,128)S(1)} %add.81.refs_2_), channel_id=1, source_target_pairs={{0,2},{1,3},{2,4},{3,5},{4,6},{5,7},{6,0},{7,1},{8,10},{9,11},{10,... | collective-permute-start | bytes 98312 | tf_op jit(solution)/shard_map/ppermute | solution.py:468
  130.5 2.5 %collective-permute-start.35 = (f32[32,256]{1,0:T(8,128)S(1)}, f32[32,256]{1,0:T(8,128)S(1)}, u32[]{:S(2)}, u32[]{:S(2)}) collective-permute-start(f32[32,256]{1,0:T(8,128)S(1)} %add.81.refs_2_), channel_id=1, source_target_pairs={{0,6},{1,7},{2,0},{3,1},{4,2},{5,3},{6,4},{7,5},{8,14},{9,15},{10,... | collective-permute-start | bytes 98312 | tf_op jit(solution)/shard_map/ppermute | solution.py:468
  133.1 2.2 %collective-permute-done.34.refs_4_ = f32[32,256]{1,0:T(8,128)S(1)} collective-permute-done((f32[32,256]{1,0:T(8,128)S(1)}, f32[32,256]{1,0:T(8,128)S(1)}, u32[]{:S(2)}, u32[]{:S(2)}) %collective-permute-start.34) | collective-permute-done | bytes 32800 | tf_op jit(solution)/shard_map/ppermute | solution.py:468
  (127 shorter events, 33.2 us)
Async XLA Ops:
  4.7 34.9 %collective-permute-start = (bf16[272,1152]{1,0:T(8,128)(2,1)}, bf16[272,1152]{1,0:T(8,128)(2,1)S(1)}, u32[]{:S(2)}, u32[]{:S(2)}) collective-permute-start(bf16[272,1152]{1,0:T(8,128)(2,1)} %get-tuple-element.78), channel_id=1, source_target_pairs={{0,8},{8,16},{16,24},{24,0},{1,9},{9,17},{17,25},{25,1},{2,10},{10... | collective-permute-start | bytes 1880072 | tf_op jit(solution)/shard_map/ppermute | solution.py:29
  5.3 34.4 %collective-permute-start.1 = (bf16[272,1152]{1,0:T(8,128)(2,1)}, bf16[272,1152]{1,0:T(8,128)(2,1)S(1)}, u32[]{:S(2)}, u32[]{:S(2)}) collective-permute-start(bf16[272,1152]{1,0:T(8,128)(2,1)} %get-tuple-element.79), channel_id=1, source_target_pairs={{0,16},{8,24},{16,0},{24,8},{1,17},{9,25},{17,1},{25,9},{2,18},{10... | collective-permute-start | bytes 1880072 | tf_op jit(solution)/shard_map/ppermute | solution.py:29
  7.7 32.0 %collective-permute-start.2 = (bf16[272,1152]{1,0:T(8,128)(2,1)}, bf16[272,1152]{1,0:T(8,128)(2,1)S(1)}, u32[]{:S(2)}, u32[]{:S(2)}) collective-permute-start(bf16[272,1152]{1,0:T(8,128)(2,1)} %get-tuple-element.80), channel_id=1, source_target_pairs={{0,24},{8,0},{16,8},{24,16},{1,25},{9,1},{17,9},{25,17},{2,26},{10... | collective-permute-start | bytes 1880072 | tf_op jit(solution)/shard_map/ppermute | solution.py:29
  7.8 9.2 %collective-permute-start.3 = (bf16[64,1152]{1,0:T(8,128)(2,1)S(1)}, bf16[64,1152]{1,0:T(8,128)(2,1)S(1)}, u32[]{:S(2)}, u32[]{:S(2)}) collective-permute-start(bf16[64,1152]{1,0:T(8,128)(2,1)S(1)} %pad_maximum_fusion.refs_0_), channel_id=1, source_target_pairs={{0,32},{32,64},{64,96},{96,128},{128,160},{160,192},{192,224},{224... | collective-permute-start | bytes 442376 | tf_op jit(solution)/shard_map/ppermute | solution.py:29
  9.8 7.2 %collective-permute-start.4 = (bf16[64,1152]{1,0:T(8,128)(2,1)S(1)}, bf16[64,1152]{1,0:T(8,128)(2,1)S(1)}, u32[]{:S(2)}, u32[]{:S(2)}) collective-permute-start(bf16[64,1152]{1,0:T(8,128)(2,1)S(1)} %pad_maximum_fusion.refs_0_), channel_id=1, source_target_pairs={{0,224},{32,0},{64,32},{96,64},{128,96},{160,128},{192,160},{224,1... | collective-permute-start | bytes 442376 | tf_op jit(solution)/shard_map/ppermute | solution.py:29
  17.0 6.4 %collective-permute-start.5 = (bf16[64,1152]{1,0:T(8,128)(2,1)S(1)}, bf16[64,1152]{1,0:T(8,128)(2,1)S(1)}, u32[]{:S(2)}, u32[]{:S(2)}) collective-permute-start(bf16[64,1152]{1,0:T(8,128)(2,1)S(1)} %collective-permute-done.3.refs_1_), channel_id=1, source_target_pairs={{0,32},{32,64},{64,96},{96,128},{128,160},{160,192},{192,224},{224... | collective-permute-start | bytes 442376 | tf_op jit(solution)/shard_map/ppermute | solution.py:29
  17.0 6.3 %collective-permute-start.6 = (bf16[64,1152]{1,0:T(8,128)(2,1)S(1)}, bf16[64,1152]{1,0:T(8,128)(2,1)S(1)}, u32[]{:S(2)}, u32[]{:S(2)}) collective-permute-start(bf16[64,1152]{1,0:T(8,128)(2,1)S(1)} %collective-permute-done.4.refs_2_), channel_id=1, source_target_pairs={{0,224},{32,0},{64,32},{96,64},{128,96},{160,128},{192,160},{224,1... | collective-permute-start | bytes 442376 | tf_op jit(solution)/shard_map/ppermute | solution.py:29
  23.3 6.4 %collective-permute-start.7 = (bf16[64,1152]{1,0:T(8,128)(2,1)S(1)}, bf16[64,1152]{1,0:T(8,128)(2,1)S(1)}, u32[]{:S(2)}, u32[]{:S(2)}) collective-permute-start(bf16[64,1152]{1,0:T(8,128)(2,1)S(1)} %collective-permute-done.5.refs_3_), channel_id=1, source_target_pairs={{0,32},{32,64},{64,96},{96,128},{128,160},{160,192},{192,224},{224... | collective-permute-start | bytes 442376 | tf_op jit(solution)/shard_map/ppermute | solution.py:29
  23.4 6.3 %collective-permute-start.8 = (bf16[64,1152]{1,0:T(8,128)(2,1)S(1)}, bf16[64,1152]{1,0:T(8,128)(2,1)S(1)}, u32[]{:S(2)}, u32[]{:S(2)}) collective-permute-start(bf16[64,1152]{1,0:T(8,128)(2,1)S(1)} %collective-permute-done.6.refs_4_), channel_id=1, source_target_pairs={{0,224},{32,0},{64,32},{96,64},{128,96},{160,128},{192,160},{224,1... | collective-permute-start | bytes 442376 | tf_op jit(solution)/shard_map/ppermute | solution.py:29
  29.7 6.4 %collective-permute-start.9 = (bf16[64,1152]{1,0:T(8,128)(2,1)S(1)}, bf16[64,1152]{1,0:T(8,128)(2,1)S(1)}, u32[]{:S(2)}, u32[]{:S(2)}) collective-permute-start(bf16[64,1152]{1,0:T(8,128)(2,1)S(1)} %collective-permute-done.7.refs_5_), channel_id=1, source_target_pairs={{0,32},{32,64},{64,96},{96,128},{128,160},{160,192},{192,224},{224... | collective-permute-start | bytes 442376 | tf_op jit(solution)/shard_map/ppermute | solution.py:29
  47.3 5.7 %collective-permute-start.11 = (bf16[512,128]{1,0:T(8,128)(2,1)S(1)}, bf16[512,128]{1,0:T(8,128)(2,1)S(1)}, u32[]{:S(2)}, u32[]{:S(2)}) collective-permute-start(bf16[512,128]{1,0:T(8,128)(2,1)S(1)} %add_convert_fusion.refs_0_), channel_id=1, source_target_pairs={{0,2},{1,3},{2,4},{3,5},{4,6},{5,7},{6,0},{7,1},{8,10},{9,11},{10,... | collective-permute-start | bytes 393224 | tf_op jit(solution)/shard_map/ppermute | solution.py:468
  49.0 7.9 %collective-permute-start.12 = (bf16[512,128]{1,0:T(8,128)(2,1)S(1)}, bf16[512,128]{1,0:T(8,128)(2,1)S(1)}, u32[]{:S(2)}, u32[]{:S(2)}) collective-permute-start(bf16[512,128]{1,0:T(8,128)(2,1)S(1)} %add_convert_fusion.refs_0_), channel_id=1, source_target_pairs={{0,4},{1,5},{2,6},{3,7},{4,0},{5,1},{6,2},{7,3},{8,12},{9,13},{10,... | collective-permute-start | bytes 393224 | tf_op jit(solution)/shard_map/ppermute | solution.py:468
  49.9 8.0 %collective-permute-start.13 = (bf16[512,128]{1,0:T(8,128)(2,1)S(1)}, bf16[512,128]{1,0:T(8,128)(2,1)S(1)}, u32[]{:S(2)}, u32[]{:S(2)}) collective-permute-start(bf16[512,128]{1,0:T(8,128)(2,1)S(1)} %add_convert_fusion.refs_0_), channel_id=1, source_target_pairs={{0,6},{1,7},{2,0},{3,1},{4,2},{5,3},{6,4},{7,5},{8,14},{9,15},{10,... | collective-permute-start | bytes 393224 | tf_op jit(solution)/shard_map/ppermute | solution.py:468
  62.7 12.0 %collective-permute-start.16 = (bf16[64,1152]{1,0:T(8,128)(2,1)}, bf16[64,1152]{1,0:T(8,128)(2,1)S(1)}, u32[]{:S(2)}, u32[]{:S(2)}) collective-permute-start(bf16[64,1152]{1,0:T(8,128)(2,1)} %get-tuple-element.112), channel_id=1, source_target_pairs={{0,32},{32,64},{64,96},{96,128},{128,160},{160,192},{192,224},{224... | collective-permute-start | bytes 442376 | tf_op jit(solution)/shard_map/ppermute | solution.py:29
  62.8 10.9 %collective-permute-start.17 = (bf16[32,1152]{1,0:T(8,128)(2,1)}, bf16[32,1152]{1,0:T(8,128)(2,1)S(1)}, u32[]{:S(2)}, u32[]{:S(2)}) collective-permute-start(bf16[32,1152]{1,0:T(8,128)(2,1)} %get-tuple-element.113), channel_id=1, source_target_pairs={{0,64},{32,96},{64,128},{96,160},{128,192},{160,224},{192,0},{224,... | collective-permute-start | bytes 221192 | tf_op jit(solution)/shard_map/ppermute | solution.py:29
  64.8 17.9 %collective-permute-start.14 = (bf16[64,1152]{1,0:T(8,128)(2,1)}, bf16[64,1152]{1,0:T(8,128)(2,1)S(1)}, u32[]{:S(2)}, u32[]{:S(2)}) collective-permute-start(bf16[64,1152]{1,0:T(8,128)(2,1)} %get-tuple-element.109), channel_id=1, source_target_pairs={{0,32},{32,64},{64,96},{96,128},{128,160},{160,192},{192,224},{224... | collective-permute-start | bytes 442376 | tf_op jit(solution)/shard_map/ppermute | solution.py:29
  68.5 14.1 %collective-permute-start.15 = (bf16[64,1152]{1,0:T(8,128)(2,1)}, bf16[64,1152]{1,0:T(8,128)(2,1)S(1)}, u32[]{:S(2)}, u32[]{:S(2)}) collective-permute-start(bf16[64,1152]{1,0:T(8,128)(2,1)} %get-tuple-element.110), channel_id=1, source_target_pairs={{0,224},{32,0},{64,32},{96,64},{128,96},{160,128},{192,160},{224,1... | collective-permute-start | bytes 442376 | tf_op jit(solution)/shard_map/ppermute | solution.py:29
  68.5 10.8 %collective-permute-start.19 = (bf16[64,1152]{1,0:T(8,128)(2,1)}, bf16[64,1152]{1,0:T(8,128)(2,1)S(1)}, u32[]{:S(2)}, u32[]{:S(2)}) collective-permute-start(bf16[64,1152]{1,0:T(8,128)(2,1)} %get-tuple-element.115), channel_id=1, source_target_pairs={{0,224},{32,0},{64,32},{96,64},{128,96},{160,128},{192,160},{224,1... | collective-permute-start | bytes 442376 | tf_op jit(solution)/shard_map/ppermute | solution.py:29
  73.8 5.6 %collective-permute-start.20 = (bf16[32,1152]{1,0:T(8,128)(2,1)}, bf16[32,1152]{1,0:T(8,128)(2,1)S(1)}, u32[]{:S(2)}, u32[]{:S(2)}) collective-permute-start(bf16[32,1152]{1,0:T(8,128)(2,1)} %get-tuple-element.116), channel_id=1, source_target_pairs={{0,192},{32,224},{64,0},{96,32},{128,64},{160,96},{192,128},{224,1... | collective-permute-start | bytes 221192 | tf_op jit(solution)/shard_map/ppermute | solution.py:29
  75.8 7.4 %collective-permute-start.18 = (bf16[64,1152]{1,0:T(8,128)(2,1)S(1)}, bf16[64,1152]{1,0:T(8,128)(2,1)S(1)}, u32[]{:S(2)}, u32[]{:S(2)}) collective-permute-start(bf16[64,1152]{1,0:T(8,128)(2,1)S(1)} %pad_maximum_fusion.1), channel_id=1, source_target_pairs={{0,64},{32,96},{64,128},{96,160},{128,192},{160,224},{192,0},{224,... | collective-permute-start | bytes 442376 | tf_op jit(solution)/shard_map/ppermute | solution.py:29
  80.3 6.1 %collective-permute-start.21 = (bf16[64,1152]{1,0:T(8,128)(2,1)S(1)}, bf16[64,1152]{1,0:T(8,128)(2,1)S(1)}, u32[]{:S(2)}, u32[]{:S(2)}) collective-permute-start(bf16[64,1152]{1,0:T(8,128)(2,1)S(1)} %pad_maximum_fusion.2), channel_id=1, source_target_pairs={{0,192},{32,224},{64,0},{96,32},{128,64},{160,96},{192,128},{224,1... | collective-permute-start | bytes 442376 | tf_op jit(solution)/shard_map/ppermute | solution.py:29
  89.9 8.9 %collective-permute-start.22 = (bf16[64,1152]{1,0:T(8,128)(2,1)}, bf16[64,1152]{1,0:T(8,128)(2,1)S(1)}, u32[]{:S(2)}, u32[]{:S(2)}) collective-permute-start(bf16[64,1152]{1,0:T(8,128)(2,1)} %get-tuple-element.135.refs_0_), channel_id=1, source_target_pairs={{0,8},{8,16},{16,24},{24,0},{1,9},{9,17},{17,25},{25,1},{2,10},{10... | collective-permute-start | bytes 442376 | tf_op jit(solution)/shard_map/ppermute | solution.py:29
  93.5 6.9 %collective-permute-start.23 = (bf16[64,1152]{1,0:T(8,128)(2,1)}, bf16[64,1152]{1,0:T(8,128)(2,1)S(1)}, u32[]{:S(2)}, u32[]{:S(2)}) collective-permute-start(bf16[64,1152]{1,0:T(8,128)(2,1)} %get-tuple-element.135.refs_0_), channel_id=1, source_target_pairs={{0,16},{8,24},{16,0},{24,8},{1,17},{9,25},{17,1},{25,9},{2,18},{10... | collective-permute-start | bytes 442376 | tf_op jit(solution)/shard_map/ppermute | solution.py:29
  94.7 7.2 %collective-permute-start.24 = (bf16[64,1152]{1,0:T(8,128)(2,1)}, bf16[64,1152]{1,0:T(8,128)(2,1)S(1)}, u32[]{:S(2)}, u32[]{:S(2)}) collective-permute-start(bf16[64,1152]{1,0:T(8,128)(2,1)} %get-tuple-element.135.refs_0_), channel_id=1, source_target_pairs={{0,24},{8,0},{16,8},{24,16},{1,25},{9,1},{17,9},{25,17},{2,26},{10... | collective-permute-start | bytes 442376 | tf_op jit(solution)/shard_map/ppermute | solution.py:29
  102.5 9.7 %collective-permute-start.27 = (bf16[64,1152]{1,0:T(8,128)(2,1)S(1)}, bf16[64,1152]{1,0:T(8,128)(2,1)S(1)}, u32[]{:S(2)}, u32[]{:S(2)}) collective-permute-start(bf16[64,1152]{1,0:T(8,128)(2,1)S(1)} %shard_map.195.refs_2_.refs_6_), channel_id=1, source_target_pairs={{0,64},{32,96},{64,128},{96,160},{128,192},{160,224},{192,0},{224,... | collective-permute-start | bytes 442376 | tf_op jit(solution)/shard_map/ppermute | solution.py:29
  104.1 10.7 %collective-permute-start.28 = (bf16[64,1152]{1,0:T(8,128)(2,1)S(1)}, bf16[64,1152]{1,0:T(8,128)(2,1)S(1)}, u32[]{:S(2)}, u32[]{:S(2)}) collective-permute-start(bf16[64,1152]{1,0:T(8,128)(2,1)S(1)} %shard_map.195.refs_2_.refs_6_), channel_id=1, source_target_pairs={{0,192},{32,224},{64,0},{96,32},{128,64},{160,96},{192,128},{224,1... | collective-permute-start | bytes 442376 | tf_op jit(solution)/shard_map/ppermute | solution.py:29
  106.8 10.5 %collective-permute-start.25 = (bf16[64,1152]{1,0:T(8,128)(2,1)S(1)}, bf16[64,1152]{1,0:T(8,128)(2,1)S(1)}, u32[]{:S(2)}, u32[]{:S(2)}) collective-permute-start(bf16[64,1152]{1,0:T(8,128)(2,1)S(1)} %shard_map.195.refs_2_.refs_6_), channel_id=1, source_target_pairs={{0,32},{32,64},{64,96},{96,128},{128,160},{160,192},{192,224},{224... | collective-permute-start | bytes 442376 | tf_op jit(solution)/shard_map/ppermute | solution.py:29
  109.7 7.6 %collective-permute-start.26 = (bf16[64,1152]{1,0:T(8,128)(2,1)S(1)}, bf16[64,1152]{1,0:T(8,128)(2,1)S(1)}, u32[]{:S(2)}, u32[]{:S(2)}) collective-permute-start(bf16[64,1152]{1,0:T(8,128)(2,1)S(1)} %shard_map.195.refs_2_.refs_6_), channel_id=1, source_target_pairs={{0,224},{32,0},{64,32},{96,64},{128,96},{160,128},{192,160},{224,1... | collective-permute-start | bytes 442376 | tf_op jit(solution)/shard_map/ppermute | solution.py:29
  112.2 7.2 %collective-permute-start.29 = (bf16[64,1152]{1,0:T(8,128)(2,1)S(1)}, bf16[64,1152]{1,0:T(8,128)(2,1)S(1)}, u32[]{:S(2)}, u32[]{:S(2)}) collective-permute-start(bf16[64,1152]{1,0:T(8,128)(2,1)S(1)} %collective-permute-done.27.refs_5_.refs_9_), channel_id=1, source_target_pairs={{0,32},{32,64},{64,96},{96,128},{128,160},{160,192},{192,224},{224... | collective-permute-start | bytes 442376 | tf_op jit(solution)/shard_map/ppermute | solution.py:29
  116.0 7.6 %collective-permute-start.31 = (bf16[64,1152]{1,0:T(8,128)(2,1)S(1)}, bf16[64,1152]{1,0:T(8,128)(2,1)S(1)}, u32[]{:S(2)}, u32[]{:S(2)}) collective-permute-start(bf16[64,1152]{1,0:T(8,128)(2,1)S(1)} %collective-permute-done.27.refs_5_.refs_9_), channel_id=1, source_target_pairs={{0,64},{32,96},{64,128},{96,160},{128,192},{160,224},{192,0},{224,... | collective-permute-start | bytes 442376 | tf_op jit(solution)/shard_map/ppermute | solution.py:29
  127.4 5.7 %collective-permute-start.33 = (f32[32,256]{1,0:T(8,128)S(1)}, f32[32,256]{1,0:T(8,128)S(1)}, u32[]{:S(2)}, u32[]{:S(2)}) collective-permute-start(f32[32,256]{1,0:T(8,128)S(1)} %add.81.refs_2_), channel_id=1, source_target_pairs={{0,2},{1,3},{2,4},{3,5},{4,6},{5,7},{6,0},{7,1},{8,10},{9,11},{10,... | collective-permute-start | bytes 98312 | tf_op jit(solution)/shard_map/ppermute | solution.py:468
  129.9 5.4 %collective-permute-start.34 = (f32[32,256]{1,0:T(8,128)S(1)}, f32[32,256]{1,0:T(8,128)S(1)}, u32[]{:S(2)}, u32[]{:S(2)}) collective-permute-start(f32[32,256]{1,0:T(8,128)S(1)} %add.81.refs_2_), channel_id=1, source_target_pairs={{0,4},{1,5},{2,6},{3,7},{4,0},{5,1},{6,2},{7,3},{8,12},{9,13},{10,... | collective-permute-start | bytes 98312 | tf_op jit(solution)/shard_map/ppermute | solution.py:468
  (32 other events, 337.3 us)
where the time goes:
time: 138 us; the launch traced here: 136 us
  starting transfers between devices  54.9 us (40%)
  waiting for transfers between devices  48.1 us (35%)
  Pallas kernels  25 us (18%)
  local copies, waits for them, and re-layouts  3.92 us (3%)
  other arithmetic  3.36 us (2%)
    ppermute x28, starting transfers between devices, shift(): lax.ppermute(x, axis, [(i, (i + distance) % size) for i in range(size)])  44 us
    ppermute x28, waiting for transfers between devices, shift(): lax.ppermute(x, axis, [(i, (i + distance) % size) for i in range(size)])  37.9 us
    ppermute x6, starting transfers between devices, tensor_parts(): lax.ppermute(x, 'tensor', [(i, (i + 2 * d) % size) for i in range(size)])  10.7 us
    ppermute x6, waiting for transfers between devices, tensor_parts(): lax.ppermute(x, 'tensor', [(i, (i + 2 * d) % size) for i in range(size)])  7.44 us
    pallas_call x2, Pallas kernels, frozen(): pl.pallas_call(frozen_kernel, grid_spec=pltpu.PrefetchScalarGridSpec(num_...  7.02 us
    pallas_call x1, Pallas kernels, grad(): pl.pallas_call(functools.partial(grad_kernel, rank, rows, len(lows), owne...  4.18 us
    pallas_call x1, Pallas kernels, begin(): pl.pallas_call(functools.partial(begin_kernel, rows, groups), in_specs=sm...  4.05 us
    pallas_call x1, Pallas kernels, low(): pl.pallas_call(functools.partial(low_kernel, rank, rows, size, owned, fir...  3.79 us
  transfers between devices with their start and end apart: 36, of which 20 were waited for; matrix products, arithmetic and copies ran while one was open for 2% of the time, Pallas kernels for 5%

commit v1 on v0

--- a/solution.py
+++ b/solution.py
@@ -57,15 +57,16 @@
 def two_stage_reduce(x, size):
     upper, lower = x[size // 2], x[-1]
     half = upper.shape[0]
-    after = [shift(x[3], "dp", 1), shift(upper, "dp", 2)]
-    before = [shift(x[5], "dp", -1), shift(lower, "dp", -2)]
+    after, before = shift(x[3], "dp", 1), shift(x[5], "dp", -1)
+    far_after, far_before = shift(upper, "dp", 2), shift(lower, "dp", -2)
+    after, before, one, other = lax.optimization_barrier((after, before, x[1], x[7]))
+    near = [shift(one, "dp", 1), shift(other, "dp", -1)]
     ahead = jnp.concatenate(
-        [add(x[2][:half], after[0][:half], after[1]), add(x[2][half:], after[0][half:])]
+        [add(x[2][:half], after[:half], far_after), add(x[2][half:], after[half:])]
     )
     behind = jnp.concatenate(
-        [add(x[6][:half], before[0][:half]), add(x[6][half:], before[0][half:], before[1])]
-    )
-    near = [shift(x[1], "dp", 1), shift(x[7], "dp", -1)]
+        [add(x[6][:half], before[:half]), add(x[6][half:], before[half:], far_before)]
+    )
     return [*near, shift(ahead, "dp", 2), shift(behind, "dp", -2)]
 
 
@@ -77,6 +78,7 @@
 smem = functools.partial(spot, pltpu.SMEM)
 anywhere = functools.partial(spot, pl.ANY)
 SMALL = pltpu.CompilerParams(vmem_limit_bytes=14 * MIB)
+MIDDLE = pltpu.CompilerParams(vmem_limit_bytes=52 * MIB)
 LARGE = pltpu.CompilerParams(vmem_limit_bytes=61 * MIB)
 
 
@@ -180,7 +182,7 @@
             x_out[...] = block[:, i * width : (i + 1) * width]
 
 
-def frozen(tensor, requests, weight, part, parts, width):
+def frozen(tensor, requests, weight, part, parts, width, params):
     count = requests.shape[0] // parts
     steps = requests.shape[1]
     width_b = weight.shape[1]
@@ -200,14 +202,15 @@
             ],
         ),
         out_shape=[shape((count * steps, width_b), F32), shape((count * steps, width))],
-        compiler_params=LARGE,
+        compiler_params=params,
     )(tensor, requests, weight)
 
 
 def low_kernel(rank, rows, size, owned, firsts, *refs):
     parts = len(firsts)
     tables, refs = refs[:parts], refs[parts:]
-    *blocks, out, names, table, here, sems = refs
+    *blocks, mine, his, names, table, here, both, sems = refs
+    core = lax.rem(lax.axis_index("tensor"), 2)
     wide = table.shape[1]
     width = wide - 128
     row = lax.axis_index("dp")
@@ -220,7 +223,6 @@
     copies = fetch([*tables, *blocks], rooms, sems)
     for copy in copies[:parts]:
         copy.wait()
-    half = used // rows * len(blocks) * rank
     for s in range(2 * len(blocks)):
         if s % 2 == 0:
             copies[parts + s // 2].wait()
@@ -232,8 +234,10 @@
         chosen = block_of(table, place, rank)[...]
         low_in = dot(chosen[:, :width], block[:, :width], ((1,), (1,)))
         low_back = dot(chosen[:, width:], block[:, width:], ((1,), (1,)))
-        out[s * rank : (s + 1) * rank, :] = low_in.astype(BF)
-        out[half + s * rank : half + (s + 1) * rank, :] = low_back.astype(BF)
+        both[0, s * rank : (s + 1) * rank, :] = low_in.astype(BF)
+        both[1, s * rank : (s + 1) * rank, :] = low_back.astype(BF)
+    mine[...] = both[core]
+    his[...] = both[1 - core]
 
 
 def low(tables, firsts, blocks, rank, rows, size, owned):
@@ -242,14 +246,16 @@
     return pl.pallas_call(
         functools.partial(low_kernel, rank, rows, size, owned, firsts),
         in_specs=anywhere(len(tables) + len(blocks)),
-        out_specs=vmem() + smem(),
+        out_specs=vmem(2) + smem(),
         out_shape=[
-            shape((4 * len(blocks) * rank, rows)),
+            shape((2 * len(blocks) * rank, rows)),
+            shape((2 * len(blocks) * rank, rows)),
             shape((2 * len(blocks),), jnp.int32),
         ],
         scratch_shapes=[
             pltpu.VMEM((total, wide), BF),
             pltpu.VMEM((len(blocks),) + blocks[0].shape, BF),
+            pltpu.VMEM((2, 2 * len(blocks) * rank, rows), BF),
             pltpu.SemaphoreType.DMA((len(tables) + len(blocks),)),
         ],
         compiler_params=LARGE,
@@ -265,7 +271,8 @@
 
 def grad_kernel(rank, rows, parts, owned, names, *refs):
     lows, refs = refs[:parts], refs[parts:]
-    groups = lows[0].shape[0] // (4 * rank)
+    groups = lows[0].shape[0] // (2 * rank)
+    core = lax.rem(lax.axis_index("tensor"), 2)
     blocks, refs = refs[:groups], refs[groups:]
     *outs, sums, lows_here, here, half, sems, out_sems = refs
     width = sums.shape[2] - 128
@@ -279,14 +286,12 @@
     sums[...] = jnp.zeros_like(sums)
     for copy in copies[:parts]:
         copy.wait()
-    total = added([lows_here.at[d] for d in range(parts)]).astype(BF)
-    middle = 2 * groups * rank
     for s in range(2 * groups):
         if s % 2 == 0:
             copies[parts + s // 2].wait()
         block = here[s // 2, (s % 2) * rows : (s % 2 + 1) * rows, :]
-        low_in = total[s * rank : (s + 1) * rank]
-        low_back = total[middle + s * rank : middle + (s + 1) * rank]
+        low_in = lows_here[core, s * rank : (s + 1) * rank, :]
+        low_back = lows_here[1 - core, s * rank : (s + 1) * rank, :]
         name = names[s]
         place = lax.rem(name // span - row + size, size) * owned + lax.rem(name, owned)
         sums[place, :, :width] += dot(low_back, block[:, :width], ((1,), (0,)))
@@ -461,13 +466,22 @@
     return total.astype(x.dtype)
 
 
-def tensor_parts(x):
+def other_core(x):
     size = lax.axis_size("tensor")
-    x = add(x, lax.ppermute(x, "tensor", [(i, i ^ 1) for i in range(size)]))
-    return [x] + [
+    return lax.ppermute(x, "tensor", [(i, i ^ 1) for i in range(size)])
+
+
+def chips(x):
+    size = lax.axis_size("tensor")
+    return [
         lax.ppermute(x, "tensor", [(i, (i + 2 * d) % size) for i in range(size)])
         for d in range(1, size // 2)
     ]
+
+
+def tensor_parts(x):
+    x = add(x, other_core(x))
+    return [x, *chips(x)]
 
 
 def local(
@@ -502,18 +516,23 @@
     rows = learn_x.shape[0] // blocks
     packed = begin(block_tenant, block_count, learn_x, learn_dy, groups)
     packed, state = barrier((packed, (adapter_a, adapter_b)))
-    arrived = [packed[0]] + [shift(packed[d], "group", d) for d in range(1, groups)]
+    order = sorted(range(1, groups), key=lambda d: min(d, groups - d))
+    moved = {d: shift(packed[d], "group", d) for d in order}
+    arrived = [packed[0]] + [moved[d] for d in range(1, groups)]
     own = jnp.concatenate([flat(x).astype(BF) for x in state], axis=1)
     tables, firsts = ring(own, rows_dp, owned)
     requests = decode_inputs[0]
     steps = requests.shape[1]
     tensor = lax.axis_index("tensor").reshape(1)
     tables, requests = barrier((tables, requests))
-    early = frozen(tensor, requests, dec_weight, 0, 2, width)
+    early = frozen(tensor, requests, dec_weight, 0, 2, width, LARGE)
     arrived, tables, early = barrier((arrived, tables, early))
 
-    partial, names = low(tables, firsts, arrived, rank, rows, rows_dp, owned)
-    sums = grad(names, tensor_parts(partial), arrived, rank, rows, rows_dp, owned)
+    mine, his, names = low(tables, firsts, arrived, rank, rows, rows_dp, owned)
+    mine = add(mine, other_core(his))
+    mine = add(mine, *chips(mine))
+    lows = [mine, other_core(mine)]
+    sums = grad(names, lows, arrived, rank, rows, rows_dp, owned)
     pieces = [sums[0], *two_stage_reduce(sums, rows_dp)]
     *new, fresh = adam(
         pieces,
@@ -555,7 +574,7 @@
     )
     in_row = spread(fresh, "group")
     fresh, wanted, slots, requests = barrier((fresh, wanted, slots, requests))
-    late = frozen(tensor, requests, dec_weight, 1, 2, width)
+    late = frozen(tensor, requests, dec_weight, 1, 2, width, MIDDLE)
     in_row, wanted, slots, late = barrier((in_row, wanted, slots, late))
     served_fresh, firsts = two_stage(pick(wanted, in_row, rank), rows_dp, owned)
 

time: 138 us -> 136 us (0.986)
  starting transfers between devices: 54.9 us -> 57.8 us
  waiting for transfers between devices: 48.1 us -> 46.4 us
    ppermute x28, starting transfers between devices: 44 us -> 47.3 us  [shift(): lax.ppermute(x, axis, [(i, (i + distance) % size) for i in range(size)])]
    ppermute x28, waiting for transfers between devices: 37.9 us -> 36.6 us  [shift(): lax.ppermute(x, axis, [(i, (i + distance) % size) for i in range(size)])]
    unnamed x56 -> x48, local copies, waits for them, and re-layouts: 3.53 us -> 2.56 us
    ppermute x8 -> x9, starting transfers between devices: 10.9 us -> 10.5 us  [the longest x6 10 us: chips(): lax.ppermute(x, 'tensor', [(i, (i + 2 * d) % size) for i in range(size)])]
    ppermute x8 -> x9, waiting for transfers between devices: 10.2 us -> 9.86 us  [the longest x6 6.31 us: chips(): lax.ppermute(x, 'tensor', [(i, (i + 2 * d) % size) for i in range(size)])]
    convert_element_type x3 -> x4, other arithmetic: 2.88 us -> 2.84 us  [add(): return total.astype(x.dtype)]
  transfers between devices with their start and end apart: 36 -> 37, of which waited for: 20 -> 21; matrix products, arithmetic and copies ran while one was open for 2% -> 2% of each run, Pallas kernels for 5% -> 5%
where the time goes in v1:
time: 136 us
  starting transfers between devices  57.8 us (42%)
  waiting for transfers between devices  46.4 us (34%)
  Pallas kernels  24.1 us (18%)
  other arithmetic  3.33 us (2%)
  local copies, waits for them, and re-layouts  2.95 us (2%)
    ppermute x28, starting transfers between devices, shift(): lax.ppermute(x, axis, [(i, (i + distance) % size) for i in range(size)])  47.3 us
    ppermute x28, waiting for transfers between devices, shift(): lax.ppermute(x, axis, [(i, (i + distance) % size) for i in range(size)])  36.6 us
    ppermute x6, starting transfers between devices, chips(): lax.ppermute(x, 'tensor', [(i, (i + 2 * d) % size) for i in range(size)])  10 us
    ppermute x6, waiting for transfers between devices, chips(): lax.ppermute(x, 'tensor', [(i, (i + 2 * d) % size) for i in range(size)])  6.31 us
    pallas_call x2, Pallas kernels, frozen(): pl.pallas_call(frozen_kernel, grid_spec=pltpu.PrefetchScalarGridSpec(num_...  6.29 us
    pallas_call x1, Pallas kernels, begin(): pl.pallas_call(functools.partial(begin_kernel, rows, groups), in_specs=sm...  4.08 us
    pallas_call x1, Pallas kernels, grad(): pl.pallas_call(functools.partial(grad_kernel, rank, rows, len(lows), owne...  3.98 us
    pallas_call x1, Pallas kernels, low(): pl.pallas_call(functools.partial(low_kernel, rank, rows, size, owned, fir...  3.81 us
  transfers between devices with their start and end apart: 37, of which 21 were waited for; matrix products, arithmetic and copies ran while one was open for 2% of the time, Pallas kernels for 5%

profile of v1, /device:TPU:14, one launch (start us, length us, event | category | flops | bytes accessed | tf_op | source)
XLA Modules:
  0.0 135.6 jit_solution(10747338036520394740)
XLA Ops:
  0.7 4.1 %shard_map.189 = (bf16[272,1152]{1,0:T(8,128)(2,1)}, bf16[272,1152]{1,0:T(8,128)(2,1)}, bf16[272,1152]{1,0:T(8,128)(2,1)}, bf16[272,1152]{1,0:T(8,128)(2,1)}) custom-call(s32[8]{0:T(128)} %tenant.1, s32[8]{0:T(128)} %count.1, bf16[1024,1024]{1,0:T(8,128)(2,1)} %x.1, bf16[1024,128]{1,0:T(8,128)(2,1)} %dy.1), custom_call_target="tpu_custom_call" | custom-call | tf_op jit(solution)/shard_map/pallas_call | solution.py:149
  5.3 2.4 %collective-permute-start.1 = (bf16[272,1152]{1,0:T(8,128)(2,1)}, bf16[272,1152]{1,0:T(8,128)(2,1)S(1)}, u32[]{:S(2)}, u32[]{:S(2)}) collective-permute-start(bf16[272,1152]{1,0:T(8,128)(2,1)} %get-tuple-element.84), channel_id=1, source_target_pairs={{0,16},{8,24},{16,0},{24,8},{1,17},{9,25},{17,1},{25,9},{2,18},{10... | collective-permute-start | bytes 1880072 | tf_op jit(solution)/shard_map/ppermute | solution.py:29
  7.8 2.0 %collective-permute-start.3 = (bf16[64,1152]{1,0:T(8,128)(2,1)S(1)}, bf16[64,1152]{1,0:T(8,128)(2,1)S(1)}, u32[]{:S(2)}, u32[]{:S(2)}) collective-permute-start(bf16[64,1152]{1,0:T(8,128)(2,1)S(1)} %pad_maximum_fusion.refs_0_), channel_id=1, source_target_pairs={{0,32},{32,64},{64,96},{96,128},{128,160},{160,192},{192,224},{224... | collective-permute-start | bytes 442376 | tf_op jit(solution)/shard_map/ppermute | solution.py:29
  9.8 4.0 %collective-permute-start.4 = (bf16[64,1152]{1,0:T(8,128)(2,1)S(1)}, bf16[64,1152]{1,0:T(8,128)(2,1)S(1)}, u32[]{:S(2)}, u32[]{:S(2)}) collective-permute-start(bf16[64,1152]{1,0:T(8,128)(2,1)S(1)} %pad_maximum_fusion.refs_0_), channel_id=1, source_target_pairs={{0,224},{32,0},{64,32},{96,64},{128,96},{160,128},{192,160},{224,1... | collective-permute-start | bytes 442376 | tf_op jit(solution)/shard_map/ppermute | solution.py:29
  13.8 3.2 %collective-permute-done.3.refs_1_ = bf16[64,1152]{1,0:T(8,128)(2,1)S(1)} collective-permute-done((bf16[64,1152]{1,0:T(8,128)(2,1)S(1)}, bf16[64,1152]{1,0:T(8,128)(2,1)S(1)}, u32[]{:S(2)}, u32[]{:S(2)}) %collective-permute-start.3) | collective-permute-done | bytes 147488 | tf_op jit(solution)/shard_map/ppermute | solution.py:29
  17.0 3.2 %collective-permute-start.6 = (bf16[64,1152]{1,0:T(8,128)(2,1)S(1)}, bf16[64,1152]{1,0:T(8,128)(2,1)S(1)}, u32[]{:S(2)}, u32[]{:S(2)}) collective-permute-start(bf16[64,1152]{1,0:T(8,128)(2,1)S(1)} %collective-permute-done.4.refs_2_), channel_id=1, source_target_pairs={{0,224},{32,0},{64,32},{96,64},{128,96},{160,128},{192,160},{224,1... | collective-permute-start | bytes 442376 | tf_op jit(solution)/shard_map/ppermute | solution.py:29
  20.3 3.1 %collective-permute-done.5.refs_3_ = bf16[64,1152]{1,0:T(8,128)(2,1)S(1)} collective-permute-done((bf16[64,1152]{1,0:T(8,128)(2,1)S(1)}, bf16[64,1152]{1,0:T(8,128)(2,1)S(1)}, u32[]{:S(2)}, u32[]{:S(2)}) %collective-permute-start.5) | collective-permute-done | bytes 147488 | tf_op jit(solution)/shard_map/ppermute | solution.py:29
  23.4 3.2 %collective-permute-start.8 = (bf16[64,1152]{1,0:T(8,128)(2,1)S(1)}, bf16[64,1152]{1,0:T(8,128)(2,1)S(1)}, u32[]{:S(2)}, u32[]{:S(2)}) collective-permute-start(bf16[64,1152]{1,0:T(8,128)(2,1)S(1)} %collective-permute-done.6.refs_4_), channel_id=1, source_target_pairs={{0,224},{32,0},{64,32},{96,64},{128,96},{160,128},{192,160},{224,1... | collective-permute-start | bytes 442376 | tf_op jit(solution)/shard_map/ppermute | solution.py:29
  26.6 3.1 %collective-permute-done.7.refs_5_ = bf16[64,1152]{1,0:T(8,128)(2,1)S(1)} collective-permute-done((bf16[64,1152]{1,0:T(8,128)(2,1)S(1)}, bf16[64,1152]{1,0:T(8,128)(2,1)S(1)}, u32[]{:S(2)}, u32[]{:S(2)}) %collective-permute-start.7) | collective-permute-done | bytes 147488 | tf_op jit(solution)/shard_map/ppermute | solution.py:29
  29.8 6.3 %collective-permute-done.9.refs_7_ = bf16[64,1152]{1,0:T(8,128)(2,1)S(1)} collective-permute-done((bf16[64,1152]{1,0:T(8,128)(2,1)S(1)}, bf16[64,1152]{1,0:T(8,128)(2,1)S(1)}, u32[]{:S(2)}, u32[]{:S(2)}) %collective-permute-start.9) | collective-permute-done | bytes 147488 | tf_op jit(solution)/shard_map/ppermute | solution.py:29
  36.1 3.5 %shard_map.190 = (f32[128,128]{1,0:T(8,128)}, bf16[128,1024]{1,0:T(8,128)(2,1)}) custom-call(s32[1]{0:T(128)} %bitcast.3.tensor, bf16[128,2,8192]{2,1,0:T(2,128)(2,1)} %bitcast.22, bf16[8192,128]{1,0:T(8,128)(2,1)} %weight.3), custom_call_target="tpu_custom_call" | custom-call | tf_op jit(solution)/shard_map/pallas_call | solution.py:190
  40.9 3.8 %shard_map.191 = (bf16[256,128]{1,0:T(8,128)(2,1)}, bf16[256,128]{1,0:T(8,128)(2,1)}, s32[8]{0:T(128)}) custom-call(bf16[64,1152]{1,0:T(8,128)(2,1)} %copy-done.7, bf16[64,1152]{1,0:T(8,128)(2,1)} %copy-done.10, bf16[64,1152]{1,0:T(8,128)(2,1)} %copy-done.12, bf16[64,1152]{1,0:T(8,128)(2,1)} %copy-done.13, bf16[64,1152]{1,0:T(8,128)(2,1)} %copy-done.14, ...), custom_call_target="tpu_custom_call" | custom-call | tf_op jit(solution)/shard_map/pallas_call | solution.py:246
  47.7 2.6 %collective-permute-start.12 = (bf16[256,128]{1,0:T(8,128)(2,1)S(1)}, bf16[256,128]{1,0:T(8,128)(2,1)S(1)}, u32[]{:S(2)}, u32[]{:S(2)}) collective-permute-start(bf16[256,128]{1,0:T(8,128)(2,1)S(1)} %add_convert_fusion.5), channel_id=1, source_target_pairs={{0,4},{1,5},{2,6},{3,7},{4,0},{5,1},{6,2},{7,3},{8,12},{9,13},{10,... | collective-permute-start | bytes 196616 | tf_op jit(solution)/shard_map/ppermute | solution.py:477
  50.3 1.9 %collective-permute-start.11 = (bf16[256,128]{1,0:T(8,128)(2,1)S(1)}, bf16[256,128]{1,0:T(8,128)(2,1)S(1)}, u32[]{:S(2)}, u32[]{:S(2)}) collective-permute-start(bf16[256,128]{1,0:T(8,128)(2,1)S(1)} %add_convert_fusion.5), channel_id=1, source_target_pairs={{0,2},{1,3},{2,4},{3,5},{4,6},{5,7},{6,0},{7,1},{8,10},{9,11},{10,... | collective-permute-start | bytes 196616 | tf_op jit(solution)/shard_map/ppermute | solution.py:477
  56.8 4.0 %shard_map.192 = (bf16[64,1152]{1,0:T(8,128)(2,1)}, bf16[64,1152]{1,0:T(8,128)(2,1)}, bf16[64,1152]{1,0:T(8,128)(2,1)}, bf16[64,1152]{1,0:T(8,128)(2,1)}, bf16[3...) custom-call(s32[8]{0:T(128)} %get-tuple-element.111.names, ...), custom_call_target="tpu_custom_call" | custom-call | tf_op jit(solution)/shard_map/pallas_call | solution.py:318
  60.9 3.2 %collective-permute-start.16 = (bf16[64,1152]{1,0:T(8,128)(2,1)}, bf16[64,1152]{1,0:T(8,128)(2,1)S(1)}, u32[]{:S(2)}, u32[]{:S(2)}) collective-permute-start(bf16[64,1152]{1,0:T(8,128)(2,1)} %get-tuple-element.116), channel_id=1, source_target_pairs={{0,224},{32,0},{64,32},{96,64},{128,96},{160,128},{192,160},{224,1... | collective-permute-start | bytes 442376 | tf_op jit(solution)/shard_map/ppermute | solution.py:29
  64.2 4.2 %collective-permute-start.21 = (bf16[32,1152]{1,0:T(8,128)(2,1)}, bf16[32,1152]{1,0:T(8,128)(2,1)S(1)}, u32[]{:S(2)}, u32[]{:S(2)}) collective-permute-start(bf16[32,1152]{1,0:T(8,128)(2,1)} %get-tuple-element.126), channel_id=1, source_target_pairs={{0,192},{32,224},{64,0},{96,32},{128,64},{160,96},{192,128},{224,1... | collective-permute-start | bytes 221192 | tf_op jit(solution)/shard_map/ppermute | solution.py:29
  69.3 3.6 %collective-permute-start.18 = (bf16[64,1152]{1,0:T(8,128)(2,1)}, bf16[64,1152]{1,0:T(8,128)(2,1)S(1)}, u32[]{:S(2)}, u32[]{:S(2)}) collective-permute-start(bf16[64,1152]{1,0:T(8,128)(2,1)} %get-tuple-element.120), channel_id=1, source_target_pairs={{0,224},{32,0},{64,32},{96,64},{128,96},{160,128},{192,160},{224,1... | collective-permute-start | bytes 442376 | tf_op jit(solution)/shard_map/ppermute | solution.py:29
  76.7 2.5 %collective-permute-start.22 = (bf16[64,1152]{1,0:T(8,128)(2,1)S(1)}, bf16[64,1152]{1,0:T(8,128)(2,1)S(1)}, u32[]{:S(2)}, u32[]{:S(2)}) collective-permute-start(bf16[64,1152]{1,0:T(8,128)(2,1)S(1)} %pad_maximum_fusion.2), channel_id=1, source_target_pairs={{0,192},{32,224},{64,0},{96,32},{128,64},{160,96},{192,128},{224,1... | collective-permute-start | bytes 442376 | tf_op jit(solution)/shard_map/ppermute | solution.py:29
  79.3 4.2 %collective-permute-done.20.refs_3_ = bf16[64,1152]{1,0:T(8,128)(2,1)S(1)} collective-permute-done((bf16[64,1152]{1,0:T(8,128)(2,1)S(1)}, bf16[64,1152]{1,0:T(8,128)(2,1)S(1)}, u32[]{:S(2)}, u32[]{:S(2)}) %collective-permute-start.20) | collective-permute-done | bytes 147488 | tf_op jit(solution)/shard_map/ppermute | solution.py:29
  84.5 2.8 %shard_map.193 = (f32[64,1024]{1,0:T(8,128)}, f32[64,1024]{1,0:T(8,128)}, f32[64,1024]{1,0:T(8,128)}, f32[64,128]{1,0:T(8,128)}, f32[64,128]{1,0:T(8,128)}, /*index=5*/f32[64,128]{1,0:T(8,128)}, bf16[64,1152]{1,0:T(8,128)(2,1)}) custom-call(bf16[64,1152]{1,0:T(8,128)(2,1)} %get-tuple-element.114.refs_0_, bf16[64,1152]{1,0:T(8,128)(2,1)} %copy-done.9, ...), custom_call_target="tpu_custom_call" | custom-call | tf_op jit(solution)/shard_map/pallas_call | solution.py:370
  87.2 3.2 %collective-permute-start.23 = (bf16[64,1152]{1,0:T(8,128)(2,1)}, bf16[64,1152]{1,0:T(8,128)(2,1)S(1)}, u32[]{:S(2)}, u32[]{:S(2)}) collective-permute-start(bf16[64,1152]{1,0:T(8,128)(2,1)} %get-tuple-element.145.refs_0_), channel_id=1, source_target_pairs={{0,8},{8,16},{16,24},{24,0},{1,9},{9,17},{17,25},{25,1},{2,10},{10... | collective-permute-start | bytes 442376 | tf_op jit(solution)/shard_map/ppermute | solution.py:29
  92.1 2.8 %shard_map.194 = (f32[128,128]{1,0:T(8,128)S(1)}, bf16[128,1024]{1,0:T(8,128)(2,1)S(1)}) custom-call(s32[1]{0:T(128)} %bitcast.3.tensor, bf16[128,2,8192]{2,1,0:T(2,128)(2,1)} %bitcast.23, bf16[8192,128]{1,0:T(8,128)(2,1)} %weight.3), custom_call_target="tpu_custom_call" | custom-call | tf_op jit(solution)/shard_map/pallas_call | solution.py:190
  96.6 2.1 %collective-permute-done.24.refs_2_ = bf16[64,1152]{1,0:T(8,128)(2,1)S(1)} collective-permute-done((bf16[64,1152]{1,0:T(8,128)(2,1)}, bf16[64,1152]{1,0:T(8,128)(2,1)S(1)}, u32[]{:S(2)}, u32[]{:S(2)}) %collective-permute-start.24) | collective-permute-done | bytes 147488 | tf_op jit(solution)/shard_map/ppermute | solution.py:29
  100.5 4.1 %collective-permute-start.28 = (bf16[64,1152]{1,0:T(8,128)(2,1)S(1)}, bf16[64,1152]{1,0:T(8,128)(2,1)S(1)}, u32[]{:S(2)}, u32[]{:S(2)}) collective-permute-start(bf16[64,1152]{1,0:T(8,128)(2,1)S(1)} %shard_map.195.refs_2_.refs_6_), channel_id=1, source_target_pairs={{0,64},{32,96},{64,128},{96,160},{128,192},{160,224},{192,0},{224,... | collective-permute-start | bytes 442376 | tf_op jit(solution)/shard_map/ppermute | solution.py:29
  108.0 3.1 %collective-permute-done.28.refs_5_.refs_9_ = bf16[64,1152]{1,0:T(8,128)(2,1)S(1)} collective-permute-done((bf16[64,1152]{1,0:T(8,128)(2,1)S(1)}, bf16[64,1152]{1,0:T(8,128)(2,1)S(1)}, u32[]{:S(2)}, u32[]{:S(2)}) %collective-permute-start.28) | collective-permute-done | bytes 147488 | tf_op jit(solution)/shard_map/ppermute | solution.py:29
  113.0 1.9 %collective-permute-start.31 = (bf16[64,1152]{1,0:T(8,128)(2,1)S(1)}, bf16[64,1152]{1,0:T(8,128)(2,1)S(1)}, u32[]{:S(2)}, u32[]{:S(2)}) collective-permute-start(bf16[64,1152]{1,0:T(8,128)(2,1)S(1)} %collective-permute-done.29.refs_6_.refs_10_), channel_id=1, source_target_pairs={{0,224},{32,0},{64,32},{96,64},{128,96},{160,128},{192,160},{224,1... | collective-permute-start | bytes 442376 | tf_op jit(solution)/shard_map/ppermute | solution.py:29
  114.9 1.9 %collective-permute-start.32 = (bf16[64,1152]{1,0:T(8,128)(2,1)S(1)}, bf16[64,1152]{1,0:T(8,128)(2,1)S(1)}, u32[]{:S(2)}, u32[]{:S(2)}) collective-permute-start(bf16[64,1152]{1,0:T(8,128)(2,1)S(1)} %collective-permute-done.28.refs_5_.refs_9_), channel_id=1, source_target_pairs={{0,64},{32,96},{64,128},{96,160},{128,192},{160,224},{192,0},{224,... | collective-permute-start | bytes 442376 | tf_op jit(solution)/shard_map/ppermute | solution.py:29
  116.8 2.0 %collective-permute-done.30.refs_7_.refs_11_ = bf16[64,1152]{1,0:T(8,128)(2,1)S(1)} collective-permute-done((bf16[64,1152]{1,0:T(8,128)(2,1)S(1)}, bf16[64,1152]{1,0:T(8,128)(2,1)S(1)}, u32[]{:S(2)}, u32[]{:S(2)}) %collective-permute-start.30) | collective-permute-done | bytes 147488 | tf_op jit(solution)/shard_map/ppermute | solution.py:29
  118.8 4.1 %collective-permute-done.32.refs_9_.refs_13_ = bf16[64,1152]{1,0:T(8,128)(2,1)S(1)} collective-permute-done((bf16[64,1152]{1,0:T(8,128)(2,1)S(1)}, bf16[64,1152]{1,0:T(8,128)(2,1)S(1)}, u32[]{:S(2)}, u32[]{:S(2)}) %collective-permute-start.32) | collective-permute-done | bytes 147488 | tf_op jit(solution)/shard_map/ppermute | solution.py:29
  127.5 3.2 %collective-permute-start.35 = (f32[32,256]{1,0:T(8,128)S(1)}, f32[32,256]{1,0:T(8,128)S(1)}, u32[]{:S(2)}, u32[]{:S(2)}) collective-permute-start(f32[32,256]{1,0:T(8,128)S(1)} %add.93.refs_2_), channel_id=1, source_target_pairs={{0,4},{1,5},{2,6},{3,7},{4,0},{5,1},{6,2},{7,3},{8,12},{9,13},{10,... | collective-permute-start | bytes 98312 | tf_op jit(solution)/shard_map/ppermute | solution.py:477
  130.7 2.2 %collective-permute-done.35.refs_4_ = f32[32,256]{1,0:T(8,128)S(1)} collective-permute-done((f32[32,256]{1,0:T(8,128)S(1)}, f32[32,256]{1,0:T(8,128)S(1)}, u32[]{:S(2)}, u32[]{:S(2)}) %collective-permute-start.35) | collective-permute-done | bytes 32800 | tf_op jit(solution)/shard_map/ppermute | solution.py:477
  (122 shorter events, 33.0 us)
Async XLA Ops:
  4.7 34.9 %collective-permute-start = (bf16[272,1152]{1,0:T(8,128)(2,1)}, bf16[272,1152]{1,0:T(8,128)(2,1)S(1)}, u32[]{:S(2)}, u32[]{:S(2)}) collective-permute-start(bf16[272,1152]{1,0:T(8,128)(2,1)} %get-tuple-element.83), channel_id=1, source_target_pairs={{0,8},{8,16},{16,24},{24,0},{1,9},{9,17},{17,25},{25,1},{2,10},{10... | collective-permute-start | bytes 1880072 | tf_op jit(solution)/shard_map/ppermute | solution.py:29
  5.3 34.4 %collective-permute-start.1 = (bf16[272,1152]{1,0:T(8,128)(2,1)}, bf16[272,1152]{1,0:T(8,128)(2,1)S(1)}, u32[]{:S(2)}, u32[]{:S(2)}) collective-permute-start(bf16[272,1152]{1,0:T(8,128)(2,1)} %get-tuple-element.84), channel_id=1, source_target_pairs={{0,16},{8,24},{16,0},{24,8},{1,17},{9,25},{17,1},{25,9},{2,18},{10... | collective-permute-start | bytes 1880072 | tf_op jit(solution)/shard_map/ppermute | solution.py:29
  7.7 32.0 %collective-permute-start.2 = (bf16[272,1152]{1,0:T(8,128)(2,1)}, bf16[272,1152]{1,0:T(8,128)(2,1)S(1)}, u32[]{:S(2)}, u32[]{:S(2)}) collective-permute-start(bf16[272,1152]{1,0:T(8,128)(2,1)} %get-tuple-element.85), channel_id=1, source_target_pairs={{0,24},{8,0},{16,8},{24,16},{1,25},{9,1},{17,9},{25,17},{2,26},{10... | collective-permute-start | bytes 1880072 | tf_op jit(solution)/shard_map/ppermute | solution.py:29
  7.8 9.2 %collective-permute-start.3 = (bf16[64,1152]{1,0:T(8,128)(2,1)S(1)}, bf16[64,1152]{1,0:T(8,128)(2,1)S(1)}, u32[]{:S(2)}, u32[]{:S(2)}) collective-permute-start(bf16[64,1152]{1,0:T(8,128)(2,1)S(1)} %pad_maximum_fusion.refs_0_), channel_id=1, source_target_pairs={{0,32},{32,64},{64,96},{96,128},{128,160},{160,192},{192,224},{224... | collective-permute-start | bytes 442376 | tf_op jit(solution)/shard_map/ppermute | solution.py:29
  9.8 7.2 %collective-permute-start.4 = (bf16[64,1152]{1,0:T(8,128)(2,1)S(1)}, bf16[64,1152]{1,0:T(8,128)(2,1)S(1)}, u32[]{:S(2)}, u32[]{:S(2)}) collective-permute-start(bf16[64,1152]{1,0:T(8,128)(2,1)S(1)} %pad_maximum_fusion.refs_0_), channel_id=1, source_target_pairs={{0,224},{32,0},{64,32},{96,64},{128,96},{160,128},{192,160},{224,1... | collective-permute-start | bytes 442376 | tf_op jit(solution)/shard_map/ppermute | solution.py:29
  17.0 6.4 %collective-permute-start.5 = (bf16[64,1152]{1,0:T(8,128)(2,1)S(1)}, bf16[64,1152]{1,0:T(8,128)(2,1)S(1)}, u32[]{:S(2)}, u32[]{:S(2)}) collective-permute-start(bf16[64,1152]{1,0:T(8,128)(2,1)S(1)} %collective-permute-done.3.refs_1_), channel_id=1, source_target_pairs={{0,32},{32,64},{64,96},{96,128},{128,160},{160,192},{192,224},{224... | collective-permute-start | bytes 442376 | tf_op jit(solution)/shard_map/ppermute | solution.py:29
  17.0 6.3 %collective-permute-start.6 = (bf16[64,1152]{1,0:T(8,128)(2,1)S(1)}, bf16[64,1152]{1,0:T(8,128)(2,1)S(1)}, u32[]{:S(2)}, u32[]{:S(2)}) collective-permute-start(bf16[64,1152]{1,0:T(8,128)(2,1)S(1)} %collective-permute-done.4.refs_2_), channel_id=1, source_target_pairs={{0,224},{32,0},{64,32},{96,64},{128,96},{160,128},{192,160},{224,1... | collective-permute-start | bytes 442376 | tf_op jit(solution)/shard_map/ppermute | solution.py:29
  23.4 6.4 %collective-permute-start.7 = (bf16[64,1152]{1,0:T(8,128)(2,1)S(1)}, bf16[64,1152]{1,0:T(8,128)(2,1)S(1)}, u32[]{:S(2)}, u32[]{:S(2)}) collective-permute-start(bf16[64,1152]{1,0:T(8,128)(2,1)S(1)} %collective-permute-done.5.refs_3_), channel_id=1, source_target_pairs={{0,32},{32,64},{64,96},{96,128},{128,160},{160,192},{192,224},{224... | collective-permute-start | bytes 442376 | tf_op jit(solution)/shard_map/ppermute | solution.py:29
  23.4 6.3 %collective-permute-start.8 = (bf16[64,1152]{1,0:T(8,128)(2,1)S(1)}, bf16[64,1152]{1,0:T(8,128)(2,1)S(1)}, u32[]{:S(2)}, u32[]{:S(2)}) collective-permute-start(bf16[64,1152]{1,0:T(8,128)(2,1)S(1)} %collective-permute-done.6.refs_4_), channel_id=1, source_target_pairs={{0,224},{32,0},{64,32},{96,64},{128,96},{160,128},{192,160},{224,1... | collective-permute-start | bytes 442376 | tf_op jit(solution)/shard_map/ppermute | solution.py:29
  29.7 6.4 %collective-permute-start.9 = (bf16[64,1152]{1,0:T(8,128)(2,1)S(1)}, bf16[64,1152]{1,0:T(8,128)(2,1)S(1)}, u32[]{:S(2)}, u32[]{:S(2)}) collective-permute-start(bf16[64,1152]{1,0:T(8,128)(2,1)S(1)} %collective-permute-done.7.refs_5_), channel_id=1, source_target_pairs={{0,32},{32,64},{64,96},{96,128},{128,160},{160,192},{192,224},{224... | collective-permute-start | bytes 442376 | tf_op jit(solution)/shard_map/ppermute | solution.py:29
  47.1 5.0 %collective-permute-start.13 = (bf16[256,128]{1,0:T(8,128)(2,1)S(1)}, bf16[256,128]{1,0:T(8,128)(2,1)S(1)}, u32[]{:S(2)}, u32[]{:S(2)}) collective-permute-start(bf16[256,128]{1,0:T(8,128)(2,1)S(1)} %add_convert_fusion.5), channel_id=1, source_target_pairs={{0,6},{1,7},{2,0},{3,1},{4,2},{5,3},{6,4},{7,5},{8,14},{9,15},{10,... | collective-permute-start | bytes 196616 | tf_op jit(solution)/shard_map/ppermute | solution.py:477
  47.7 6.2 %collective-permute-start.12 = (bf16[256,128]{1,0:T(8,128)(2,1)S(1)}, bf16[256,128]{1,0:T(8,128)(2,1)S(1)}, u32[]{:S(2)}, u32[]{:S(2)}) collective-permute-start(bf16[256,128]{1,0:T(8,128)(2,1)S(1)} %add_convert_fusion.5), channel_id=1, source_target_pairs={{0,4},{1,5},{2,6},{3,7},{4,0},{5,1},{6,2},{7,3},{8,12},{9,13},{10,... | collective-permute-start | bytes 196616 | tf_op jit(solution)/shard_map/ppermute | solution.py:477
  60.8 8.5 %collective-permute-start.15 = (bf16[64,1152]{1,0:T(8,128)(2,1)}, bf16[64,1152]{1,0:T(8,128)(2,1)S(1)}, u32[]{:S(2)}, u32[]{:S(2)}) collective-permute-start(bf16[64,1152]{1,0:T(8,128)(2,1)} %get-tuple-element.115), channel_id=1, source_target_pairs={{0,32},{32,64},{64,96},{96,128},{128,160},{160,192},{192,224},{224... | collective-permute-start | bytes 442376 | tf_op jit(solution)/shard_map/ppermute | solution.py:29
  60.9 8.4 %collective-permute-start.16 = (bf16[64,1152]{1,0:T(8,128)(2,1)}, bf16[64,1152]{1,0:T(8,128)(2,1)S(1)}, u32[]{:S(2)}, u32[]{:S(2)}) collective-permute-start(bf16[64,1152]{1,0:T(8,128)(2,1)} %get-tuple-element.116), channel_id=1, source_target_pairs={{0,224},{32,0},{64,32},{96,64},{128,96},{160,128},{192,160},{224,1... | collective-permute-start | bytes 442376 | tf_op jit(solution)/shard_map/ppermute | solution.py:29
  64.1 8.8 %collective-permute-start.19 = (bf16[32,1152]{1,0:T(8,128)(2,1)}, bf16[32,1152]{1,0:T(8,128)(2,1)S(1)}, u32[]{:S(2)}, u32[]{:S(2)}) collective-permute-start(bf16[32,1152]{1,0:T(8,128)(2,1)} %get-tuple-element.123), channel_id=1, source_target_pairs={{0,64},{32,96},{64,128},{96,160},{128,192},{160,224},{192,0},{224,... | collective-permute-start | bytes 221192 | tf_op jit(solution)/shard_map/ppermute | solution.py:29
  64.2 11.5 %collective-permute-start.21 = (bf16[32,1152]{1,0:T(8,128)(2,1)}, bf16[32,1152]{1,0:T(8,128)(2,1)S(1)}, u32[]{:S(2)}, u32[]{:S(2)}) collective-permute-start(bf16[32,1152]{1,0:T(8,128)(2,1)} %get-tuple-element.126), channel_id=1, source_target_pairs={{0,192},{32,224},{64,0},{96,32},{128,64},{160,96},{192,128},{224,1... | collective-permute-start | bytes 221192 | tf_op jit(solution)/shard_map/ppermute | solution.py:29
  69.3 10.0 %collective-permute-start.17 = (bf16[64,1152]{1,0:T(8,128)(2,1)}, bf16[64,1152]{1,0:T(8,128)(2,1)S(1)}, u32[]{:S(2)}, u32[]{:S(2)}) collective-permute-start(bf16[64,1152]{1,0:T(8,128)(2,1)} %get-tuple-element.119), channel_id=1, source_target_pairs={{0,32},{32,64},{64,96},{96,128},{128,160},{160,192},{192,224},{224... | collective-permute-start | bytes 442376 | tf_op jit(solution)/shard_map/ppermute | solution.py:29
  69.3 10.1 %collective-permute-start.18 = (bf16[64,1152]{1,0:T(8,128)(2,1)}, bf16[64,1152]{1,0:T(8,128)(2,1)S(1)}, u32[]{:S(2)}, u32[]{:S(2)}) collective-permute-start(bf16[64,1152]{1,0:T(8,128)(2,1)} %get-tuple-element.120), channel_id=1, source_target_pairs={{0,224},{32,0},{64,32},{96,64},{128,96},{160,128},{192,160},{224,1... | collective-permute-start | bytes 442376 | tf_op jit(solution)/shard_map/ppermute | solution.py:29
  73.9 9.6 %collective-permute-start.20 = (bf16[64,1152]{1,0:T(8,128)(2,1)S(1)}, bf16[64,1152]{1,0:T(8,128)(2,1)S(1)}, u32[]{:S(2)}, u32[]{:S(2)}) collective-permute-start(bf16[64,1152]{1,0:T(8,128)(2,1)S(1)} %pad_maximum_fusion.1), channel_id=1, source_target_pairs={{0,64},{32,96},{64,128},{96,160},{128,192},{160,224},{192,0},{224,... | collective-permute-start | bytes 442376 | tf_op jit(solution)/shard_map/ppermute | solution.py:29
  76.7 7.1 %collective-permute-start.22 = (bf16[64,1152]{1,0:T(8,128)(2,1)S(1)}, bf16[64,1152]{1,0:T(8,128)(2,1)S(1)}, u32[]{:S(2)}, u32[]{:S(2)}) collective-permute-start(bf16[64,1152]{1,0:T(8,128)(2,1)S(1)} %pad_maximum_fusion.2), channel_id=1, source_target_pairs={{0,192},{32,224},{64,0},{96,32},{128,64},{160,96},{192,128},{224,1... | collective-permute-start | bytes 442376 | tf_op jit(solution)/shard_map/ppermute | solution.py:29
  87.2 9.3 %collective-permute-start.23 = (bf16[64,1152]{1,0:T(8,128)(2,1)}, bf16[64,1152]{1,0:T(8,128)(2,1)S(1)}, u32[]{:S(2)}, u32[]{:S(2)}) collective-permute-start(bf16[64,1152]{1,0:T(8,128)(2,1)} %get-tuple-element.145.refs_0_), channel_id=1, source_target_pairs={{0,8},{8,16},{16,24},{24,0},{1,9},{9,17},{17,25},{25,1},{2,10},{10... | collective-permute-start | bytes 442376 | tf_op jit(solution)/shard_map/ppermute | solution.py:29
  90.4 8.2 %collective-permute-start.24 = (bf16[64,1152]{1,0:T(8,128)(2,1)}, bf16[64,1152]{1,0:T(8,128)(2,1)S(1)}, u32[]{:S(2)}, u32[]{:S(2)}) collective-permute-start(bf16[64,1152]{1,0:T(8,128)(2,1)} %get-tuple-element.145.refs_0_), channel_id=1, source_target_pairs={{0,16},{8,24},{16,0},{24,8},{1,17},{9,25},{17,1},{25,9},{2,18},{10... | collective-permute-start | bytes 442376 | tf_op jit(solution)/shard_map/ppermute | solution.py:29
  90.5 9.4 %collective-permute-start.25 = (bf16[64,1152]{1,0:T(8,128)(2,1)}, bf16[64,1152]{1,0:T(8,128)(2,1)S(1)}, u32[]{:S(2)}, u32[]{:S(2)}) collective-permute-start(bf16[64,1152]{1,0:T(8,128)(2,1)} %get-tuple-element.145.refs_0_), channel_id=1, source_target_pairs={{0,24},{8,0},{16,8},{24,16},{1,25},{9,1},{17,9},{25,17},{2,26},{10... | collective-permute-start | bytes 442376 | tf_op jit(solution)/shard_map/ppermute | solution.py:29
  100.5 10.5 %collective-permute-start.28 = (bf16[64,1152]{1,0:T(8,128)(2,1)S(1)}, bf16[64,1152]{1,0:T(8,128)(2,1)S(1)}, u32[]{:S(2)}, u32[]{:S(2)}) collective-permute-start(bf16[64,1152]{1,0:T(8,128)(2,1)S(1)} %shard_map.195.refs_2_.refs_6_), channel_id=1, source_target_pairs={{0,64},{32,96},{64,128},{96,160},{128,192},{160,224},{192,0},{224,... | collective-permute-start | bytes 442376 | tf_op jit(solution)/shard_map/ppermute | solution.py:29
  104.6 8.3 %collective-permute-start.29 = (bf16[64,1152]{1,0:T(8,128)(2,1)S(1)}, bf16[64,1152]{1,0:T(8,128)(2,1)S(1)}, u32[]{:S(2)}, u32[]{:S(2)}) collective-permute-start(bf16[64,1152]{1,0:T(8,128)(2,1)S(1)} %shard_map.195.refs_2_.refs_6_), channel_id=1, source_target_pairs={{0,192},{32,224},{64,0},{96,32},{128,64},{160,96},{192,128},{224,1... | collective-permute-start | bytes 442376 | tf_op jit(solution)/shard_map/ppermute | solution.py:29
  104.7 12.1 %collective-permute-start.26 = (bf16[64,1152]{1,0:T(8,128)(2,1)S(1)}, bf16[64,1152]{1,0:T(8,128)(2,1)S(1)}, u32[]{:S(2)}, u32[]{:S(2)}) collective-permute-start(bf16[64,1152]{1,0:T(8,128)(2,1)S(1)} %shard_map.195.refs_2_.refs_6_), channel_id=1, source_target_pairs={{0,32},{32,64},{64,96},{96,128},{128,160},{160,192},{192,224},{224... | collective-permute-start | bytes 442376 | tf_op jit(solution)/shard_map/ppermute | solution.py:29
  106.2 10.5 %collective-permute-start.27 = (bf16[64,1152]{1,0:T(8,128)(2,1)S(1)}, bf16[64,1152]{1,0:T(8,128)(2,1)S(1)}, u32[]{:S(2)}, u32[]{:S(2)}) collective-permute-start(bf16[64,1152]{1,0:T(8,128)(2,1)S(1)} %shard_map.195.refs_2_.refs_6_), channel_id=1, source_target_pairs={{0,224},{32,0},{64,32},{96,64},{128,96},{160,128},{192,160},{224,1... | collective-permute-start | bytes 442376 | tf_op jit(solution)/shard_map/ppermute | solution.py:29
  111.0 7.7 %collective-permute-start.30 = (bf16[64,1152]{1,0:T(8,128)(2,1)S(1)}, bf16[64,1152]{1,0:T(8,128)(2,1)S(1)}, u32[]{:S(2)}, u32[]{:S(2)}) collective-permute-start(bf16[64,1152]{1,0:T(8,128)(2,1)S(1)} %collective-permute-done.28.refs_5_.refs_9_), channel_id=1, source_target_pairs={{0,32},{32,64},{64,96},{96,128},{128,160},{160,192},{192,224},{224... | collective-permute-start | bytes 442376 | tf_op jit(solution)/shard_map/ppermute | solution.py:29
  113.0 5.8 %collective-permute-start.31 = (bf16[64,1152]{1,0:T(8,128)(2,1)S(1)}, bf16[64,1152]{1,0:T(8,128)(2,1)S(1)}, u32[]{:S(2)}, u32[]{:S(2)}) collective-permute-start(bf16[64,1152]{1,0:T(8,128)(2,1)S(1)} %collective-permute-done.29.refs_6_.refs_10_), channel_id=1, source_target_pairs={{0,224},{32,0},{64,32},{96,64},{128,96},{160,128},{192,160},{224,1... | collective-permute-start | bytes 442376 | tf_op jit(solution)/shard_map/ppermute | solution.py:29
  114.9 8.0 %collective-permute-start.32 = (bf16[64,1152]{1,0:T(8,128)(2,1)S(1)}, bf16[64,1152]{1,0:T(8,128)(2,1)S(1)}, u32[]{:S(2)}, u32[]{:S(2)}) collective-permute-start(bf16[64,1152]{1,0:T(8,128)(2,1)S(1)} %collective-permute-done.28.refs_5_.refs_9_), channel_id=1, source_target_pairs={{0,64},{32,96},{64,128},{96,160},{128,192},{160,224},{192,0},{224,... | collective-permute-start | bytes 442376 | tf_op jit(solution)/shard_map/ppermute | solution.py:29
  125.7 5.0 %collective-permute-start.34 = (f32[32,256]{1,0:T(8,128)S(1)}, f32[32,256]{1,0:T(8,128)S(1)}, u32[]{:S(2)}, u32[]{:S(2)}) collective-permute-start(f32[32,256]{1,0:T(8,128)S(1)} %add.93.refs_2_), channel_id=1, source_target_pairs={{0,2},{1,3},{2,4},{3,5},{4,6},{5,7},{6,0},{7,1},{8,10},{9,11},{10,... | collective-permute-start | bytes 98312 | tf_op jit(solution)/shard_map/ppermute | solution.py:477
  127.5 5.4 %collective-permute-start.35 = (f32[32,256]{1,0:T(8,128)S(1)}, f32[32,256]{1,0:T(8,128)S(1)}, u32[]{:S(2)}, u32[]{:S(2)}) collective-permute-start(f32[32,256]{1,0:T(8,128)S(1)} %add.93.refs_2_), channel_id=1, source_target_pairs={{0,4},{1,5},{2,6},{3,7},{4,0},{5,1},{6,2},{7,3},{8,12},{9,13},{10,... | collective-permute-start | bytes 98312 | tf_op jit(solution)/shard_map/ppermute | solution.py:477
  (29 other events, 289.7 us)

commit v2 on v1

--- a/solution.py
+++ b/solution.py
@@ -79,6 +79,7 @@
 anywhere = functools.partial(spot, pl.ANY)
 SMALL = pltpu.CompilerParams(vmem_limit_bytes=14 * MIB)
 MIDDLE = pltpu.CompilerParams(vmem_limit_bytes=52 * MIB)
+WHOLE = pltpu.CompilerParams(vmem_limit_bytes=64 * MIB)
 LARGE = pltpu.CompilerParams(vmem_limit_bytes=61 * MIB)
 
 
@@ -525,7 +526,7 @@
     steps = requests.shape[1]
     tensor = lax.axis_index("tensor").reshape(1)
     tables, requests = barrier((tables, requests))
-    early = frozen(tensor, requests, dec_weight, 0, 2, width, LARGE)
+    early = frozen(tensor, requests, dec_weight, 0, 2, width, WHOLE)
     arrived, tables, early = barrier((arrived, tables, early))
 
     mine, his, names = low(tables, firsts, arrived, rank, rows, rows_dp, owned)

time: 136 us -> 136 us (level)
  waiting for transfers between devices: 46.4 us -> 44.6 us
    ppermute x28, waiting for transfers between devices: 36.6 us -> 34.7 us  [shift(): lax.ppermute(x, axis, [(i, (i + distance) % size) for i in range(size)])]
    unnamed x48 -> x42, local copies, waits for them, and re-layouts: 2.56 us -> 3.93 us
where the time goes in v2:
time: 136 us
  starting transfers between devices  58.4 us (43%)
  waiting for transfers between devices  44.6 us (33%)
  Pallas kernels  24 us (18%)
  local copies, waits for them, and re-layouts  4.31 us (3%)
  other arithmetic  3.33 us (2%)
    ppermute x28, starting transfers between devices, shift(): lax.ppermute(x, axis, [(i, (i + distance) % size) for i in range(size)])  47.6 us
    ppermute x28, waiting for transfers between devices, shift(): lax.ppermute(x, axis, [(i, (i + distance) % size) for i in range(size)])  34.7 us
    ppermute x6, starting transfers between devices, chips(): lax.ppermute(x, 'tensor', [(i, (i + 2 * d) % size) for i in range(size)])  10.3 us
    ppermute x6, waiting for transfers between devices, chips(): lax.ppermute(x, 'tensor', [(i, (i + 2 * d) % size) for i in range(size)])  6.32 us
    pallas_call x2, Pallas kernels, frozen(): pl.pallas_call(frozen_kernel, grid_spec=pltpu.PrefetchScalarGridSpec(num_...  6.24 us
    pallas_call x1, Pallas kernels, begin(): pl.pallas_call(functools.partial(begin_kernel, rows, groups), in_specs=sm...  4.1 us
    pallas_call x1, Pallas kernels, grad(): pl.pallas_call(functools.partial(grad_kernel, rank, rows, len(lows), owne...  3.97 us
    unnamed x42, local copies, waits for them, and re-layouts  3.93 us
  transfers between devices with their start and end apart: 37, of which 21 were waited for; matrix products, arithmetic and copies ran while one was open for 2% of the time, Pallas kernels for 5%

profile of v2, /device:TPU:14, one launch (start us, length us, event | category | flops | bytes accessed | tf_op | source)
XLA Modules:
  0.0 135.6 jit_solution(13670210191072594870)
XLA Ops:
  0.7 4.1 %shard_map.189 = (bf16[272,1152]{1,0:T(8,128)(2,1)}, bf16[272,1152]{1,0:T(8,128)(2,1)}, bf16[272,1152]{1,0:T(8,128)(2,1)}, bf16[272,1152]{1,0:T(8,128)(2,1)}) custom-call(s32[8]{0:T(128)} %tenant.1, s32[8]{0:T(128)} %count.1, bf16[1024,1024]{1,0:T(8,128)(2,1)} %x.1, bf16[1024,128]{1,0:T(8,128)(2,1)} %dy.1), custom_call_target="tpu_custom_call" | custom-call | tf_op jit(solution)/shard_map/pallas_call | solution.py:150
  5.3 2.4 %collective-permute-start.1 = (bf16[272,1152]{1,0:T(8,128)(2,1)}, bf16[272,1152]{1,0:T(8,128)(2,1)}, u32[]{:S(2)}, u32[]{:S(2)}) collective-permute-start(bf16[272,1152]{1,0:T(8,128)(2,1)} %get-tuple-element.84), channel_id=1, source_target_pairs={{0,16},{8,24},{16,0},{24,8},{1,17},{9,25},{17,1},{25,9},{2,18},{10... | collective-permute-start | bytes 1880072 | tf_op jit(solution)/shard_map/ppermute | solution.py:29
  7.8 2.0 %collective-permute-start.3 = (bf16[64,1152]{1,0:T(8,128)(2,1)S(1)}, bf16[64,1152]{1,0:T(8,128)(2,1)S(1)}, u32[]{:S(2)}, u32[]{:S(2)}) collective-permute-start(bf16[64,1152]{1,0:T(8,128)(2,1)S(1)} %pad_maximum_fusion.refs_0_), channel_id=1, source_target_pairs={{0,32},{32,64},{64,96},{96,128},{128,160},{160,192},{192,224},{224... | collective-permute-start | bytes 442376 | tf_op jit(solution)/shard_map/ppermute | solution.py:29
  9.8 4.5 %collective-permute-start.4 = (bf16[64,1152]{1,0:T(8,128)(2,1)S(1)}, bf16[64,1152]{1,0:T(8,128)(2,1)S(1)}, u32[]{:S(2)}, u32[]{:S(2)}) collective-permute-start(bf16[64,1152]{1,0:T(8,128)(2,1)S(1)} %pad_maximum_fusion.refs_0_), channel_id=1, source_target_pairs={{0,224},{32,0},{64,32},{96,64},{128,96},{160,128},{192,160},{224,1... | collective-permute-start | bytes 442376 | tf_op jit(solution)/shard_map/ppermute | solution.py:29
  14.3 2.7 %collective-permute-done.3.refs_1_ = bf16[64,1152]{1,0:T(8,128)(2,1)S(1)} collective-permute-done((bf16[64,1152]{1,0:T(8,128)(2,1)S(1)}, bf16[64,1152]{1,0:T(8,128)(2,1)S(1)}, u32[]{:S(2)}, u32[]{:S(2)}) %collective-permute-start.3) | collective-permute-done | bytes 147488 | tf_op jit(solution)/shard_map/ppermute | solution.py:29
  17.7 3.0 %collective-permute-start.6 = (bf16[64,1152]{1,0:T(8,128)(2,1)S(1)}, bf16[64,1152]{1,0:T(8,128)(2,1)S(1)}, u32[]{:S(2)}, u32[]{:S(2)}) collective-permute-start(bf16[64,1152]{1,0:T(8,128)(2,1)S(1)} %collective-permute-done.4.refs_2_), channel_id=1, source_target_pairs={{0,224},{32,0},{64,32},{96,64},{128,96},{160,128},{192,160},{224,1... | collective-permute-start | bytes 442376 | tf_op jit(solution)/shard_map/ppermute | solution.py:29
  20.7 2.7 %collective-permute-done.5.refs_3_ = bf16[64,1152]{1,0:T(8,128)(2,1)S(1)} collective-permute-done((bf16[64,1152]{1,0:T(8,128)(2,1)S(1)}, bf16[64,1152]{1,0:T(8,128)(2,1)S(1)}, u32[]{:S(2)}, u32[]{:S(2)}) %collective-permute-start.5) | collective-permute-done | bytes 147488 | tf_op jit(solution)/shard_map/ppermute | solution.py:29
  24.1 3.0 %collective-permute-start.8 = (bf16[64,1152]{1,0:T(8,128)(2,1)S(1)}, bf16[64,1152]{1,0:T(8,128)(2,1)S(1)}, u32[]{:S(2)}, u32[]{:S(2)}) collective-permute-start(bf16[64,1152]{1,0:T(8,128)(2,1)S(1)} %collective-permute-done.6.refs_4_), channel_id=1, source_target_pairs={{0,224},{32,0},{64,32},{96,64},{128,96},{160,128},{192,160},{224,1... | collective-permute-start | bytes 442376 | tf_op jit(solution)/shard_map/ppermute | solution.py:29
  27.1 2.7 %collective-permute-done.7.refs_5_ = bf16[64,1152]{1,0:T(8,128)(2,1)S(1)} collective-permute-done((bf16[64,1152]{1,0:T(8,128)(2,1)S(1)}, bf16[64,1152]{1,0:T(8,128)(2,1)S(1)}, u32[]{:S(2)}, u32[]{:S(2)}) %collective-permute-start.7) | collective-permute-done | bytes 147488 | tf_op jit(solution)/shard_map/ppermute | solution.py:29
  30.4 5.7 %collective-permute-done.9.refs_7_ = bf16[64,1152]{1,0:T(8,128)(2,1)S(1)} collective-permute-done((bf16[64,1152]{1,0:T(8,128)(2,1)S(1)}, bf16[64,1152]{1,0:T(8,128)(2,1)S(1)}, u32[]{:S(2)}, u32[]{:S(2)}) %collective-permute-start.9) | collective-permute-done | bytes 147488 | tf_op jit(solution)/shard_map/ppermute | solution.py:29
  36.8 3.4 %shard_map.190 = (f32[128,128]{1,0:T(8,128)}, bf16[128,1024]{1,0:T(8,128)(2,1)}) custom-call(s32[1]{0:T(128)} %bitcast.3.tensor, bf16[128,2,8192]{2,1,0:T(2,128)(2,1)} %bitcast.22, bf16[8192,128]{1,0:T(8,128)(2,1)} %weight.3), custom_call_target="tpu_custom_call" | custom-call | tf_op jit(solution)/shard_map/pallas_call | solution.py:191
  40.2 3.8 %shard_map.191 = (bf16[256,128]{1,0:T(8,128)(2,1)}, bf16[256,128]{1,0:T(8,128)(2,1)}, s32[8]{0:T(128)}) custom-call(bf16[64,1152]{1,0:T(8,128)(2,1)} %copy-done.4, bf16[64,1152]{1,0:T(8,128)(2,1)} %copy-done.7, bf16[64,1152]{1,0:T(8,128)(2,1)} %copy-done.9, bf16[64,1152]{1,0:T(8,128)(2,1)} %copy-done.10, bf16[64,1152]{1,0:T(8,128)(2,1)} %copy-done.11, ...), custom_call_target="tpu_custom_call" | custom-call | tf_op jit(solution)/shard_map/pallas_call | solution.py:247
  47.0 2.6 %collective-permute-start.12 = (bf16[256,128]{1,0:T(8,128)(2,1)S(1)}, bf16[256,128]{1,0:T(8,128)(2,1)S(1)}, u32[]{:S(2)}, u32[]{:S(2)}) collective-permute-start(bf16[256,128]{1,0:T(8,128)(2,1)S(1)} %add_convert_fusion.5), channel_id=1, source_target_pairs={{0,4},{1,5},{2,6},{3,7},{4,0},{5,1},{6,2},{7,3},{8,12},{9,13},{10,... | collective-permute-start | bytes 196616 | tf_op jit(solution)/shard_map/ppermute | solution.py:478
  49.6 1.9 %collective-permute-start.11 = (bf16[256,128]{1,0:T(8,128)(2,1)S(1)}, bf16[256,128]{1,0:T(8,128)(2,1)S(1)}, u32[]{:S(2)}, u32[]{:S(2)}) collective-permute-start(bf16[256,128]{1,0:T(8,128)(2,1)S(1)} %add_convert_fusion.5), channel_id=1, source_target_pairs={{0,2},{1,3},{2,4},{3,5},{4,6},{5,7},{6,0},{7,1},{8,10},{9,11},{10,... | collective-permute-start | bytes 196616 | tf_op jit(solution)/shard_map/ppermute | solution.py:478
  56.1 4.0 %shard_map.192 = (bf16[64,1152]{1,0:T(8,128)(2,1)}, bf16[64,1152]{1,0:T(8,128)(2,1)}, bf16[64,1152]{1,0:T(8,128)(2,1)}, bf16[64,1152]{1,0:T(8,128)(2,1)}, bf16[3...) custom-call(s32[8]{0:T(128)} %get-tuple-element.111.names, ...), custom_call_target="tpu_custom_call" | custom-call | tf_op jit(solution)/shard_map/pallas_call | solution.py:319
  60.2 3.2 %collective-permute-start.16 = (bf16[64,1152]{1,0:T(8,128)(2,1)}, bf16[64,1152]{1,0:T(8,128)(2,1)S(1)}, u32[]{:S(2)}, u32[]{:S(2)}) collective-permute-start(bf16[64,1152]{1,0:T(8,128)(2,1)} %get-tuple-element.116), channel_id=1, source_target_pairs={{0,224},{32,0},{64,32},{96,64},{128,96},{160,128},{192,160},{224,1... | collective-permute-start | bytes 442376 | tf_op jit(solution)/shard_map/ppermute | solution.py:29
  63.6 4.2 %collective-permute-start.21 = (bf16[32,1152]{1,0:T(8,128)(2,1)}, bf16[32,1152]{1,0:T(8,128)(2,1)S(1)}, u32[]{:S(2)}, u32[]{:S(2)}) collective-permute-start(bf16[32,1152]{1,0:T(8,128)(2,1)} %get-tuple-element.126), channel_id=1, source_target_pairs={{0,192},{32,224},{64,0},{96,32},{128,64},{160,96},{192,128},{224,1... | collective-permute-start | bytes 221192 | tf_op jit(solution)/shard_map/ppermute | solution.py:29
  68.6 3.6 %collective-permute-start.18 = (bf16[64,1152]{1,0:T(8,128)(2,1)}, bf16[64,1152]{1,0:T(8,128)(2,1)S(1)}, u32[]{:S(2)}, u32[]{:S(2)}) collective-permute-start(bf16[64,1152]{1,0:T(8,128)(2,1)} %get-tuple-element.120), channel_id=1, source_target_pairs={{0,224},{32,0},{64,32},{96,64},{128,96},{160,128},{192,160},{224,1... | collective-permute-start | bytes 442376 | tf_op jit(solution)/shard_map/ppermute | solution.py:29
  76.0 2.5 %collective-permute-start.22 = (bf16[64,1152]{1,0:T(8,128)(2,1)S(1)}, bf16[64,1152]{1,0:T(8,128)(2,1)S(1)}, u32[]{:S(2)}, u32[]{:S(2)}) collective-permute-start(bf16[64,1152]{1,0:T(8,128)(2,1)S(1)} %pad_maximum_fusion.2), channel_id=1, source_target_pairs={{0,192},{32,224},{64,0},{96,32},{128,64},{160,96},{192,128},{224,1... | collective-permute-start | bytes 442376 | tf_op jit(solution)/shard_map/ppermute | solution.py:29
  78.7 4.2 %collective-permute-done.20.refs_3_ = bf16[64,1152]{1,0:T(8,128)(2,1)S(1)} collective-permute-done((bf16[64,1152]{1,0:T(8,128)(2,1)S(1)}, bf16[64,1152]{1,0:T(8,128)(2,1)S(1)}, u32[]{:S(2)}, u32[]{:S(2)}) %collective-permute-start.20) | collective-permute-done | bytes 147488 | tf_op jit(solution)/shard_map/ppermute | solution.py:29
  83.9 2.7 %shard_map.193 = (f32[64,1024]{1,0:T(8,128)}, f32[64,1024]{1,0:T(8,128)}, f32[64,1024]{1,0:T(8,128)}, f32[64,128]{1,0:T(8,128)}, f32[64,128]{1,0:T(8,128)}, /*index=5*/f32[64,128]{1,0:T(8,128)}, bf16[64,1152]{1,0:T(8,128)(2,1)}) custom-call(bf16[64,1152]{1,0:T(8,128)(2,1)} %get-tuple-element.114.refs_0_, bf16[64,1152]{1,0:T(8,128)(2,1)} %copy-done.6, ...), custom_call_target="tpu_custom_call" | custom-call | tf_op jit(solution)/shard_map/pallas_call | solution.py:371
  86.7 3.1 %collective-permute-start.23 = (bf16[64,1152]{1,0:T(8,128)(2,1)}, bf16[64,1152]{1,0:T(8,128)(2,1)S(1)}, u32[]{:S(2)}, u32[]{:S(2)}) collective-permute-start(bf16[64,1152]{1,0:T(8,128)(2,1)} %get-tuple-element.145.refs_0_), channel_id=1, source_target_pairs={{0,8},{8,16},{16,24},{24,0},{1,9},{9,17},{17,25},{25,1},{2,10},{10... | collective-permute-start | bytes 442376 | tf_op jit(solution)/shard_map/ppermute | solution.py:29
  91.5 2.8 %shard_map.194 = (f32[128,128]{1,0:T(8,128)S(1)}, bf16[128,1024]{1,0:T(8,128)(2,1)S(1)}) custom-call(s32[1]{0:T(128)} %bitcast.3.tensor, bf16[128,2,8192]{2,1,0:T(2,128)(2,1)} %bitcast.23, bf16[8192,128]{1,0:T(8,128)(2,1)} %weight.3), custom_call_target="tpu_custom_call" | custom-call | tf_op jit(solution)/shard_map/pallas_call | solution.py:191
  95.9 2.1 %collective-permute-done.24.refs_2_ = bf16[64,1152]{1,0:T(8,128)(2,1)S(1)} collective-permute-done((bf16[64,1152]{1,0:T(8,128)(2,1)}, bf16[64,1152]{1,0:T(8,128)(2,1)S(1)}, u32[]{:S(2)}, u32[]{:S(2)}) %collective-permute-start.24) | collective-permute-done | bytes 147488 | tf_op jit(solution)/shard_map/ppermute | solution.py:29
  99.9 3.9 %collective-permute-start.28 = (bf16[64,1152]{1,0:T(8,128)(2,1)S(1)}, bf16[64,1152]{1,0:T(8,128)(2,1)S(1)}, u32[]{:S(2)}, u32[]{:S(2)}) collective-permute-start(bf16[64,1152]{1,0:T(8,128)(2,1)S(1)} %shard_map.195.refs_2_.refs_6_), channel_id=1, source_target_pairs={{0,64},{32,96},{64,128},{96,160},{128,192},{160,224},{192,0},{224,... | collective-permute-start | bytes 442376 | tf_op jit(solution)/shard_map/ppermute | solution.py:29
  107.4 3.0 %collective-permute-done.28.refs_5_.refs_9_ = bf16[64,1152]{1,0:T(8,128)(2,1)S(1)} collective-permute-done((bf16[64,1152]{1,0:T(8,128)(2,1)S(1)}, bf16[64,1152]{1,0:T(8,128)(2,1)S(1)}, u32[]{:S(2)}, u32[]{:S(2)}) %collective-permute-start.28) | collective-permute-done | bytes 147488 | tf_op jit(solution)/shard_map/ppermute | solution.py:29
  114.4 2.1 %collective-permute-start.32 = (bf16[64,1152]{1,0:T(8,128)(2,1)S(1)}, bf16[64,1152]{1,0:T(8,128)(2,1)S(1)}, u32[]{:S(2)}, u32[]{:S(2)}) collective-permute-start(bf16[64,1152]{1,0:T(8,128)(2,1)S(1)} %collective-permute-done.28.refs_5_.refs_9_), channel_id=1, source_target_pairs={{0,64},{32,96},{64,128},{96,160},{128,192},{160,224},{192,0},{224,... | collective-permute-start | bytes 442376 | tf_op jit(solution)/shard_map/ppermute | solution.py:29
  116.4 2.5 %collective-permute-done.30.refs_7_.refs_11_ = bf16[64,1152]{1,0:T(8,128)(2,1)S(1)} collective-permute-done((bf16[64,1152]{1,0:T(8,128)(2,1)S(1)}, bf16[64,1152]{1,0:T(8,128)(2,1)S(1)}, u32[]{:S(2)}, u32[]{:S(2)}) %collective-permute-start.30) | collective-permute-done | bytes 147488 | tf_op jit(solution)/shard_map/ppermute | solution.py:29
  118.9 3.7 %collective-permute-done.32.refs_9_.refs_13_ = bf16[64,1152]{1,0:T(8,128)(2,1)S(1)} collective-permute-done((bf16[64,1152]{1,0:T(8,128)(2,1)S(1)}, bf16[64,1152]{1,0:T(8,128)(2,1)S(1)}, u32[]{:S(2)}, u32[]{:S(2)}) %collective-permute-start.32) | collective-permute-done | bytes 147488 | tf_op jit(solution)/shard_map/ppermute | solution.py:29
  127.1 3.6 %collective-permute-start.35 = (f32[32,256]{1,0:T(8,128)S(1)}, f32[32,256]{1,0:T(8,128)S(1)}, u32[]{:S(2)}, u32[]{:S(2)}) collective-permute-start(f32[32,256]{1,0:T(8,128)S(1)} %add.93.refs_2_), channel_id=1, source_target_pairs={{0,4},{1,5},{2,6},{3,7},{4,0},{5,1},{6,2},{7,3},{8,12},{9,13},{10,... | collective-permute-start | bytes 98312 | tf_op jit(solution)/shard_map/ppermute | solution.py:478
  130.7 2.1 %collective-permute-done.35.refs_4_ = f32[32,256]{1,0:T(8,128)S(1)} collective-permute-done((f32[32,256]{1,0:T(8,128)S(1)}, f32[32,256]{1,0:T(8,128)S(1)}, u32[]{:S(2)}, u32[]{:S(2)}) %collective-permute-start.35) | collective-permute-done | bytes 32800 | tf_op jit(solution)/shard_map/ppermute | solution.py:478
  132.8 1.8 %collective-permute-done.36.refs_5_ = f32[32,256]{1,0:T(8,128)S(1)} collective-permute-done((f32[32,256]{1,0:T(8,128)S(1)}, f32[32,256]{1,0:T(8,128)S(1)}, u32[]{:S(2)}, u32[]{:S(2)}) %collective-permute-start.36) | collective-permute-done | bytes 32800 | tf_op jit(solution)/shard_map/ppermute | solution.py:478
  (116 shorter events, 35.0 us)
Async XLA Ops:
  4.8 35.5 %collective-permute-start = (bf16[272,1152]{1,0:T(8,128)(2,1)}, bf16[272,1152]{1,0:T(8,128)(2,1)}, u32[]{:S(2)}, u32[]{:S(2)}) collective-permute-start(bf16[272,1152]{1,0:T(8,128)(2,1)} %get-tuple-element.83), channel_id=1, source_target_pairs={{0,8},{8,16},{16,24},{24,0},{1,9},{9,17},{17,25},{25,1},{2,10},{10... | collective-permute-start | bytes 1880072 | tf_op jit(solution)/shard_map/ppermute | solution.py:29
  5.3 34.9 %collective-permute-start.1 = (bf16[272,1152]{1,0:T(8,128)(2,1)}, bf16[272,1152]{1,0:T(8,128)(2,1)}, u32[]{:S(2)}, u32[]{:S(2)}) collective-permute-start(bf16[272,1152]{1,0:T(8,128)(2,1)} %get-tuple-element.84), channel_id=1, source_target_pairs={{0,16},{8,24},{16,0},{24,8},{1,17},{9,25},{17,1},{25,9},{2,18},{10... | collective-permute-start | bytes 1880072 | tf_op jit(solution)/shard_map/ppermute | solution.py:29
  7.7 32.5 %collective-permute-start.2 = (bf16[272,1152]{1,0:T(8,128)(2,1)}, bf16[272,1152]{1,0:T(8,128)(2,1)}, u32[]{:S(2)}, u32[]{:S(2)}) collective-permute-start(bf16[272,1152]{1,0:T(8,128)(2,1)} %get-tuple-element.85), channel_id=1, source_target_pairs={{0,24},{8,0},{16,8},{24,16},{1,25},{9,1},{17,9},{25,17},{2,26},{10... | collective-permute-start | bytes 1880072 | tf_op jit(solution)/shard_map/ppermute | solution.py:29
  7.8 9.2 %collective-permute-start.3 = (bf16[64,1152]{1,0:T(8,128)(2,1)S(1)}, bf16[64,1152]{1,0:T(8,128)(2,1)S(1)}, u32[]{:S(2)}, u32[]{:S(2)}) collective-permute-start(bf16[64,1152]{1,0:T(8,128)(2,1)S(1)} %pad_maximum_fusion.refs_0_), channel_id=1, source_target_pairs={{0,32},{32,64},{64,96},{96,128},{128,160},{160,192},{192,224},{224... | collective-permute-start | bytes 442376 | tf_op jit(solution)/shard_map/ppermute | solution.py:29
  9.8 7.2 %collective-permute-start.4 = (bf16[64,1152]{1,0:T(8,128)(2,1)S(1)}, bf16[64,1152]{1,0:T(8,128)(2,1)S(1)}, u32[]{:S(2)}, u32[]{:S(2)}) collective-permute-start(bf16[64,1152]{1,0:T(8,128)(2,1)S(1)} %pad_maximum_fusion.refs_0_), channel_id=1, source_target_pairs={{0,224},{32,0},{64,32},{96,64},{128,96},{160,128},{192,160},{224,1... | collective-permute-start | bytes 442376 | tf_op jit(solution)/shard_map/ppermute | solution.py:29
  17.0 6.4 %collective-permute-start.5 = (bf16[64,1152]{1,0:T(8,128)(2,1)S(1)}, bf16[64,1152]{1,0:T(8,128)(2,1)S(1)}, u32[]{:S(2)}, u32[]{:S(2)}) collective-permute-start(bf16[64,1152]{1,0:T(8,128)(2,1)S(1)} %collective-permute-done.3.refs_1_), channel_id=1, source_target_pairs={{0,32},{32,64},{64,96},{96,128},{128,160},{160,192},{192,224},{224... | collective-permute-start | bytes 442376 | tf_op jit(solution)/shard_map/ppermute | solution.py:29
  17.7 5.7 %collective-permute-start.6 = (bf16[64,1152]{1,0:T(8,128)(2,1)S(1)}, bf16[64,1152]{1,0:T(8,128)(2,1)S(1)}, u32[]{:S(2)}, u32[]{:S(2)}) collective-permute-start(bf16[64,1152]{1,0:T(8,128)(2,1)S(1)} %collective-permute-done.4.refs_2_), channel_id=1, source_target_pairs={{0,224},{32,0},{64,32},{96,64},{128,96},{160,128},{192,160},{224,1... | collective-permute-start | bytes 442376 | tf_op jit(solution)/shard_map/ppermute | solution.py:29
  23.4 6.4 %collective-permute-start.7 = (bf16[64,1152]{1,0:T(8,128)(2,1)S(1)}, bf16[64,1152]{1,0:T(8,128)(2,1)S(1)}, u32[]{:S(2)}, u32[]{:S(2)}) collective-permute-start(bf16[64,1152]{1,0:T(8,128)(2,1)S(1)} %collective-permute-done.5.refs_3_), channel_id=1, source_target_pairs={{0,32},{32,64},{64,96},{96,128},{128,160},{160,192},{192,224},{224... | collective-permute-start | bytes 442376 | tf_op jit(solution)/shard_map/ppermute | solution.py:29
  24.1 5.7 %collective-permute-start.8 = (bf16[64,1152]{1,0:T(8,128)(2,1)S(1)}, bf16[64,1152]{1,0:T(8,128)(2,1)S(1)}, u32[]{:S(2)}, u32[]{:S(2)}) collective-permute-start(bf16[64,1152]{1,0:T(8,128)(2,1)S(1)} %collective-permute-done.6.refs_4_), channel_id=1, source_target_pairs={{0,224},{32,0},{64,32},{96,64},{128,96},{160,128},{192,160},{224,1... | collective-permute-start | bytes 442376 | tf_op jit(solution)/shard_map/ppermute | solution.py:29
  29.8 6.4 %collective-permute-start.9 = (bf16[64,1152]{1,0:T(8,128)(2,1)S(1)}, bf16[64,1152]{1,0:T(8,128)(2,1)S(1)}, u32[]{:S(2)}, u32[]{:S(2)}) collective-permute-start(bf16[64,1152]{1,0:T(8,128)(2,1)S(1)} %collective-permute-done.7.refs_5_), channel_id=1, source_target_pairs={{0,32},{32,64},{64,96},{96,128},{128,160},{160,192},{192,224},{224... | collective-permute-start | bytes 442376 | tf_op jit(solution)/shard_map/ppermute | solution.py:29
  46.5 5.1 %collective-permute-start.13 = (bf16[256,128]{1,0:T(8,128)(2,1)S(1)}, bf16[256,128]{1,0:T(8,128)(2,1)S(1)}, u32[]{:S(2)}, u32[]{:S(2)}) collective-permute-start(bf16[256,128]{1,0:T(8,128)(2,1)S(1)} %add_convert_fusion.5), channel_id=1, source_target_pairs={{0,6},{1,7},{2,0},{3,1},{4,2},{5,3},{6,4},{7,5},{8,14},{9,15},{10,... | collective-permute-start | bytes 196616 | tf_op jit(solution)/shard_map/ppermute | solution.py:478
  47.0 6.2 %collective-permute-start.12 = (bf16[256,128]{1,0:T(8,128)(2,1)S(1)}, bf16[256,128]{1,0:T(8,128)(2,1)S(1)}, u32[]{:S(2)}, u32[]{:S(2)}) collective-permute-start(bf16[256,128]{1,0:T(8,128)(2,1)S(1)} %add_convert_fusion.5), channel_id=1, source_target_pairs={{0,4},{1,5},{2,6},{3,7},{4,0},{5,1},{6,2},{7,3},{8,12},{9,13},{10,... | collective-permute-start | bytes 196616 | tf_op jit(solution)/shard_map/ppermute | solution.py:478
  60.1 8.5 %collective-permute-start.15 = (bf16[64,1152]{1,0:T(8,128)(2,1)}, bf16[64,1152]{1,0:T(8,128)(2,1)S(1)}, u32[]{:S(2)}, u32[]{:S(2)}) collective-permute-start(bf16[64,1152]{1,0:T(8,128)(2,1)} %get-tuple-element.115), channel_id=1, source_target_pairs={{0,32},{32,64},{64,96},{96,128},{128,160},{160,192},{192,224},{224... | collective-permute-start | bytes 442376 | tf_op jit(solution)/shard_map/ppermute | solution.py:29
  60.2 8.4 %collective-permute-start.16 = (bf16[64,1152]{1,0:T(8,128)(2,1)}, bf16[64,1152]{1,0:T(8,128)(2,1)S(1)}, u32[]{:S(2)}, u32[]{:S(2)}) collective-permute-start(bf16[64,1152]{1,0:T(8,128)(2,1)} %get-tuple-element.116), channel_id=1, source_target_pairs={{0,224},{32,0},{64,32},{96,64},{128,96},{160,128},{192,160},{224,1... | collective-permute-start | bytes 442376 | tf_op jit(solution)/shard_map/ppermute | solution.py:29
  63.5 8.8 %collective-permute-start.19 = (bf16[32,1152]{1,0:T(8,128)(2,1)}, bf16[32,1152]{1,0:T(8,128)(2,1)S(1)}, u32[]{:S(2)}, u32[]{:S(2)}) collective-permute-start(bf16[32,1152]{1,0:T(8,128)(2,1)} %get-tuple-element.123), channel_id=1, source_target_pairs={{0,64},{32,96},{64,128},{96,160},{128,192},{160,224},{192,0},{224,... | collective-permute-start | bytes 221192 | tf_op jit(solution)/shard_map/ppermute | solution.py:29
  63.6 11.4 %collective-permute-start.21 = (bf16[32,1152]{1,0:T(8,128)(2,1)}, bf16[32,1152]{1,0:T(8,128)(2,1)S(1)}, u32[]{:S(2)}, u32[]{:S(2)}) collective-permute-start(bf16[32,1152]{1,0:T(8,128)(2,1)} %get-tuple-element.126), channel_id=1, source_target_pairs={{0,192},{32,224},{64,0},{96,32},{128,64},{160,96},{192,128},{224,1... | collective-permute-start | bytes 221192 | tf_op jit(solution)/shard_map/ppermute | solution.py:29
  68.6 10.1 %collective-permute-start.17 = (bf16[64,1152]{1,0:T(8,128)(2,1)}, bf16[64,1152]{1,0:T(8,128)(2,1)S(1)}, u32[]{:S(2)}, u32[]{:S(2)}) collective-permute-start(bf16[64,1152]{1,0:T(8,128)(2,1)} %get-tuple-element.119), channel_id=1, source_target_pairs={{0,32},{32,64},{64,96},{96,128},{128,160},{160,192},{192,224},{224... | collective-permute-start | bytes 442376 | tf_op jit(solution)/shard_map/ppermute | solution.py:29
  68.6 10.1 %collective-permute-start.18 = (bf16[64,1152]{1,0:T(8,128)(2,1)}, bf16[64,1152]{1,0:T(8,128)(2,1)S(1)}, u32[]{:S(2)}, u32[]{:S(2)}) collective-permute-start(bf16[64,1152]{1,0:T(8,128)(2,1)} %get-tuple-element.120), channel_id=1, source_target_pairs={{0,224},{32,0},{64,32},{96,64},{128,96},{160,128},{192,160},{224,1... | collective-permute-start | bytes 442376 | tf_op jit(solution)/shard_map/ppermute | solution.py:29
  73.2 9.6 %collective-permute-start.20 = (bf16[64,1152]{1,0:T(8,128)(2,1)S(1)}, bf16[64,1152]{1,0:T(8,128)(2,1)S(1)}, u32[]{:S(2)}, u32[]{:S(2)}) collective-permute-start(bf16[64,1152]{1,0:T(8,128)(2,1)S(1)} %pad_maximum_fusion.1), channel_id=1, source_target_pairs={{0,64},{32,96},{64,128},{96,160},{128,192},{160,224},{192,0},{224,... | collective-permute-start | bytes 442376 | tf_op jit(solution)/shard_map/ppermute | solution.py:29
  76.0 7.3 %collective-permute-start.22 = (bf16[64,1152]{1,0:T(8,128)(2,1)S(1)}, bf16[64,1152]{1,0:T(8,128)(2,1)S(1)}, u32[]{:S(2)}, u32[]{:S(2)}) collective-permute-start(bf16[64,1152]{1,0:T(8,128)(2,1)S(1)} %pad_maximum_fusion.2), channel_id=1, source_target_pairs={{0,192},{32,224},{64,0},{96,32},{128,64},{160,96},{192,128},{224,1... | collective-permute-start | bytes 442376 | tf_op jit(solution)/shard_map/ppermute | solution.py:29
  86.7 9.2 %collective-permute-start.23 = (bf16[64,1152]{1,0:T(8,128)(2,1)}, bf16[64,1152]{1,0:T(8,128)(2,1)S(1)}, u32[]{:S(2)}, u32[]{:S(2)}) collective-permute-start(bf16[64,1152]{1,0:T(8,128)(2,1)} %get-tuple-element.145.refs_0_), channel_id=1, source_target_pairs={{0,8},{8,16},{16,24},{24,0},{1,9},{9,17},{17,25},{25,1},{2,10},{10... | collective-permute-start | bytes 442376 | tf_op jit(solution)/shard_map/ppermute | solution.py:29
  89.7 8.2 %collective-permute-start.24 = (bf16[64,1152]{1,0:T(8,128)(2,1)}, bf16[64,1152]{1,0:T(8,128)(2,1)S(1)}, u32[]{:S(2)}, u32[]{:S(2)}) collective-permute-start(bf16[64,1152]{1,0:T(8,128)(2,1)} %get-tuple-element.145.refs_0_), channel_id=1, source_target_pairs={{0,16},{8,24},{16,0},{24,8},{1,17},{9,25},{17,1},{25,9},{2,18},{10... | collective-permute-start | bytes 442376 | tf_op jit(solution)/shard_map/ppermute | solution.py:29
  89.9 9.5 %collective-permute-start.25 = (bf16[64,1152]{1,0:T(8,128)(2,1)}, bf16[64,1152]{1,0:T(8,128)(2,1)S(1)}, u32[]{:S(2)}, u32[]{:S(2)}) collective-permute-start(bf16[64,1152]{1,0:T(8,128)(2,1)} %get-tuple-element.145.refs_0_), channel_id=1, source_target_pairs={{0,24},{8,0},{16,8},{24,16},{1,25},{9,1},{17,9},{25,17},{2,26},{10... | collective-permute-start | bytes 442376 | tf_op jit(solution)/shard_map/ppermute | solution.py:29
  99.9 10.5 %collective-permute-start.28 = (bf16[64,1152]{1,0:T(8,128)(2,1)S(1)}, bf16[64,1152]{1,0:T(8,128)(2,1)S(1)}, u32[]{:S(2)}, u32[]{:S(2)}) collective-permute-start(bf16[64,1152]{1,0:T(8,128)(2,1)S(1)} %shard_map.195.refs_2_.refs_6_), channel_id=1, source_target_pairs={{0,64},{32,96},{64,128},{96,160},{128,192},{160,224},{192,0},{224,... | collective-permute-start | bytes 442376 | tf_op jit(solution)/shard_map/ppermute | solution.py:29
  103.8 9.1 %collective-permute-start.29 = (bf16[64,1152]{1,0:T(8,128)(2,1)S(1)}, bf16[64,1152]{1,0:T(8,128)(2,1)S(1)}, u32[]{:S(2)}, u32[]{:S(2)}) collective-permute-start(bf16[64,1152]{1,0:T(8,128)(2,1)S(1)} %shard_map.195.refs_2_.refs_6_), channel_id=1, source_target_pairs={{0,192},{32,224},{64,0},{96,32},{128,64},{160,96},{192,128},{224,1... | collective-permute-start | bytes 442376 | tf_op jit(solution)/shard_map/ppermute | solution.py:29
  104.1 12.3 %collective-permute-start.26 = (bf16[64,1152]{1,0:T(8,128)(2,1)S(1)}, bf16[64,1152]{1,0:T(8,128)(2,1)S(1)}, u32[]{:S(2)}, u32[]{:S(2)}) collective-permute-start(bf16[64,1152]{1,0:T(8,128)(2,1)S(1)} %shard_map.195.refs_2_.refs_6_), channel_id=1, source_target_pairs={{0,32},{32,64},{64,96},{96,128},{128,160},{160,192},{192,224},{224... | collective-permute-start | bytes 442376 | tf_op jit(solution)/shard_map/ppermute | solution.py:29
  105.7 10.7 %collective-permute-start.27 = (bf16[64,1152]{1,0:T(8,128)(2,1)S(1)}, bf16[64,1152]{1,0:T(8,128)(2,1)S(1)}, u32[]{:S(2)}, u32[]{:S(2)}) collective-permute-start(bf16[64,1152]{1,0:T(8,128)(2,1)S(1)} %shard_map.195.refs_2_.refs_6_), channel_id=1, source_target_pairs={{0,224},{32,0},{64,32},{96,64},{128,96},{160,128},{192,160},{224,1... | collective-permute-start | bytes 442376 | tf_op jit(solution)/shard_map/ppermute | solution.py:29
  110.4 8.5 %collective-permute-start.30 = (bf16[64,1152]{1,0:T(8,128)(2,1)S(1)}, bf16[64,1152]{1,0:T(8,128)(2,1)S(1)}, u32[]{:S(2)}, u32[]{:S(2)}) collective-permute-start(bf16[64,1152]{1,0:T(8,128)(2,1)S(1)} %collective-permute-done.28.refs_5_.refs_9_), channel_id=1, source_target_pairs={{0,32},{32,64},{64,96},{96,128},{128,160},{160,192},{192,224},{224... | collective-permute-start | bytes 442376 | tf_op jit(solution)/shard_map/ppermute | solution.py:29
  112.8 6.0 %collective-permute-start.31 = (bf16[64,1152]{1,0:T(8,128)(2,1)S(1)}, bf16[64,1152]{1,0:T(8,128)(2,1)S(1)}, u32[]{:S(2)}, u32[]{:S(2)}) collective-permute-start(bf16[64,1152]{1,0:T(8,128)(2,1)S(1)} %collective-permute-done.29.refs_6_.refs_10_), channel_id=1, source_target_pairs={{0,224},{32,0},{64,32},{96,64},{128,96},{160,128},{192,160},{224,1... | collective-permute-start | bytes 442376 | tf_op jit(solution)/shard_map/ppermute | solution.py:29
  114.4 8.2 %collective-permute-start.32 = (bf16[64,1152]{1,0:T(8,128)(2,1)S(1)}, bf16[64,1152]{1,0:T(8,128)(2,1)S(1)}, u32[]{:S(2)}, u32[]{:S(2)}) collective-permute-start(bf16[64,1152]{1,0:T(8,128)(2,1)S(1)} %collective-permute-done.28.refs_5_.refs_9_), channel_id=1, source_target_pairs={{0,64},{32,96},{64,128},{96,160},{128,192},{160,224},{192,0},{224,... | collective-permute-start | bytes 442376 | tf_op jit(solution)/shard_map/ppermute | solution.py:29
  125.4 5.3 %collective-permute-start.34 = (f32[32,256]{1,0:T(8,128)S(1)}, f32[32,256]{1,0:T(8,128)S(1)}, u32[]{:S(2)}, u32[]{:S(2)}) collective-permute-start(f32[32,256]{1,0:T(8,128)S(1)} %add.93.refs_2_), channel_id=1, source_target_pairs={{0,2},{1,3},{2,4},{3,5},{4,6},{5,7},{6,0},{7,1},{8,10},{9,11},{10,... | collective-permute-start | bytes 98312 | tf_op jit(solution)/shard_map/ppermute | solution.py:478
  127.1 5.7 %collective-permute-start.35 = (f32[32,256]{1,0:T(8,128)S(1)}, f32[32,256]{1,0:T(8,128)S(1)}, u32[]{:S(2)}, u32[]{:S(2)}) collective-permute-start(f32[32,256]{1,0:T(8,128)S(1)} %add.93.refs_2_), channel_id=1, source_target_pairs={{0,4},{1,5},{2,6},{3,7},{4,0},{5,1},{6,2},{7,3},{8,12},{9,13},{10,... | collective-permute-start | bytes 98312 | tf_op jit(solution)/shard_map/ppermute | solution.py:478
  (26 other events, 176.8 us)

commit v3 on v2

--- a/solution.py
+++ b/solution.py
@@ -408,14 +408,14 @@
     )(index, *arrays)
 
 
-def decode_in_kernel(rank, firsts, parts, slots, *refs):
+def decode_in_kernel(rank, firsts, parts, slots, before, *refs):
     xs, refs = refs[:parts], refs[parts:]
     *refs, out = refs
     width = xs[0].shape[1]
     count = xs[0].shape[0]
     for i, x in enumerate(xs):
         here = slots[:, i * count : (i + 1) * count]
-        total = jnp.zeros((rank, count), F32)
+        total = before[:, i * count : (i + 1) * count]
         for first, ref in zip(firsts, refs):
             both = dot(ref[:, :width], x[...], ((1,), (1,)))
             for j in range(ref.shape[0] // rank):
@@ -423,14 +423,14 @@
         out[:, i * count : (i + 1) * count] = total
 
 
-def decode_in(slots, xs, fresh, firsts, rank):
+def decode_in(slots, before, xs, fresh, firsts, rank):
     return pl.pallas_call(
         functools.partial(decode_in_kernel, rank, firsts, len(xs)),
-        in_specs=vmem(1 + len(xs) + len(fresh)),
+        in_specs=vmem(2 + len(xs) + len(fresh)),
         out_specs=vmem()[0],
         out_shape=shape((rank, slots.shape[1]), F32),
         compiler_params=SMALL,
-    )(slots, *xs, *fresh)
+    )(slots, before, *xs, *fresh)
 
 
 def decode_out_kernel(rank, parts, firsts, slots, *refs):
@@ -579,7 +579,10 @@
     in_row, wanted, slots, late = barrier((in_row, wanted, slots, late))
     served_fresh, firsts = two_stage(pick(wanted, in_row, rank), rows_dp, owned)
 
-    dec_part = decode_in(slots, [early[1], late[1]], served_fresh, firsts, rank)
+    near, xs = 5, [early[1], late[1]]
+    dec_part = jnp.zeros((rank, count), F32)
+    dec_part = decode_in(slots, dec_part, xs, served_fresh[:near], firsts[:near], rank)
+    dec_part = decode_in(slots, dec_part, xs, served_fresh[near:], firsts[near:], rank)
     decoded = decode_out(
         slots, [early[0], late[0]], tensor_parts(dec_part), served_fresh, firsts, rank
     )

time: 136 us -> 135 us (level)
  no operation moved by 1% of the time
where the time goes in v3:
time: 135 us; the launch traced here: 134 us
  starting transfers between devices  58.2 us (43%)
  waiting for transfers between devices  43.3 us (32%)
  Pallas kernels  24.2 us (18%)
  local copies, waits for them, and re-layouts  4.31 us (3%)
  other arithmetic  3.33 us (2%)
    ppermute x28, starting transfers between devices, shift(): lax.ppermute(x, axis, [(i, (i + distance) % size) for i in range(size)])  47.7 us
    ppermute x28, waiting for transfers between devices, shift(): lax.ppermute(x, axis, [(i, (i + distance) % size) for i in range(size)])  33.4 us
    ppermute x6, starting transfers between devices, chips(): lax.ppermute(x, 'tensor', [(i, (i + 2 * d) % size) for i in range(size)])  10 us
    ppermute x6, waiting for transfers between devices, chips(): lax.ppermute(x, 'tensor', [(i, (i + 2 * d) % size) for i in range(size)])  6.31 us
    pallas_call x2, Pallas kernels, frozen(): pl.pallas_call(frozen_kernel, grid_spec=pltpu.PrefetchScalarGridSpec(num_...  6.24 us
    pallas_call x1, Pallas kernels, begin(): pl.pallas_call(functools.partial(begin_kernel, rows, groups), in_specs=sm...  4.1 us
    pallas_call x1, Pallas kernels, grad(): pl.pallas_call(functools.partial(grad_kernel, rank, rows, len(lows), owne...  3.98 us
    unnamed x42, local copies, waits for them, and re-layouts  3.93 us
  transfers between devices with their start and end apart: 37, of which 21 were waited for; matrix products, arithmetic and copies ran while one was open for 2% of the time, Pallas kernels for 5%

profile of v3, /device:TPU:14, one launch (start us, length us, event | category | flops | bytes accessed | tf_op | source)
XLA Modules:
  0.0 134.3 jit_solution(15320808536400739473)
XLA Ops:
  0.7 4.1 %shard_map.189 = (bf16[272,1152]{1,0:T(8,128)(2,1)}, bf16[272,1152]{1,0:T(8,128)(2,1)}, bf16[272,1152]{1,0:T(8,128)(2,1)}, bf16[272,1152]{1,0:T(8,128)(2,1)}) custom-call(s32[8]{0:T(128)} %tenant.1, s32[8]{0:T(128)} %count.1, bf16[1024,1024]{1,0:T(8,128)(2,1)} %x.1, bf16[1024,128]{1,0:T(8,128)(2,1)} %dy.1), custom_call_target="tpu_custom_call" | custom-call | tf_op jit(solution)/shard_map/pallas_call | solution.py:150
  5.3 2.4 %collective-permute-start.1 = (bf16[272,1152]{1,0:T(8,128)(2,1)}, bf16[272,1152]{1,0:T(8,128)(2,1)}, u32[]{:S(2)}, u32[]{:S(2)}) collective-permute-start(bf16[272,1152]{1,0:T(8,128)(2,1)} %get-tuple-element.84), channel_id=1, source_target_pairs={{0,16},{8,24},{16,0},{24,8},{1,17},{9,25},{17,1},{25,9},{2,18},{10... | collective-permute-start | bytes 1880072 | tf_op jit(solution)/shard_map/ppermute | solution.py:29
  7.8 2.0 %collective-permute-start.3 = (bf16[64,1152]{1,0:T(8,128)(2,1)S(1)}, bf16[64,1152]{1,0:T(8,128)(2,1)S(1)}, u32[]{:S(2)}, u32[]{:S(2)}) collective-permute-start(bf16[64,1152]{1,0:T(8,128)(2,1)S(1)} %pad_maximum_fusion.refs_0_), channel_id=1, source_target_pairs={{0,32},{32,64},{64,96},{96,128},{128,160},{160,192},{192,224},{224... | collective-permute-start | bytes 442376 | tf_op jit(solution)/shard_map/ppermute | solution.py:29
  9.8 4.5 %collective-permute-start.4 = (bf16[64,1152]{1,0:T(8,128)(2,1)S(1)}, bf16[64,1152]{1,0:T(8,128)(2,1)S(1)}, u32[]{:S(2)}, u32[]{:S(2)}) collective-permute-start(bf16[64,1152]{1,0:T(8,128)(2,1)S(1)} %pad_maximum_fusion.refs_0_), channel_id=1, source_target_pairs={{0,224},{32,0},{64,32},{96,64},{128,96},{160,128},{192,160},{224,1... | collective-permute-start | bytes 442376 | tf_op jit(solution)/shard_map/ppermute | solution.py:29
  14.3 2.7 %collective-permute-done.3.refs_1_ = bf16[64,1152]{1,0:T(8,128)(2,1)S(1)} collective-permute-done((bf16[64,1152]{1,0:T(8,128)(2,1)S(1)}, bf16[64,1152]{1,0:T(8,128)(2,1)S(1)}, u32[]{:S(2)}, u32[]{:S(2)}) %collective-permute-start.3) | collective-permute-done | bytes 147488 | tf_op jit(solution)/shard_map/ppermute | solution.py:29
  17.7 3.0 %collective-permute-start.6 = (bf16[64,1152]{1,0:T(8,128)(2,1)S(1)}, bf16[64,1152]{1,0:T(8,128)(2,1)S(1)}, u32[]{:S(2)}, u32[]{:S(2)}) collective-permute-start(bf16[64,1152]{1,0:T(8,128)(2,1)S(1)} %collective-permute-done.4.refs_2_), channel_id=1, source_target_pairs={{0,224},{32,0},{64,32},{96,64},{128,96},{160,128},{192,160},{224,1... | collective-permute-start | bytes 442376 | tf_op jit(solution)/shard_map/ppermute | solution.py:29
  20.7 2.7 %collective-permute-done.5.refs_3_ = bf16[64,1152]{1,0:T(8,128)(2,1)S(1)} collective-permute-done((bf16[64,1152]{1,0:T(8,128)(2,1)S(1)}, bf16[64,1152]{1,0:T(8,128)(2,1)S(1)}, u32[]{:S(2)}, u32[]{:S(2)}) %collective-permute-start.5) | collective-permute-done | bytes 147488 | tf_op jit(solution)/shard_map/ppermute | solution.py:29
  24.1 3.0 %collective-permute-start.8 = (bf16[64,1152]{1,0:T(8,128)(2,1)S(1)}, bf16[64,1152]{1,0:T(8,128)(2,1)S(1)}, u32[]{:S(2)}, u32[]{:S(2)}) collective-permute-start(bf16[64,1152]{1,0:T(8,128)(2,1)S(1)} %collective-permute-done.6.refs_4_), channel_id=1, source_target_pairs={{0,224},{32,0},{64,32},{96,64},{128,96},{160,128},{192,160},{224,1... | collective-permute-start | bytes 442376 | tf_op jit(solution)/shard_map/ppermute | solution.py:29
  27.1 2.7 %collective-permute-done.7.refs_5_ = bf16[64,1152]{1,0:T(8,128)(2,1)S(1)} collective-permute-done((bf16[64,1152]{1,0:T(8,128)(2,1)S(1)}, bf16[64,1152]{1,0:T(8,128)(2,1)S(1)}, u32[]{:S(2)}, u32[]{:S(2)}) %collective-permute-start.7) | collective-permute-done | bytes 147488 | tf_op jit(solution)/shard_map/ppermute | solution.py:29
  30.4 5.7 %collective-permute-done.9.refs_7_ = bf16[64,1152]{1,0:T(8,128)(2,1)S(1)} collective-permute-done((bf16[64,1152]{1,0:T(8,128)(2,1)S(1)}, bf16[64,1152]{1,0:T(8,128)(2,1)S(1)}, u32[]{:S(2)}, u32[]{:S(2)}) %collective-permute-start.9) | collective-permute-done | bytes 147488 | tf_op jit(solution)/shard_map/ppermute | solution.py:29
  36.8 3.4 %shard_map.190 = (f32[128,128]{1,0:T(8,128)}, bf16[128,1024]{1,0:T(8,128)(2,1)}) custom-call(s32[1]{0:T(128)} %bitcast.3.tensor, bf16[128,2,8192]{2,1,0:T(2,128)(2,1)} %bitcast.22, bf16[8192,128]{1,0:T(8,128)(2,1)} %weight.3), custom_call_target="tpu_custom_call" | custom-call | tf_op jit(solution)/shard_map/pallas_call | solution.py:191
  40.2 3.8 %shard_map.191 = (bf16[256,128]{1,0:T(8,128)(2,1)}, bf16[256,128]{1,0:T(8,128)(2,1)}, s32[8]{0:T(128)}) custom-call(bf16[64,1152]{1,0:T(8,128)(2,1)} %copy-done.4, bf16[64,1152]{1,0:T(8,128)(2,1)} %copy-done.7, bf16[64,1152]{1,0:T(8,128)(2,1)} %copy-done.9, bf16[64,1152]{1,0:T(8,128)(2,1)} %copy-done.10, bf16[64,1152]{1,0:T(8,128)(2,1)} %copy-done.11, ...), custom_call_target="tpu_custom_call" | custom-call | tf_op jit(solution)/shard_map/pallas_call | solution.py:247
  47.0 2.6 %collective-permute-start.12 = (bf16[256,128]{1,0:T(8,128)(2,1)S(1)}, bf16[256,128]{1,0:T(8,128)(2,1)S(1)}, u32[]{:S(2)}, u32[]{:S(2)}) collective-permute-start(bf16[256,128]{1,0:T(8,128)(2,1)S(1)} %add_convert_fusion.5), channel_id=1, source_target_pairs={{0,4},{1,5},{2,6},{3,7},{4,0},{5,1},{6,2},{7,3},{8,12},{9,13},{10,... | collective-permute-start | bytes 196616 | tf_op jit(solution)/shard_map/ppermute | solution.py:478
  49.6 1.9 %collective-permute-start.11 = (bf16[256,128]{1,0:T(8,128)(2,1)S(1)}, bf16[256,128]{1,0:T(8,128)(2,1)S(1)}, u32[]{:S(2)}, u32[]{:S(2)}) collective-permute-start(bf16[256,128]{1,0:T(8,128)(2,1)S(1)} %add_convert_fusion.5), channel_id=1, source_target_pairs={{0,2},{1,3},{2,4},{3,5},{4,6},{5,7},{6,0},{7,1},{8,10},{9,11},{10,... | collective-permute-start | bytes 196616 | tf_op jit(solution)/shard_map/ppermute | solution.py:478
  56.1 4.0 %shard_map.192 = (bf16[64,1152]{1,0:T(8,128)(2,1)}, bf16[64,1152]{1,0:T(8,128)(2,1)}, bf16[64,1152]{1,0:T(8,128)(2,1)}, bf16[64,1152]{1,0:T(8,128)(2,1)}, bf16[3...) custom-call(s32[8]{0:T(128)} %get-tuple-element.111.names, ...), custom_call_target="tpu_custom_call" | custom-call | tf_op jit(solution)/shard_map/pallas_call | solution.py:319
  60.2 3.2 %collective-permute-start.16 = (bf16[64,1152]{1,0:T(8,128)(2,1)}, bf16[64,1152]{1,0:T(8,128)(2,1)S(1)}, u32[]{:S(2)}, u32[]{:S(2)}) collective-permute-start(bf16[64,1152]{1,0:T(8,128)(2,1)} %get-tuple-element.116), channel_id=1, source_target_pairs={{0,224},{32,0},{64,32},{96,64},{128,96},{160,128},{192,160},{224,1... | collective-permute-start | bytes 442376 | tf_op jit(solution)/shard_map/ppermute | solution.py:29
  63.6 4.2 %collective-permute-start.21 = (bf16[32,1152]{1,0:T(8,128)(2,1)}, bf16[32,1152]{1,0:T(8,128)(2,1)S(1)}, u32[]{:S(2)}, u32[]{:S(2)}) collective-permute-start(bf16[32,1152]{1,0:T(8,128)(2,1)} %get-tuple-element.126), channel_id=1, source_target_pairs={{0,192},{32,224},{64,0},{96,32},{128,64},{160,96},{192,128},{224,1... | collective-permute-start | bytes 221192 | tf_op jit(solution)/shard_map/ppermute | solution.py:29
  68.6 3.6 %collective-permute-start.18 = (bf16[64,1152]{1,0:T(8,128)(2,1)}, bf16[64,1152]{1,0:T(8,128)(2,1)S(1)}, u32[]{:S(2)}, u32[]{:S(2)}) collective-permute-start(bf16[64,1152]{1,0:T(8,128)(2,1)} %get-tuple-element.120), channel_id=1, source_target_pairs={{0,224},{32,0},{64,32},{96,64},{128,96},{160,128},{192,160},{224,1... | collective-permute-start | bytes 442376 | tf_op jit(solution)/shard_map/ppermute | solution.py:29
  76.0 2.5 %collective-permute-start.22 = (bf16[64,1152]{1,0:T(8,128)(2,1)S(1)}, bf16[64,1152]{1,0:T(8,128)(2,1)S(1)}, u32[]{:S(2)}, u32[]{:S(2)}) collective-permute-start(bf16[64,1152]{1,0:T(8,128)(2,1)S(1)} %pad_maximum_fusion.2), channel_id=1, source_target_pairs={{0,192},{32,224},{64,0},{96,32},{128,64},{160,96},{192,128},{224,1... | collective-permute-start | bytes 442376 | tf_op jit(solution)/shard_map/ppermute | solution.py:29
  78.7 4.2 %collective-permute-done.20.refs_3_ = bf16[64,1152]{1,0:T(8,128)(2,1)S(1)} collective-permute-done((bf16[64,1152]{1,0:T(8,128)(2,1)S(1)}, bf16[64,1152]{1,0:T(8,128)(2,1)S(1)}, u32[]{:S(2)}, u32[]{:S(2)}) %collective-permute-start.20) | collective-permute-done | bytes 147488 | tf_op jit(solution)/shard_map/ppermute | solution.py:29
  83.8 2.7 %shard_map.193 = (f32[64,1024]{1,0:T(8,128)}, f32[64,1024]{1,0:T(8,128)}, f32[64,1024]{1,0:T(8,128)}, f32[64,128]{1,0:T(8,128)}, f32[64,128]{1,0:T(8,128)}, /*index=5*/f32[64,128]{1,0:T(8,128)}, bf16[64,1152]{1,0:T(8,128)(2,1)}) custom-call(bf16[64,1152]{1,0:T(8,128)(2,1)} %get-tuple-element.114.refs_0_, bf16[64,1152]{1,0:T(8,128)(2,1)} %copy-done.6, ...), custom_call_target="tpu_custom_call" | custom-call | tf_op jit(solution)/shard_map/pallas_call | solution.py:371
  86.6 3.1 %collective-permute-start.23 = (bf16[64,1152]{1,0:T(8,128)(2,1)}, bf16[64,1152]{1,0:T(8,128)(2,1)S(1)}, u32[]{:S(2)}, u32[]{:S(2)}) collective-permute-start(bf16[64,1152]{1,0:T(8,128)(2,1)} %get-tuple-element.145.refs_0_), channel_id=1, source_target_pairs={{0,8},{8,16},{16,24},{24,0},{1,9},{9,17},{17,25},{25,1},{2,10},{10... | collective-permute-start | bytes 442376 | tf_op jit(solution)/shard_map/ppermute | solution.py:29
  91.6 2.8 %shard_map.194 = (f32[128,128]{1,0:T(8,128)S(1)}, bf16[128,1024]{1,0:T(8,128)(2,1)S(1)}) custom-call(s32[1]{0:T(128)} %bitcast.3.tensor, bf16[128,2,8192]{2,1,0:T(2,128)(2,1)} %bitcast.23, bf16[8192,128]{1,0:T(8,128)(2,1)} %weight.3), custom_call_target="tpu_custom_call" | custom-call | tf_op jit(solution)/shard_map/pallas_call | solution.py:191
  95.9 2.1 %collective-permute-done.24.refs_2_ = bf16[64,1152]{1,0:T(8,128)(2,1)S(1)} collective-permute-done((bf16[64,1152]{1,0:T(8,128)(2,1)}, bf16[64,1152]{1,0:T(8,128)(2,1)S(1)}, u32[]{:S(2)}, u32[]{:S(2)}) %collective-permute-start.24) | collective-permute-done | bytes 147488 | tf_op jit(solution)/shard_map/ppermute | solution.py:29
  99.9 4.0 %collective-permute-start.28 = (bf16[64,1152]{1,0:T(8,128)(2,1)S(1)}, bf16[64,1152]{1,0:T(8,128)(2,1)S(1)}, u32[]{:S(2)}, u32[]{:S(2)}) collective-permute-start(bf16[64,1152]{1,0:T(8,128)(2,1)S(1)} %shard_map.195.refs_2_.refs_6_), channel_id=1, source_target_pairs={{0,64},{32,96},{64,128},{96,160},{128,192},{160,224},{192,0},{224,... | collective-permute-start | bytes 442376 | tf_op jit(solution)/shard_map/ppermute | solution.py:29
  105.6 1.8 %collective-permute-start.27 = (bf16[64,1152]{1,0:T(8,128)(2,1)S(1)}, bf16[64,1152]{1,0:T(8,128)(2,1)S(1)}, u32[]{:S(2)}, u32[]{:S(2)}) collective-permute-start(bf16[64,1152]{1,0:T(8,128)(2,1)S(1)} %shard_map.195.refs_2_.refs_6_), channel_id=1, source_target_pairs={{0,224},{32,0},{64,32},{96,64},{128,96},{160,128},{192,160},{224,1... | collective-permute-start | bytes 442376 | tf_op jit(solution)/shard_map/ppermute | solution.py:29
  107.4 3.0 %collective-permute-done.28.refs_5_.refs_9_ = bf16[64,1152]{1,0:T(8,128)(2,1)S(1)} collective-permute-done((bf16[64,1152]{1,0:T(8,128)(2,1)S(1)}, bf16[64,1152]{1,0:T(8,128)(2,1)S(1)}, u32[]{:S(2)}, u32[]{:S(2)}) %collective-permute-start.28) | collective-permute-done | bytes 147488 | tf_op jit(solution)/shard_map/ppermute | solution.py:29
  114.2 2.1 %collective-permute-start.32 = (bf16[64,1152]{1,0:T(8,128)(2,1)S(1)}, bf16[64,1152]{1,0:T(8,128)(2,1)S(1)}, u32[]{:S(2)}, u32[]{:S(2)}) collective-permute-start(bf16[64,1152]{1,0:T(8,128)(2,1)S(1)} %collective-permute-done.28.refs_5_.refs_9_), channel_id=1, source_target_pairs={{0,64},{32,96},{64,128},{96,160},{128,192},{160,224},{192,0},{224,... | collective-permute-start | bytes 442376 | tf_op jit(solution)/shard_map/ppermute | solution.py:29
  118.7 3.7 %collective-permute-done.32.refs_4_.refs_13_ = bf16[64,1152]{1,0:T(8,128)(2,1)S(1)} collective-permute-done((bf16[64,1152]{1,0:T(8,128)(2,1)S(1)}, bf16[64,1152]{1,0:T(8,128)(2,1)S(1)}, u32[]{:S(2)}, u32[]{:S(2)}) %collective-permute-start.32) | collective-permute-done | bytes 147488 | tf_op jit(solution)/shard_map/ppermute | solution.py:29
  124.3 1.9 %collective-permute-start.34 = (f32[32,256]{1,0:T(8,128)S(1)}, f32[32,256]{1,0:T(8,128)S(1)}, u32[]{:S(2)}, u32[]{:S(2)}) collective-permute-start(f32[32,256]{1,0:T(8,128)S(1)} %add.93.refs_2_), channel_id=1, source_target_pairs={{0,2},{1,3},{2,4},{3,5},{4,6},{5,7},{6,0},{7,1},{8,10},{9,11},{10,... | collective-permute-start | bytes 98312 | tf_op jit(solution)/shard_map/ppermute | solution.py:478
  126.2 3.1 %collective-permute-start.35 = (f32[32,256]{1,0:T(8,128)S(1)}, f32[32,256]{1,0:T(8,128)S(1)}, u32[]{:S(2)}, u32[]{:S(2)}) collective-permute-start(f32[32,256]{1,0:T(8,128)S(1)} %add.93.refs_2_), channel_id=1, source_target_pairs={{0,4},{1,5},{2,6},{3,7},{4,0},{5,1},{6,2},{7,3},{8,12},{9,13},{10,... | collective-permute-start | bytes 98312 | tf_op jit(solution)/shard_map/ppermute | solution.py:478
  129.3 2.3 %collective-permute-done.35.refs_4_ = f32[32,256]{1,0:T(8,128)S(1)} collective-permute-done((f32[32,256]{1,0:T(8,128)S(1)}, f32[32,256]{1,0:T(8,128)S(1)}, u32[]{:S(2)}, u32[]{:S(2)}) %collective-permute-start.35) | collective-permute-done | bytes 32800 | tf_op jit(solution)/shard_map/ppermute | solution.py:478
  (118 shorter events, 34.3 us)
Async XLA Ops:
  4.8 35.5 %collective-permute-start = (bf16[272,1152]{1,0:T(8,128)(2,1)}, bf16[272,1152]{1,0:T(8,128)(2,1)}, u32[]{:S(2)}, u32[]{:S(2)}) collective-permute-start(bf16[272,1152]{1,0:T(8,128)(2,1)} %get-tuple-element.83), channel_id=1, source_target_pairs={{0,8},{8,16},{16,24},{24,0},{1,9},{9,17},{17,25},{25,1},{2,10},{10... | collective-permute-start | bytes 1880072 | tf_op jit(solution)/shard_map/ppermute | solution.py:29
  5.3 34.9 %collective-permute-start.1 = (bf16[272,1152]{1,0:T(8,128)(2,1)}, bf16[272,1152]{1,0:T(8,128)(2,1)}, u32[]{:S(2)}, u32[]{:S(2)}) collective-permute-start(bf16[272,1152]{1,0:T(8,128)(2,1)} %get-tuple-element.84), channel_id=1, source_target_pairs={{0,16},{8,24},{16,0},{24,8},{1,17},{9,25},{17,1},{25,9},{2,18},{10... | collective-permute-start | bytes 1880072 | tf_op jit(solution)/shard_map/ppermute | solution.py:29
  7.7 32.5 %collective-permute-start.2 = (bf16[272,1152]{1,0:T(8,128)(2,1)}, bf16[272,1152]{1,0:T(8,128)(2,1)}, u32[]{:S(2)}, u32[]{:S(2)}) collective-permute-start(bf16[272,1152]{1,0:T(8,128)(2,1)} %get-tuple-element.85), channel_id=1, source_target_pairs={{0,24},{8,0},{16,8},{24,16},{1,25},{9,1},{17,9},{25,17},{2,26},{10... | collective-permute-start | bytes 1880072 | tf_op jit(solution)/shard_map/ppermute | solution.py:29
  7.8 9.2 %collective-permute-start.3 = (bf16[64,1152]{1,0:T(8,128)(2,1)S(1)}, bf16[64,1152]{1,0:T(8,128)(2,1)S(1)}, u32[]{:S(2)}, u32[]{:S(2)}) collective-permute-start(bf16[64,1152]{1,0:T(8,128)(2,1)S(1)} %pad_maximum_fusion.refs_0_), channel_id=1, source_target_pairs={{0,32},{32,64},{64,96},{96,128},{128,160},{160,192},{192,224},{224... | collective-permute-start | bytes 442376 | tf_op jit(solution)/shard_map/ppermute | solution.py:29
  9.8 7.2 %collective-permute-start.4 = (bf16[64,1152]{1,0:T(8,128)(2,1)S(1)}, bf16[64,1152]{1,0:T(8,128)(2,1)S(1)}, u32[]{:S(2)}, u32[]{:S(2)}) collective-permute-start(bf16[64,1152]{1,0:T(8,128)(2,1)S(1)} %pad_maximum_fusion.refs_0_), channel_id=1, source_target_pairs={{0,224},{32,0},{64,32},{96,64},{128,96},{160,128},{192,160},{224,1... | collective-permute-start | bytes 442376 | tf_op jit(solution)/shard_map/ppermute | solution.py:29
  17.0 6.4 %collective-permute-start.5 = (bf16[64,1152]{1,0:T(8,128)(2,1)S(1)}, bf16[64,1152]{1,0:T(8,128)(2,1)S(1)}, u32[]{:S(2)}, u32[]{:S(2)}) collective-permute-start(bf16[64,1152]{1,0:T(8,128)(2,1)S(1)} %collective-permute-done.3.refs_1_), channel_id=1, source_target_pairs={{0,32},{32,64},{64,96},{96,128},{128,160},{160,192},{192,224},{224... | collective-permute-start | bytes 442376 | tf_op jit(solution)/shard_map/ppermute | solution.py:29
  17.7 5.7 %collective-permute-start.6 = (bf16[64,1152]{1,0:T(8,128)(2,1)S(1)}, bf16[64,1152]{1,0:T(8,128)(2,1)S(1)}, u32[]{:S(2)}, u32[]{:S(2)}) collective-permute-start(bf16[64,1152]{1,0:T(8,128)(2,1)S(1)} %collective-permute-done.4.refs_2_), channel_id=1, source_target_pairs={{0,224},{32,0},{64,32},{96,64},{128,96},{160,128},{192,160},{224,1... | collective-permute-start | bytes 442376 | tf_op jit(solution)/shard_map/ppermute | solution.py:29
  23.4 6.4 %collective-permute-start.7 = (bf16[64,1152]{1,0:T(8,128)(2,1)S(1)}, bf16[64,1152]{1,0:T(8,128)(2,1)S(1)}, u32[]{:S(2)}, u32[]{:S(2)}) collective-permute-start(bf16[64,1152]{1,0:T(8,128)(2,1)S(1)} %collective-permute-done.5.refs_3_), channel_id=1, source_target_pairs={{0,32},{32,64},{64,96},{96,128},{128,160},{160,192},{192,224},{224... | collective-permute-start | bytes 442376 | tf_op jit(solution)/shard_map/ppermute | solution.py:29
  24.1 5.7 %collective-permute-start.8 = (bf16[64,1152]{1,0:T(8,128)(2,1)S(1)}, bf16[64,1152]{1,0:T(8,128)(2,1)S(1)}, u32[]{:S(2)}, u32[]{:S(2)}) collective-permute-start(bf16[64,1152]{1,0:T(8,128)(2,1)S(1)} %collective-permute-done.6.refs_4_), channel_id=1, source_target_pairs={{0,224},{32,0},{64,32},{96,64},{128,96},{160,128},{192,160},{224,1... | collective-permute-start | bytes 442376 | tf_op jit(solution)/shard_map/ppermute | solution.py:29
  29.8 6.4 %collective-permute-start.9 = (bf16[64,1152]{1,0:T(8,128)(2,1)S(1)}, bf16[64,1152]{1,0:T(8,128)(2,1)S(1)}, u32[]{:S(2)}, u32[]{:S(2)}) collective-permute-start(bf16[64,1152]{1,0:T(8,128)(2,1)S(1)} %collective-permute-done.7.refs_5_), channel_id=1, source_target_pairs={{0,32},{32,64},{64,96},{96,128},{128,160},{160,192},{192,224},{224... | collective-permute-start | bytes 442376 | tf_op jit(solution)/shard_map/ppermute | solution.py:29
  46.5 5.1 %collective-permute-start.13 = (bf16[256,128]{1,0:T(8,128)(2,1)S(1)}, bf16[256,128]{1,0:T(8,128)(2,1)S(1)}, u32[]{:S(2)}, u32[]{:S(2)}) collective-permute-start(bf16[256,128]{1,0:T(8,128)(2,1)S(1)} %add_convert_fusion.5), channel_id=1, source_target_pairs={{0,6},{1,7},{2,0},{3,1},{4,2},{5,3},{6,4},{7,5},{8,14},{9,15},{10,... | collective-permute-start | bytes 196616 | tf_op jit(solution)/shard_map/ppermute | solution.py:478
  47.0 6.2 %collective-permute-start.12 = (bf16[256,128]{1,0:T(8,128)(2,1)S(1)}, bf16[256,128]{1,0:T(8,128)(2,1)S(1)}, u32[]{:S(2)}, u32[]{:S(2)}) collective-permute-start(bf16[256,128]{1,0:T(8,128)(2,1)S(1)} %add_convert_fusion.5), channel_id=1, source_target_pairs={{0,4},{1,5},{2,6},{3,7},{4,0},{5,1},{6,2},{7,3},{8,12},{9,13},{10,... | collective-permute-start | bytes 196616 | tf_op jit(solution)/shard_map/ppermute | solution.py:478
  60.1 8.5 %collective-permute-start.15 = (bf16[64,1152]{1,0:T(8,128)(2,1)}, bf16[64,1152]{1,0:T(8,128)(2,1)S(1)}, u32[]{:S(2)}, u32[]{:S(2)}) collective-permute-start(bf16[64,1152]{1,0:T(8,128)(2,1)} %get-tuple-element.115), channel_id=1, source_target_pairs={{0,32},{32,64},{64,96},{96,128},{128,160},{160,192},{192,224},{224... | collective-permute-start | bytes 442376 | tf_op jit(solution)/shard_map/ppermute | solution.py:29
  60.2 8.4 %collective-permute-start.16 = (bf16[64,1152]{1,0:T(8,128)(2,1)}, bf16[64,1152]{1,0:T(8,128)(2,1)S(1)}, u32[]{:S(2)}, u32[]{:S(2)}) collective-permute-start(bf16[64,1152]{1,0:T(8,128)(2,1)} %get-tuple-element.116), channel_id=1, source_target_pairs={{0,224},{32,0},{64,32},{96,64},{128,96},{160,128},{192,160},{224,1... | collective-permute-start | bytes 442376 | tf_op jit(solution)/shard_map/ppermute | solution.py:29
  63.5 8.8 %collective-permute-start.19 = (bf16[32,1152]{1,0:T(8,128)(2,1)}, bf16[32,1152]{1,0:T(8,128)(2,1)S(1)}, u32[]{:S(2)}, u32[]{:S(2)}) collective-permute-start(bf16[32,1152]{1,0:T(8,128)(2,1)} %get-tuple-element.123), channel_id=1, source_target_pairs={{0,64},{32,96},{64,128},{96,160},{128,192},{160,224},{192,0},{224,... | collective-permute-start | bytes 221192 | tf_op jit(solution)/shard_map/ppermute | solution.py:29
  63.6 11.4 %collective-permute-start.21 = (bf16[32,1152]{1,0:T(8,128)(2,1)}, bf16[32,1152]{1,0:T(8,128)(2,1)S(1)}, u32[]{:S(2)}, u32[]{:S(2)}) collective-permute-start(bf16[32,1152]{1,0:T(8,128)(2,1)} %get-tuple-element.126), channel_id=1, source_target_pairs={{0,192},{32,224},{64,0},{96,32},{128,64},{160,96},{192,128},{224,1... | collective-permute-start | bytes 221192 | tf_op jit(solution)/shard_map/ppermute | solution.py:29
  68.6 10.0 %collective-permute-start.17 = (bf16[64,1152]{1,0:T(8,128)(2,1)}, bf16[64,1152]{1,0:T(8,128)(2,1)S(1)}, u32[]{:S(2)}, u32[]{:S(2)}) collective-permute-start(bf16[64,1152]{1,0:T(8,128)(2,1)} %get-tuple-element.119), channel_id=1, source_target_pairs={{0,32},{32,64},{64,96},{96,128},{128,160},{160,192},{192,224},{224... | collective-permute-start | bytes 442376 | tf_op jit(solution)/shard_map/ppermute | solution.py:29
  68.6 10.1 %collective-permute-start.18 = (bf16[64,1152]{1,0:T(8,128)(2,1)}, bf16[64,1152]{1,0:T(8,128)(2,1)S(1)}, u32[]{:S(2)}, u32[]{:S(2)}) collective-permute-start(bf16[64,1152]{1,0:T(8,128)(2,1)} %get-tuple-element.120), channel_id=1, source_target_pairs={{0,224},{32,0},{64,32},{96,64},{128,96},{160,128},{192,160},{224,1... | collective-permute-start | bytes 442376 | tf_op jit(solution)/shard_map/ppermute | solution.py:29
  73.2 9.6 %collective-permute-start.20 = (bf16[64,1152]{1,0:T(8,128)(2,1)S(1)}, bf16[64,1152]{1,0:T(8,128)(2,1)S(1)}, u32[]{:S(2)}, u32[]{:S(2)}) collective-permute-start(bf16[64,1152]{1,0:T(8,128)(2,1)S(1)} %pad_maximum_fusion.1), channel_id=1, source_target_pairs={{0,64},{32,96},{64,128},{96,160},{128,192},{160,224},{192,0},{224,... | collective-permute-start | bytes 442376 | tf_op jit(solution)/shard_map/ppermute | solution.py:29
  76.0 7.2 %collective-permute-start.22 = (bf16[64,1152]{1,0:T(8,128)(2,1)S(1)}, bf16[64,1152]{1,0:T(8,128)(2,1)S(1)}, u32[]{:S(2)}, u32[]{:S(2)}) collective-permute-start(bf16[64,1152]{1,0:T(8,128)(2,1)S(1)} %pad_maximum_fusion.2), channel_id=1, source_target_pairs={{0,192},{32,224},{64,0},{96,32},{128,64},{160,96},{192,128},{224,1... | collective-permute-start | bytes 442376 | tf_op jit(solution)/shard_map/ppermute | solution.py:29
  86.6 9.3 %collective-permute-start.23 = (bf16[64,1152]{1,0:T(8,128)(2,1)}, bf16[64,1152]{1,0:T(8,128)(2,1)S(1)}, u32[]{:S(2)}, u32[]{:S(2)}) collective-permute-start(bf16[64,1152]{1,0:T(8,128)(2,1)} %get-tuple-element.145.refs_0_), channel_id=1, source_target_pairs={{0,8},{8,16},{16,24},{24,0},{1,9},{9,17},{17,25},{25,1},{2,10},{10... | collective-permute-start | bytes 442376 | tf_op jit(solution)/shard_map/ppermute | solution.py:29
  89.7 8.2 %collective-permute-start.24 = (bf16[64,1152]{1,0:T(8,128)(2,1)}, bf16[64,1152]{1,0:T(8,128)(2,1)S(1)}, u32[]{:S(2)}, u32[]{:S(2)}) collective-permute-start(bf16[64,1152]{1,0:T(8,128)(2,1)} %get-tuple-element.145.refs_0_), channel_id=1, source_target_pairs={{0,16},{8,24},{16,0},{24,8},{1,17},{9,25},{17,1},{25,9},{2,18},{10... | collective-permute-start | bytes 442376 | tf_op jit(solution)/shard_map/ppermute | solution.py:29
  89.9 9.5 %collective-permute-start.25 = (bf16[64,1152]{1,0:T(8,128)(2,1)}, bf16[64,1152]{1,0:T(8,128)(2,1)S(1)}, u32[]{:S(2)}, u32[]{:S(2)}) collective-permute-start(bf16[64,1152]{1,0:T(8,128)(2,1)} %get-tuple-element.145.refs_0_), channel_id=1, source_target_pairs={{0,24},{8,0},{16,8},{24,16},{1,25},{9,1},{17,9},{25,17},{2,26},{10... | collective-permute-start | bytes 442376 | tf_op jit(solution)/shard_map/ppermute | solution.py:29
  99.9 10.4 %collective-permute-start.28 = (bf16[64,1152]{1,0:T(8,128)(2,1)S(1)}, bf16[64,1152]{1,0:T(8,128)(2,1)S(1)}, u32[]{:S(2)}, u32[]{:S(2)}) collective-permute-start(bf16[64,1152]{1,0:T(8,128)(2,1)S(1)} %shard_map.195.refs_2_.refs_6_), channel_id=1, source_target_pairs={{0,64},{32,96},{64,128},{96,160},{128,192},{160,224},{192,0},{224,... | collective-permute-start | bytes 442376 | tf_op jit(solution)/shard_map/ppermute | solution.py:29
  103.9 8.9 %collective-permute-start.29 = (bf16[64,1152]{1,0:T(8,128)(2,1)S(1)}, bf16[64,1152]{1,0:T(8,128)(2,1)S(1)}, u32[]{:S(2)}, u32[]{:S(2)}) collective-permute-start(bf16[64,1152]{1,0:T(8,128)(2,1)S(1)} %shard_map.195.refs_2_.refs_6_), channel_id=1, source_target_pairs={{0,192},{32,224},{64,0},{96,32},{128,64},{160,96},{192,128},{224,1... | collective-permute-start | bytes 442376 | tf_op jit(solution)/shard_map/ppermute | solution.py:29
  104.2 12.1 %collective-permute-start.26 = (bf16[64,1152]{1,0:T(8,128)(2,1)S(1)}, bf16[64,1152]{1,0:T(8,128)(2,1)S(1)}, u32[]{:S(2)}, u32[]{:S(2)}) collective-permute-start(bf16[64,1152]{1,0:T(8,128)(2,1)S(1)} %shard_map.195.refs_2_.refs_6_), channel_id=1, source_target_pairs={{0,32},{32,64},{64,96},{96,128},{128,160},{160,192},{192,224},{224... | collective-permute-start | bytes 442376 | tf_op jit(solution)/shard_map/ppermute | solution.py:29
  105.6 10.7 %collective-permute-start.27 = (bf16[64,1152]{1,0:T(8,128)(2,1)S(1)}, bf16[64,1152]{1,0:T(8,128)(2,1)S(1)}, u32[]{:S(2)}, u32[]{:S(2)}) collective-permute-start(bf16[64,1152]{1,0:T(8,128)(2,1)S(1)} %shard_map.195.refs_2_.refs_6_), channel_id=1, source_target_pairs={{0,224},{32,0},{64,32},{96,64},{128,96},{160,128},{192,160},{224,1... | collective-permute-start | bytes 442376 | tf_op jit(solution)/shard_map/ppermute | solution.py:29
  110.4 8.3 %collective-permute-start.30 = (bf16[64,1152]{1,0:T(8,128)(2,1)S(1)}, bf16[64,1152]{1,0:T(8,128)(2,1)S(1)}, u32[]{:S(2)}, u32[]{:S(2)}) collective-permute-start(bf16[64,1152]{1,0:T(8,128)(2,1)S(1)} %collective-permute-done.28.refs_5_.refs_9_), channel_id=1, source_target_pairs={{0,32},{32,64},{64,96},{96,128},{128,160},{160,192},{192,224},{224... | collective-permute-start | bytes 442376 | tf_op jit(solution)/shard_map/ppermute | solution.py:29
  112.8 5.8 %collective-permute-start.31 = (bf16[64,1152]{1,0:T(8,128)(2,1)S(1)}, bf16[64,1152]{1,0:T(8,128)(2,1)S(1)}, u32[]{:S(2)}, u32[]{:S(2)}) collective-permute-start(bf16[64,1152]{1,0:T(8,128)(2,1)S(1)} %collective-permute-done.29.refs_6_.refs_10_), channel_id=1, source_target_pairs={{0,224},{32,0},{64,32},{96,64},{128,96},{160,128},{192,160},{224,1... | collective-permute-start | bytes 442376 | tf_op jit(solution)/shard_map/ppermute | solution.py:29
  114.2 8.2 %collective-permute-start.32 = (bf16[64,1152]{1,0:T(8,128)(2,1)S(1)}, bf16[64,1152]{1,0:T(8,128)(2,1)S(1)}, u32[]{:S(2)}, u32[]{:S(2)}) collective-permute-start(bf16[64,1152]{1,0:T(8,128)(2,1)S(1)} %collective-permute-done.28.refs_5_.refs_9_), channel_id=1, source_target_pairs={{0,64},{32,96},{64,128},{96,160},{128,192},{160,224},{192,0},{224,... | collective-permute-start | bytes 442376 | tf_op jit(solution)/shard_map/ppermute | solution.py:29
  124.3 5.0 %collective-permute-start.34 = (f32[32,256]{1,0:T(8,128)S(1)}, f32[32,256]{1,0:T(8,128)S(1)}, u32[]{:S(2)}, u32[]{:S(2)}) collective-permute-start(f32[32,256]{1,0:T(8,128)S(1)} %add.93.refs_2_), channel_id=1, source_target_pairs={{0,2},{1,3},{2,4},{3,5},{4,6},{5,7},{6,0},{7,1},{8,10},{9,11},{10,... | collective-permute-start | bytes 98312 | tf_op jit(solution)/shard_map/ppermute | solution.py:478
  126.2 5.4 %collective-permute-start.35 = (f32[32,256]{1,0:T(8,128)S(1)}, f32[32,256]{1,0:T(8,128)S(1)}, u32[]{:S(2)}, u32[]{:S(2)}) collective-permute-start(f32[32,256]{1,0:T(8,128)S(1)} %add.93.refs_2_), channel_id=1, source_target_pairs={{0,4},{1,5},{2,6},{3,7},{4,0},{5,1},{6,2},{7,3},{8,12},{9,13},{10,... | collective-permute-start | bytes 98312 | tf_op jit(solution)/shard_map/ppermute | solution.py:478
  (26 other events, 168.9 us)
